TPU v7x, 32 devices: a whole 2x2x4 slice. The times are simulated.
32 devices in a mesh: groups: 1, dev: 8 (over y, x, core), head: 4 (over z).
Axes of the slice: x: 2, y: 2, z: 4, core: 2. Of those that a mesh axis runs over, the one named last changes fastest.
Arguments:
- queries: bfloat16 [4, 128, 2048], P(None, ('groups', 'dev'), 'head'), may hold values from -6 to 6
- keys_in: bfloat16 [4, 128, 2048], P(None, ('groups', 'dev'), 'head'), may hold values from -6 to 6
- values_in: bfloat16 [4, 128, 4096], P(None, ('groups', 'dev'), 'head'), may hold values from -6 to 6
- out_gate: bfloat16 [4, 128, 4096], P(None, ('groups', 'dev'), 'head'), may hold values from -6 to 6
- beta_logit: float32 [4, 128, 32], P(None, ('groups', 'dev'), 'head'), may hold values from -6 to 6
- decay_rate: float32 [4, 128, 32], P(None, ('groups', 'dev'), 'head'), may hold values from 0.3 to 1
- states: float32 [128, 32, 128, 128], P(('groups', 'dev'), 'head'), may hold values from -3 to 3
- out_weight: bfloat16 [4096, 2048], P('head'), may hold values from -0.09375 to 0.09375
- head_gain: float32 [128], replicated, may hold values from 0.1 to 1.9
- residual: bfloat16 [4, 128, 2048], P(None, ('groups', 'dev', 'head')), may hold values from -3 to 3
- post_gain: float32 [2048], replicated, may hold values from 0.5 to 1.5
- expert_ids: int32 [4, 128, 10], P(None, 'groups'), may hold values from 0 to 31, all different within a row; in each aligned block of 128 rows (0 to 127, 128 to 255, ..., all dimensions but the last counted through in order) at most 48 rows name the same one
- route_weight: float32 [4, 128, 10], P(None, 'groups'), may hold values from 0.05 to 1
- expert_gate: bfloat16 [32, 2048, 512], P(('dev', 'head')), may hold values from -0.25 to 0.25
- expert_up: bfloat16 [32, 2048, 512], P(('dev', 'head')), may hold values from -0.25 to 0.25
- expert_down: bfloat16 [32, 512, 2048], P(('dev', 'head')), may hold values from -0.25 to 0.25
Outputs:
- layer_out: bfloat16 [4, 128, 2048], P(None, ('groups', 'dev', 'head'))
Inputs may be any that keep to these rules, and one draw needn't show every extreme that they name: `expert_ids`: the 10 experts of one request and step differ. In each step no expert is named by more than 48 requests of the group, a bound that some block reaches.
All inputs are finite; a program needn't handle non-finite values.
Results may differ from a plain program's by a relative error of at most 0.0075.
Values may be sent and summed in bfloat16 or wider, within the bound.
No kernel may reach another device: no remote copies, remote signals or barrier semaphores. Data moves between devices by JAX's collectives and lax.ppermute only.
A program may use at most 128 MiB of HBM per device.

v0:
```python
import jax
import jax.numpy as jnp
from jax import lax
from jax.sharding import PartitionSpec as P

HK = 128
HV = 128
TOPK = 10
STEPS = 4
MOST = 48


def unit_rows(values):
    return values * lax.rsqrt(jnp.sum(values * values, axis=-1, keepdims=True) + 1e-06)


def rms_scale(values):
    return values * lax.rsqrt(jnp.mean(values * values, axis=-1, keepdims=True) + 1e-06)


def expert_mlp(rows, gate_mat, up_mat, down_mat):
    gated = jnp.dot(rows, gate_mat, preferred_element_type=jnp.float32)
    lifted = jnp.dot(rows, up_mat, preferred_element_type=jnp.float32)
    hidden = (jax.nn.silu(gated) * lifted).astype(jnp.bfloat16)
    return jnp.dot(hidden, down_mat, preferred_element_type=jnp.float32).astype(jnp.bfloat16)


def attend(
    moment,
    memory,
    queries,
    keys_in,
    values_in,
    out_gate,
    beta_logit,
    decay_rate,
    head_gain,
    out_weight,
):
    highest = lax.Precision.HIGHEST
    request_rows = queries.shape[1]
    qk_local = queries.shape[2] // HK
    v_local = values_in.shape[2] // HV
    repeat_count = v_local // qk_local
    query_rows = unit_rows(
        queries[moment].astype(jnp.float32).reshape(request_rows, qk_local, HK)
    ) * HK ** (-0.5)
    query_rows = jnp.repeat(query_rows, repeat_count, axis=1)
    key_rows = jnp.repeat(
        unit_rows(keys_in[moment].astype(jnp.float32).reshape(request_rows, qk_local, HK)),
        repeat_count,
        axis=1,
    )
    value_rows = values_in[moment].astype(jnp.float32).reshape(request_rows, v_local, HV)
    gate_rows = out_gate[moment].astype(jnp.float32).reshape(request_rows, v_local, HV)
    beta_rows = jax.nn.sigmoid(beta_logit[moment])
    memory = memory * decay_rate[moment][:, :, None, None]
    recalled = jnp.einsum("rhk,rhkv->rhv", key_rows, memory, precision=highest)
    delta_rows = (value_rows - recalled) * beta_rows[:, :, None]
    memory = memory + key_rows[:, :, :, None] * delta_rows[:, :, None, :]
    read_out = jnp.einsum("rhk,rhkv->rhv", query_rows, memory, precision=highest)
    gated = rms_scale(read_out) * head_gain * jax.nn.silu(gate_rows)
    flattened = gated.reshape(request_rows, v_local * HV).astype(jnp.bfloat16)
    return (memory, jnp.dot(flattened, out_weight, preferred_element_type=jnp.float32))


def mixture(
    normed,
    step_ids,
    step_shares,
    step_count,
    owners,
    own_index,
    per_step,
    expert_gate,
    expert_up,
    expert_down,
):
    highest = lax.Precision.HIGHEST
    capacity = step_count * MOST
    gathered = lax.all_gather(normed, ("dev", "head"), axis=0, tiled=True)
    ordered = (
        step_ids.reshape(step_count, owners, per_step, TOPK).transpose(1, 0, 2, 3).reshape(-1, TOPK)
    )
    weights = (
        step_shares.reshape(step_count, owners, per_step, TOPK)
        .transpose(1, 0, 2, 3)
        .reshape(-1, TOPK)
    )
    matches = ordered == own_index
    chosen = jnp.any(matches, axis=-1)
    picked_share = jnp.sum(jnp.where(matches, weights, 0.0), axis=-1)
    slot_rows = jnp.nonzero(chosen, size=capacity, fill_value=0)[0].astype(jnp.int32)
    filled = jnp.arange(capacity) < jnp.sum(chosen.astype(jnp.int32))
    picked = jnp.take(gathered, slot_rows, axis=0)
    served = expert_mlp(picked, expert_gate[0], expert_up[0], expert_down[0]).astype(jnp.float32)
    scaled = served * jnp.where(filled, jnp.take(picked_share, slot_rows), 0.0)[:, None]
    positions = jnp.arange(lax.axis_size(("dev", "head")) * normed.shape[0], dtype=jnp.int32)
    selector = (slot_rows[None, :] == positions[:, None]).astype(jnp.float32)
    return lax.psum_scatter(
        jnp.dot(selector, scaled, precision=highest),
        ("dev", "head"),
        scatter_dimension=0,
        tiled=True,
    )


def shards(
    queries,
    keys_in,
    values_in,
    out_gate,
    beta_logit,
    decay_rate,
    states,
    out_weight,
    head_gain,
    residual,
    post_gain,
    expert_ids,
    route_weight,
    expert_gate,
    expert_up,
    expert_down,
):
    owners = lax.axis_size("dev") * lax.axis_size("head")
    own_index = lax.axis_index("dev") * lax.axis_size("head") + lax.axis_index("head")
    per_step = residual.shape[1]
    shares = route_weight / jnp.sum(route_weight, axis=-1, keepdims=True)
    memory = states
    outputs = []
    for moment in range(STEPS):
        memory, partial_value = attend(
            moment,
            memory,
            queries,
            keys_in,
            values_in,
            out_gate,
            beta_logit,
            decay_rate,
            head_gain,
            out_weight,
        )
        arrived = lax.psum_scatter(partial_value, "head", scatter_dimension=0, tiled=True)
        stream = residual[moment].astype(jnp.float32) + arrived
        normed = (rms_scale(stream) * post_gain).astype(jnp.bfloat16)
        routed = mixture(
            normed,
            expert_ids[moment : moment + 1],
            shares[moment : moment + 1],
            1,
            owners,
            own_index,
            per_step,
            expert_gate,
            expert_up,
            expert_down,
        )
        outputs.append((stream + routed).astype(jnp.bfloat16))
    return jnp.stack(outputs)


def solution(mesh):
    return jax.shard_map(
        shards,
        mesh=mesh,
        in_specs=(
            P(None, ("groups", "dev"), "head"),
            P(None, ("groups", "dev"), "head"),
            P(None, ("groups", "dev"), "head"),
            P(None, ("groups", "dev"), "head"),
            P(None, ("groups", "dev"), "head"),
            P(None, ("groups", "dev"), "head"),
            P(("groups", "dev"), "head", None, None),
            P("head", None),
            P(),
            P(None, ("groups", "dev", "head"), None),
            P(),
            P(None, "groups", None),
            P(None, "groups", None),
            P(("dev", "head"), None, None),
            P(("dev", "head"), None, None),
            P(("dev", "head"), None, None),
        ),
        out_specs=P(None, ("groups", "dev", "head"), None),
        check_vma=False,
    )
```

profile of v0, /device:TPU:0, one launch (start us, length us, event | category | flops | bytes accessed | tf_op | source)
XLA Modules:
  0.0 622.9 jit_solution(7297087957754058872)
XLA Ops:
  6.5 0.9 divide_bitcast_fusion
  8.8 0.8 slice_convert_fusion.5
  10.4 0.8 slice_convert_fusion.4
  12.1 1.0 convert_bitcast_fusion.1
  13.2 10.8 %fusion.10 = f32[16,8,1,128]{3,2,1,0:T(1,128)S(1)} fusion(f32[16,8,128,1]{2,3,1,0:T(1,128)S(1)} %bitcast.323, f32[16,8,128,128]{3,2,1,0:T(8,128)} %param.26, f32[16,8]{1,0:T(8,128)S(1)} %copy.49), kind=kOutput, calls=%fused_computation.25 | convolution fusion | flops 27262976 | bytes 8520192 | tf_op jit(solution)/shard_map/rhk,rhkv->rhv/dot_general | solution.py:58
  24.1 7.9 %fusion.12 = f32[16,8,1,128]{3,2,1,0:T(1,128)S(1)} fusion(f32[16,8,128,1]{2,3,1,0:T(1,128)S(1)} %bitcast.334, f32[16,8,128,128]{3,2,1,0:T(8,128)S(1)} %copy-done.2, f32[16,8,128]{2,1,0:T(8,128)S(1)} %fusion.139, f32[16,8,128]{2,1,0:T(8,128)S(1)} %bitcast.324, f32[16,8]{1,0:T(8,128)S(1)} %copy.49), kind=kOutput, calls=%fused_computation.27 | convolution fusion | flops 31457280 | bytes 8651264 | tf_op jit(solution)/shard_map/rhk,rhkv->rhv/dot_general | solution.py:61
  32.1 8.2 %fusion.8 = f32[16,8,1,128]{3,2,1,0:T(1,128)S(1)} fusion(f32[16,8,128,1]{2,3,1,0:T(1,128)S(1)} %bitcast.350, f32[16,8,128,128]{3,2,1,0:T(8,128)S(1)} %copy-done.2, f32[16,8]{1,0:T(8,128)S(1)} %copy.53, f32[16,8,128]{2,1,0:T(8,128)S(1)} %fusion.139, f32[16,8,128]{2,1,0:T(8,128)S(1)} %bitcast.325, f32[16,8]{1,0:T(8,128)S(1)} %copy.49), kind=kOutput, calls=%fused_computation.23 | convolution fusion | flops 33554432 | bytes 8651776 | tf_op jit(solution)/shard_map/rhk,rhkv->rhv/dot_general | solution.py:58
  40.4 11.5 %fusion.212 = f32[16,8,1,128]{3,2,1,0:T(1,128)S(1)} fusion(f32[16,8,128,1]{2,3,1,0:T(1,128)S(1)} %bitcast.363, f32[16,8,128,128]{3,2,1,0:T(8,128)S(1)} %copy-done.2, f32[16,8,128]{2,1,0:T(8,128)S(1)} %fusion.134, f32[16,8,128]{2,1,0:T(8,128)S(1)} %bitcast.351, f32[16,8]{1,0:T(8,128)S(1)} %copy.53, f32[16,8,128]{2,1,0:T(8,128)S(1)} %fusion.139, ...), kind=kOutput, calls=%fused_computation.353 | convolution fusion | flops 37748736 | bytes 8782848 | tf_op jit(solution)/shard_map/rhk,rhkv->rhv/dot_general | solution.py:61
  52.1 11.7 %fusion.6 = f32[16,8,1,128]{3,2,1,0:T(1,128)S(1)} fusion(f32[16,8,128,1]{2,3,1,0:T(1,128)S(1)} %bitcast.356, f32[16,8]{1,0:T(8,128)S(1)} %copy.57, f32[16,8,128,128]{3,2,1,0:T(8,128)S(1)} %copy-done.2, f32[16,8,128]{2,1,0:T(8,128)S(1)} %fusion.134, f32[16,8,128]{2,1,0:T(8,128)S(1)} %bitcast.352, f32[16,8]{1,0:T(8,128)S(1)} %copy.53, ...), kind=kOutput, calls=%fused_computation.21 | convolution fusion | flops 39845888 | bytes 8783360 | tf_op jit(solution)/shard_map/rhk,rhkv->rhv/dot_general | solution.py:58
  63.9 15.4 %fusion.13 = f32[16,8,1,128]{3,2,1,0:T(1,128)S(1)} fusion(f32[16,8,128,1]{2,3,1,0:T(1,128)S(1)} %bitcast.364, f32[16,8,128]{2,1,0:T(8,128)S(1)} %fusion.129, f32[16,8,128]{2,1,0:T(8,128)S(1)} %bitcast.357, f32[16,8]{1,0:T(8,128)S(1)} %copy.57, f32[16,8,128,128]{3,2,1,0:T(8,128)S(1)} %copy-done.2, f32[16,8,128]{2,1,0:T(8,128)S(1)} %fusion.134, ...), kind=kOutput, calls=%fused_computation.28 | convolution fusion | flops 44040192 | bytes 8914432 | tf_op jit(solution)/shard_map/rhk,rhkv->rhv/dot_general | solution.py:61
  79.5 15.6 %fusion.4 = f32[16,8,1,128]{3,2,1,0:T(1,128)S(1)} fusion(f32[16,8,128,1]{2,3,1,0:T(1,128)S(1)} %bitcast.360, f32[16,8]{1,0:T(8,128)S(1)} %copy.61, f32[16,8,128]{2,1,0:T(8,128)S(1)} %fusion.129, f32[16,8,128]{2,1,0:T(8,128)S(1)} %bitcast.358, f32[16,8]{1,0:T(8,128)S(1)} %copy.57, f32[16,8,128,128]{3,2,1,0:T(8,128)S(1)} %copy-done.2, ...), kind=kOutput, calls=%fused_computation.19 | convolution fusion | flops 46137344 | bytes 8914944 | tf_op jit(solution)/shard_map/rhk,rhkv->rhv/dot_general | solution.py:58
  95.2 21.0 %fusion = f32[16,8,1,128]{3,2,1,0:T(1,128)S(1)} fusion(f32[16,8,128,1]{2,3,1,0:T(1,128)S(1)} %bitcast.362, f32[16,8,128]{2,1,0:T(8,128)S(1)} %fusion.124, f32[16,8,128]{2,1,0:T(8,128)S(1)} %bitcast.361, f32[16,8]{1,0:T(8,128)S(1)} %copy.61, f32[16,8,128]{2,1,0:T(8,128)S(1)} %fusion.129, f32[16,8,128]{2,1,0:T(8,128)S(1)} %bitcast.359, ...), kind=kOutput, calls=%fused_computation.12 | convolution fusion | flops 50331648 | bytes 9046016 | tf_op jit(solution)/shard_map/rhk,rhkv->rhv/dot_general | solution.py:61
  116.6 1.3 fusion.155
  118.0 1.3 fusion.158
  119.3 1.3 fusion.152
  120.6 1.3 fusion.161
  123.8 1.6 scatter_custom_fusion.3
  126.9 1.4 scatter_custom_fusion.1
  129.7 1.4 scatter_custom_fusion.2
  132.4 1.4 scatter_custom_fusion
  136.2 1.2 compare_select_fusion.20
  138.2 1.2 compare_select_fusion.24
  141.6 1.2 compare_select_fusion.22
  142.7 1.1 compare_select_fusion.26
  143.9 19.9 %all-reduce.15.cloned.1.call-done = (f32[16,2048]{1,0:T(8,128)}, f32[16,2048]{1,0:T(8,128)}, f32[16,2048]{1,0:T(8,128)}, f32[16,2048]{1,0:T(8,128)}) async-done(((f32[16,2048]{1,0:T(8,128)}, f32[16,2048]{1,0:T(8,128)}, f32[16,2048]{1,0:T(8,128)}, f32[16,2048]{1,0:T(8,128)}), (f32[16,2048]{1,0:T(8,128)}, f32[16,2048]{1,0:T(8,128)}, f32[16,2048]{1,0:T(8,128)}, ...) | async-done | bytes 524304
  163.8 1.1 multiply_reduce_fusion.13
  165.0 1.6 fusion.172
  166.7 69.9 %all-gather = bf16[32,4,2048]{2,1,0:T(4,128)(2,1)S(1)} all-gather(bf16[1,4,2048]{2,1,0:T(4,128)(2,1)S(1)} %get-tuple-element.51), channel_id=1, replica_groups=mesh['groups'=1,'dev'=8,'head'=4] {'dev','head'}, dimensions={0}, use_global_device_ids=true | all-gather | bytes 540672 | tf_op jit(solution)/shard_map/all_gather | solution.py:81
  237.4 67.8 %all-gather.1 = bf16[32,4,2048]{2,1,0:T(4,128)(2,1)S(1)} all-gather(bf16[1,4,2048]{2,1,0:T(4,128)(2,1)S(1)} %get-tuple-element.52), channel_id=1, replica_groups=mesh['groups'=1,'dev'=8,'head'=4] {'dev','head'}, dimensions={0}, use_global_device_ids=true | all-gather | bytes 540672 | tf_op jit(solution)/shard_map/all_gather | solution.py:81
  305.4 0.8 gather_fusion.2
  306.2 69.6 %all-gather.2 = bf16[32,4,2048]{2,1,0:T(4,128)(2,1)S(1)} all-gather(bf16[1,4,2048]{2,1,0:T(4,128)(2,1)} %get-tuple-element.53), channel_id=1, replica_groups=mesh['groups'=1,'dev'=8,'head'=4] {'dev','head'}, dimensions={0}, use_global_device_ids=true | all-gather | bytes 540672 | tf_op jit(solution)/shard_map/all_gather | solution.py:81
  376.0 1.5 gather_fusion.4
  377.5 68.2 %all-gather.3 = bf16[32,4,2048]{2,1,0:T(4,128)(2,1)S(1)} all-gather(bf16[1,4,2048]{2,1,0:T(4,128)(2,1)S(1)} %get-tuple-element.54), channel_id=1, replica_groups=mesh['groups'=1,'dev'=8,'head'=4] {'dev','head'}, dimensions={0}, use_global_device_ids=true | all-gather | bytes 540672 | tf_op jit(solution)/shard_map/all_gather | solution.py:81
  445.8 1.0 gather_fusion.6
  446.8 2.1 fusion.56
  448.9 2.5 fusion.37
  451.5 1.6 fusion.147
  453.1 2.1 fusion.58
  455.2 2.5 fusion.39
  457.8 1.6 fusion.146
  459.4 2.1 fusion.60
  461.5 2.5 fusion.41
  464.1 1.6 fusion.145
  465.7 2.1 fusion.62
  467.8 2.5 fusion.43
  470.4 1.5 fusion.144
  471.9 142.0 %all-reduce.13.cloned.1.call-done = (f32[128,2048]{1,0:T(8,128)}, f32[128,2048]{1,0:T(8,128)}, f32[128,2048]{1,0:T(8,128)}, f32[128,2048]{1,0:T(8,128)}) async-done(((f32[128,2048]{1,0:T(8,128)}, f32[128,2048]{1,0:T(8,128)}, f32[128,2048]{1,0:T(8,128)}, f32[128,2048]{1,0:T(8,128)}), (f32[128,2048]{1,0:T(8,128)}, f32[128,2048]{1,0:T(8,128)}, f32[128,2048]{1,0:T(8,128)}, ...) | async-done | bytes 4194320
  614.0 1.1 fusion.176
  (188 shorter events, 16.5 us)
Async XLA Ops:
  6.5 442.4 %copy-start = (bf16[1,512,2048]{2,1,0:T(8,128)(2,1)S(1)}, bf16[1,512,2048]{2,1,0:T(8,128)(2,1)}, u32[]{:S(2)}) copy-start(bf16[1,512,2048]{2,1,0:T(8,128)(2,1)} %param.35) | copy-start | bytes 6291460
  6.5 157.2 %all-reduce.15.cloned.1.call-start = ((), (), s32[]{:S(2)}) async-start(), calls=%async_computation.1 | async-start | bytes 1048576
  11.9 12.2 %copy-start.2 = (f32[16,8,128,128]{3,2,1,0:T(8,128)S(1)}, f32[16,8,128,128]{3,2,1,0:T(8,128)}, u32[]{:S(2)}) copy-start(f32[16,8,128,128]{3,2,1,0:T(8,128)} %param.26) | copy-start | bytes 25165828
  95.1 21.1 %copy-start.6 = (bf16[4,16,1024]{2,1,0:T(8,128)(2,1)S(1)}, bf16[4,16,1024]{2,1,0:T(8,128)(2,1)}, u32[]{:S(2)}) copy-start(bf16[4,16,1024]{2,1,0:T(8,128)(2,1)} %param.23) | copy-start | bytes 393220
  95.2 21.3 %copy-start.27 = (f32[128]{0:T(128)S(1)}, f32[128]{0:T(128)}, u32[]{:S(2)}) copy-start(f32[128]{0:T(128)} %param.28) | copy-start | bytes 1540
  95.2 21.4 %copy-start.1 = (bf16[1024,2048]{1,0:T(8,128)(2,1)S(1)}, bf16[1024,2048]{1,0:T(8,128)(2,1)}, u32[]{:S(2)}) copy-start(bf16[1024,2048]{1,0:T(8,128)(2,1)} %param.27) | copy-start | bytes 12582916
  116.6 5.4 copy-start.8
  116.6 6.7 %copy-start.7 = (f32[4,128,10]{1,0,2:T(4,128)S(1)}, f32[4,128,10]{1,0,2:T(4,128)}, u32[]{:S(2)}) copy-start(f32[4,128,10]{1,0,2:T(4,128)} %param.32) | copy-start | bytes 61444
  118.0 16.1 %copy-start.28 = (u32[32]{0:T(128)S(1)}, u32[32]{0:T(128)}, u32[]{:S(2)}) copy-start(u32[32]{0:T(128)} %constant.170) | copy-start | bytes 388
  118.0 45.8 %copy-start.4 = (bf16[4,4,2048]{2,1,0:T(4,128)(2,1)S(1)}, bf16[4,4,2048]{2,1,0:T(4,128)(2,1)}, u32[]{:S(2)}) copy-start(bf16[4,4,2048]{2,1,0:T(4,128)(2,1)} %param.29) | copy-start | bytes 196612
  118.0 47.0 %copy-start.9 = (f32[2048]{0:T(1024)S(1)}, f32[2048]{0:T(1024)}, u32[]{:S(2)}) copy-start(f32[2048]{0:T(1024)} %param.30) | copy-start | bytes 24580
  121.9 492.0 %all-reduce.13.cloned.1.call-start = ((), (), s32[]{:S(2)}) async-start(), calls=%async_computation | async-start | bytes 8388608
  126.4 40.2 %copy-start.13 = (s32[48]{0:T(128)}, s32[48]{0:T(128)S(1)}, u32[]{:S(2)}) copy-start(s32[48]{0:T(128)S(1)} %get-tuple-element.42) | copy-start | bytes 580
  126.5 40.2 %copy-start.10 = (s32[1024]{0:T(1024)}, s32[1024]{0:T(1024)S(1)}, u32[]{:S(2)}) copy-start(s32[1024]{0:T(1024)S(1)} %pad_clamp_fusion) | copy-start | bytes 12292
  129.2 37.4 %copy-start.15 = (s32[48]{0:T(128)}, s32[48]{0:T(128)S(1)}, u32[]{:S(2)}) copy-start(s32[48]{0:T(128)S(1)} %get-tuple-element.34) | copy-start | bytes 580
  129.2 37.4 %copy-start.11 = (s32[1024]{0:T(1024)}, s32[1024]{0:T(1024)S(1)}, u32[]{:S(2)}) copy-start(s32[1024]{0:T(1024)S(1)} %pad_clamp_fusion.2) | copy-start | bytes 12292
  132.0 34.7 %copy-start.17 = (s32[48]{0:T(128)}, s32[48]{0:T(128)S(1)}, u32[]{:S(2)}) copy-start(s32[48]{0:T(128)S(1)} %get-tuple-element.38) | copy-start | bytes 580
  132.0 34.7 %copy-start.12 = (s32[1024]{0:T(1024)}, s32[1024]{0:T(1024)S(1)}, u32[]{:S(2)}) copy-start(s32[1024]{0:T(1024)S(1)} %pad_clamp_fusion.1) | copy-start | bytes 12292
  140.8 25.9 %copy-start.19 = (s32[48]{0:T(128)}, s32[48]{0:T(128)S(1)}, u32[]{:S(2)}) copy-start(s32[48]{0:T(128)S(1)} %get-tuple-element.30) | copy-start | bytes 580
  445.7 5.8 copy-start.14
  445.7 7.4 %copy-start.23 = (pred[48]{0:T(512)(128)(4,1)S(1)}, pred[48]{0:T(512)(128)(4,1)}, u32[]{:S(2)}) copy-start(pred[48]{0:T(512)(128)(4,1)} %get-tuple-element.36) | copy-start | bytes 148
  445.7 9.5 %copy-start.26 = (f32[48]{0:T(128)S(1)}, f32[48]{0:T(128)}, u32[]{:S(2)}) copy-start(f32[48]{0:T(128)} %get-tuple-element.35) | copy-start | bytes 580
  445.8 7.3 %copy-start.3 = (bf16[48,2048]{1,0:T(8,128)(2,1)S(1)}, bf16[48,2048]{1,0:T(8,128)(2,1)}, u32[]{:S(2)}) copy-start(bf16[48,2048]{1,0:T(8,128)(2,1)} %gather_fusion.4) | copy-start | bytes 589828
  446.8 11.0 %copy-start.18 = (s32[48]{0:T(128)S(1)}, s32[48]{0:T(128)}, u32[]{:S(2)}) copy-start(s32[48]{0:T(128)} %copy-done.17) | copy-start | bytes 580
  446.8 12.6 %copy-start.21 = (pred[48]{0:T(512)(128)(4,1)S(1)}, pred[48]{0:T(512)(128)(4,1)}, u32[]{:S(2)}) copy-start(pred[48]{0:T(512)(128)(4,1)} %get-tuple-element.32) | copy-start | bytes 148
  448.9 12.6 %copy-start.24 = (f32[48]{0:T(128)S(1)}, f32[48]{0:T(128)}, u32[]{:S(2)}) copy-start(f32[48]{0:T(128)} %get-tuple-element.31) | copy-start | bytes 580
  451.5 12.6 %copy-start.16 = (s32[48]{0:T(128)S(1)}, s32[48]{0:T(128)}, u32[]{:S(2)}) copy-start(s32[48]{0:T(128)} %copy-done.15) | copy-start | bytes 580
  453.1 12.6 %copy-start.22 = (pred[48]{0:T(512)(128)(4,1)S(1)}, pred[48]{0:T(512)(128)(4,1)}, u32[]{:S(2)}) copy-start(pred[48]{0:T(512)(128)(4,1)} %get-tuple-element.28) | copy-start | bytes 148
  455.2 12.6 %copy-start.25 = (f32[48]{0:T(128)S(1)}, f32[48]{0:T(128)}, u32[]{:S(2)}) copy-start(f32[48]{0:T(128)} %get-tuple-element.27) | copy-start | bytes 580
  457.8 12.6 %copy-start.20 = (s32[48]{0:T(128)S(1)}, s32[48]{0:T(128)}, u32[]{:S(2)}) copy-start(s32[48]{0:T(128)} %copy-done.19) | copy-start | bytes 580
  464.1 149.9 %copy-start.5 = (bf16[4,4,2048]{2,1,0:T(4,128)(2,1)S(1)}, bf16[4,4,2048]{2,1,0:T(4,128)(2,1)}, u32[]{:S(2)}) copy-start(bf16[4,4,2048]{2,1,0:T(4,128)(2,1)} %param.29) | copy-start | bytes 196612
Sparse Core Ops, SparseCore 0:
  122.0 41.6 all-reduce.14
  472.1 141.8 all-reduce.12
where the time goes:
time: 627 us; the launch traced here: 623 us
  blocking collectives  276 us (44%)
  waiting for transfers between devices  162 us (26%)
  matrix products  132 us (21%)
  other arithmetic  26.7 us (4%)
  between operations  15.4 us (2%)
  local copies, waits for them, and re-layouts  10.9 us (2%)
    all_gather x4, blocking collectives, mixture(): gathered = lax.all_gather(normed, ('dev', 'head'), axis=0, tiled=True)  276 us
    unnamed x4, waiting for transfers between devices  162 us
    dot_general x4, matrix products, attend(): jnp.einsum('rhk,rhkv->rhv', query_rows, memory, precision=highest)  55.8 us
    dot_general x4, matrix products, attend(): recalled = jnp.einsum('rhk,rhkv->rhv', key_rows, memory, precision=highest)  46.2 us
  transfers between devices with their start and end apart: 2, of which 2 were waited for; matrix products, arithmetic and copies ran while one was open for 3% of the time, Pallas kernels for 0%

commit v1 on v0

v1 whole, which is shorter than its diff:
```python
import functools

import jax
import jax.numpy as jnp
from jax import lax
from jax.experimental import pallas as pl
from jax.experimental.pallas import tpu as pltpu
from jax.sharding import PartitionSpec as P

HK = 128
HV = 128
EPS = 1e-06


def attend_kernel(
    place,
    q_ref,
    k_ref,
    v_ref,
    gate_ref,
    beta_ref,
    decay_ref,
    gain_ref,
    states_hbm,
    weight_hbm,
    *rest,
    blocks,
):
    own_ref, send_refs = rest[0], rest[1:blocks]
    state, weight, rows, reads, gated, state_sems, weight_sem = rest[blocks:]
    steps, requests, _ = q_ref.shape
    heads = v_ref.shape[2] // HV
    pairs = q_ref.shape[2] // HK
    repeat = heads // pairs
    each = requests // blocks
    vectors = 2 * steps

    for r in range(requests):
        pltpu.make_async_copy(states_hbm.at[r], state.at[r], state_sems.at[r]).start()
    pltpu.make_async_copy(weight_hbm, weight, weight_sem.at[0]).start()

    unit_q, unit_k = {}, {}
    for g in range(pairs):
        lanes = slice(g * HK, (g + 1) * HK)
        for t in range(steps):
            q = q_ref[t, :, lanes].astype(jnp.float32)
            k = k_ref[t, :, lanes].astype(jnp.float32)
            q = q * lax.rsqrt(jnp.sum(q * q, axis=-1, keepdims=True) + EPS) * HK ** (-0.5)
            k = k * lax.rsqrt(jnp.sum(k * k, axis=-1, keepdims=True) + EPS)
            rows[g, pl.ds(t, requests, stride=vectors), :] = q
            rows[g, pl.ds(steps + t, requests, stride=vectors), :] = k
            unit_q[g, t], unit_k[g, t] = q, k

    def read_states(r, carry):
        pltpu.make_async_copy(states_hbm.at[r], state.at[r], state_sems.at[r]).wait()
        at = pl.ds(pl.multiple_of(r * vectors, vectors), vectors)
        for g in range(pairs):
            left = rows[g, at, :].astype(jnp.bfloat16)
            for h in range(g * repeat, (g + 1) * repeat):
                reads[h, at, :] = jnp.dot(
                    left, state[r, h].astype(jnp.bfloat16), preferred_element_type=jnp.float32
                )
        return carry

    lax.fori_loop(0, requests, read_states, 0)

    for g in range(pairs):
        kk, qk = {}, {}
        for t in range(steps):
            for s in range(t + 1):
                qk[t, s] = jnp.sum(unit_q[g, t] * unit_k[g, s], axis=-1, keepdims=True)
                if s < t:
                    kk[t, s] = jnp.sum(unit_k[g, t] * unit_k[g, s], axis=-1, keepdims=True)
        for h in range(g * repeat, (g + 1) * repeat):
            lanes = slice(h * HV, (h + 1) * HV)
            decay = [decay_ref[t, :, h : h + 1] for t in range(steps)]
            span = {}
            for t in range(steps):
                span[t, t] = None
                for s in range(t - 1, -2, -1):
                    last = span[t, s + 1]
                    span[t, s] = decay[s + 1] if last is None else last * decay[s + 1]
            deltas = []
            for t in range(steps):
                start_q = reads[h, pl.ds(t, requests, stride=vectors), :]
                start_k = reads[h, pl.ds(steps + t, requests, stride=vectors), :]
                recalled = span[t, -1] * start_k
                for s in range(t):
                    recalled = recalled + (span[t, s] * kk[t, s]) * deltas[s]
                beta = jax.nn.sigmoid(beta_ref[t, :, h : h + 1])
                deltas.append((v_ref[t, :, lanes].astype(jnp.float32) - recalled) * beta)
                read = span[t, -1] * start_q
                for s in range(t + 1):
                    factor = qk[t, s] if s == t else span[t, s] * qk[t, s]
                    read = read + factor * deltas[s]
                scale = lax.rsqrt(jnp.mean(read * read, axis=-1, keepdims=True) + EPS)
                gate = gate_ref[t, :, lanes].astype(jnp.float32)
                value = read * scale * gain_ref[...] * jax.nn.silu(gate)
                gated[pl.ds(t * requests, requests), lanes] = value.astype(jnp.bfloat16)

    total = steps * requests
    new = lax.broadcasted_iota(jnp.int32, (total, total), 0)
    old = lax.broadcasted_iota(jnp.int32, (total, total), 1)
    block = new // (steps * each) + place[0]
    block = jnp.where(block >= blocks, block - blocks, block)
    within = new % (steps * each)
    source = (within // each) * requests + block * each + within % each
    chosen = jnp.where(source == old, 1.0, 0.0).astype(jnp.bfloat16)
    ordered = jnp.dot(chosen, gated[...], preferred_element_type=jnp.float32).astype(jnp.bfloat16)

    pltpu.make_async_copy(weight_hbm, weight, weight_sem.at[0]).wait()
    size = steps * each
    columns = weight.shape[1]
    tile = min(512, columns)
    for c in range(0, columns, tile):
        part = jnp.dot(ordered, weight[:, c : c + tile], preferred_element_type=jnp.float32)
        own_ref[:, c : c + tile] = part[:size]
        for k in range(1, blocks):
            send_refs[k - 1][:, c : c + tile] = part[k * size : (k + 1) * size].astype(jnp.bfloat16)


def attend(place, queries, keys_in, values_in, out_gate, beta_logit, decay_rate, gain, states, weight, blocks):
    steps, requests, _ = queries.shape
    heads = values_in.shape[2] // HV
    pairs = queries.shape[2] // HK
    size = steps * requests // blocks
    columns = weight.shape[1]
    whole = pl.BlockSpec(memory_space=pltpu.VMEM)
    away = pl.BlockSpec(memory_space=pl.ANY)
    return pl.pallas_call(
        functools.partial(attend_kernel, blocks=blocks),
        out_shape=[jax.ShapeDtypeStruct((size, columns), jnp.float32)]
        + [jax.ShapeDtypeStruct((size, columns), jnp.bfloat16)] * (blocks - 1),
        in_specs=[pl.BlockSpec(memory_space=pltpu.SMEM)] + [whole] * 7 + [away] * 2,
        out_specs=[whole] * blocks,
        scratch_shapes=[
            pltpu.VMEM(states.shape, jnp.float32),
            pltpu.VMEM(weight.shape, jnp.bfloat16),
            pltpu.VMEM((pairs, requests * 2 * steps, HK), jnp.float32),
            pltpu.VMEM((heads, requests * 2 * steps, HV), jnp.float32),
            pltpu.VMEM((steps * requests, heads * HV), jnp.bfloat16),
            pltpu.SemaphoreType.DMA((requests,)),
            pltpu.SemaphoreType.DMA((1,)),
        ],
        compiler_params=pltpu.CompilerParams(vmem_limit_bytes=32 << 20),
        name="attend",
    )(place, queries, keys_in, values_in, out_gate, beta_logit, decay_rate, gain, states, weight)


def norm_kernel(own_ref, residual_ref, gain_ref, *rest):
    stream_ref, normed_ref = rest[-2:]
    stream = residual_ref[...].astype(jnp.float32) + own_ref[...]
    for ref in rest[:-2]:
        stream = stream + ref[...].astype(jnp.float32)
    stream_ref[...] = stream
    scale = lax.rsqrt(jnp.mean(stream * stream, axis=-1, keepdims=True) + EPS)
    normed_ref[...] = (stream * scale * gain_ref[...]).astype(jnp.bfloat16)


def experts_kernel(x_ref, share_ref, gate_hbm, up_hbm, down_hbm, out_ref, gate, up, down, sems):
    copies = [
        pltpu.make_async_copy(src, dst, sems.at[i])
        for i, (src, dst) in enumerate(((gate_hbm, gate), (up_hbm, up), (down_hbm, down)))
    ]
    for copy in copies:
        copy.start()
    for copy in copies:
        copy.wait()
    count = x_ref.shape[0]
    tile = min(128, count)

    def serve(i, carry):
        at = pl.ds(pl.multiple_of(i * tile, tile), tile)
        x = x_ref[at, :]
        gated = jnp.dot(x, gate[...], preferred_element_type=jnp.float32)
        lifted = jnp.dot(x, up[...], preferred_element_type=jnp.float32)
        hidden = (jax.nn.silu(gated) * lifted).astype(jnp.bfloat16)
        served = jnp.dot(hidden, down[...], preferred_element_type=jnp.float32)
        served = served.astype(jnp.bfloat16).astype(jnp.float32) * share_ref[at, :]
        out_ref[at, :] = served.astype(out_ref.dtype)
        return carry

    lax.fori_loop(0, count // tile, serve, 0)


def experts(x, share, gate, up, down, dtype):
    whole = pl.BlockSpec(memory_space=pltpu.VMEM)
    away = pl.BlockSpec(memory_space=pl.ANY)
    return pl.pallas_call(
        experts_kernel,
        out_shape=jax.ShapeDtypeStruct(x.shape, dtype),
        in_specs=[whole, whole, away, away, away],
        out_specs=whole,
        scratch_shapes=[
            pltpu.VMEM(gate.shape, gate.dtype),
            pltpu.VMEM(up.shape, up.dtype),
            pltpu.VMEM(down.shape, down.dtype),
            pltpu.SemaphoreType.DMA((3,)),
        ],
        compiler_params=pltpu.CompilerParams(vmem_limit_bytes=32 << 20),
        name="experts",
    )(x, share, gate, up, down)


def shards(
    queries,
    keys_in,
    values_in,
    out_gate,
    beta_logit,
    decay_rate,
    states,
    out_weight,
    head_gain,
    residual,
    post_gain,
    expert_ids,
    route_weight,
    expert_gate,
    expert_up,
    expert_down,
):
    ring, width = lax.axis_size("head"), lax.axis_size("dev")
    place, spot = lax.axis_index("head"), lax.axis_index("dev")
    steps, each, columns = residual.shape
    size = steps * each
    bits = (width // 2).bit_length() - 1
    core = spot % 2

    def along(x, k):
        return lax.ppermute(x, "head", [(i, (i + k) % ring) for i in range(ring)])

    def across(x, j):
        return lax.ppermute(
            x, "dev", [(i, i ^ (2 << ((j + i % 2) % bits))) for i in range(width)]
        )

    def other(x):
        return lax.ppermute(x, "dev", [(i, i ^ 1) for i in range(width)])

    def shares_of(spot, core):
        owners = []
        for m in range(1 << bits):
            mask = 0
            for j in range(bits):
                if m >> j & 1:
                    mask = mask + (2 << ((j + core) % bits))
            for k in range(ring):
                owners.append((spot ^ mask) * ring + (place + k) % ring)
        return jnp.stack(owners)

    shares = route_weight / jnp.sum(route_weight, axis=-1, keepdims=True)
    own = spot * ring + place
    picked = jnp.sum(jnp.where(expert_ids == own, shares, 0.0), axis=-1)
    picked = picked.reshape(steps, width * ring, each).transpose(1, 0, 2).reshape(width * ring, size)

    own_shares = jnp.take(picked, shares_of(spot, core), axis=0).reshape(-1, 1)
    peer_shares = jnp.take(picked, shares_of(spot ^ 1, 1 - core), axis=0).reshape(-1, 1)

    parts = attend(
        place.astype(jnp.int32).reshape(1),
        queries,
        keys_in,
        values_in,
        out_gate,
        beta_logit,
        decay_rate,
        head_gain.reshape(1, HV),
        states,
        out_weight,
        ring,
    )
    arrived = [along(parts[k], k) for k in range(1, ring)]
    stream, normed = pl.pallas_call(
        norm_kernel,
        out_shape=[
            jax.ShapeDtypeStruct((size, columns), jnp.float32),
            jax.ShapeDtypeStruct((size, columns), jnp.bfloat16),
        ],
        name="norm",
    )(parts[0], residual.reshape(size, columns), post_gain.reshape(1, columns), *arrived)

    rows = jnp.concatenate([normed] + [along(normed, ring - k) for k in range(1, ring)])
    for j in range(bits):
        rows = jnp.concatenate([rows, across(rows, j)])
    peer_rows = other(rows)
    weights = (expert_gate[0], expert_up[0], expert_down[0])
    peer_served = experts(peer_rows, peer_shares, *weights, jnp.bfloat16)
    served = experts(rows, own_shares, *weights, jnp.float32)
    total = served + other(peer_served).astype(jnp.float32)
    for j in reversed(range(bits)):
        half = total.shape[0] // 2
        total = total[:half] + across(total[half:].astype(jnp.bfloat16), j).astype(jnp.float32)
    routed = stream + total[:size]
    for k in range(1, ring):
        block = total[k * size : (k + 1) * size].astype(jnp.bfloat16)
        routed = routed + along(block, k).astype(jnp.float32)
    return routed.astype(jnp.bfloat16).reshape(steps, each, columns)


def solution(mesh):
    return jax.shard_map(
        shards,
        mesh=mesh,
        in_specs=(
            P(None, ("groups", "dev"), "head"),
            P(None, ("groups", "dev"), "head"),
            P(None, ("groups", "dev"), "head"),
            P(None, ("groups", "dev"), "head"),
            P(None, ("groups", "dev"), "head"),
            P(None, ("groups", "dev"), "head"),
            P(("groups", "dev"), "head", None, None),
            P("head", None),
            P(),
            P(None, ("groups", "dev", "head"), None),
            P(),
            P(None, "groups", None),
            P(None, "groups", None),
            P(("dev", "head"), None, None),
            P(("dev", "head"), None, None),
            P(("dev", "head"), None, None),
        ),
        out_specs=P(None, ("groups", "dev", "head"), None),
        check_vma=False,
    )
```

time: 627 us -> 106 us (0.17)
  blocking collectives: 276 us -> 0 us
  matrix products: 132 us -> 0 us
  waiting for transfers between devices: 162 us -> 36.5 us
  other arithmetic: 26.7 us -> 2.82 us
  starting transfers between devices: 0.04 us -> 20.8 us
  Pallas kernels: 0 us -> 17.5 us
  local copies, waits for them, and re-layouts: 10.9 us -> 27.3 us
  between operations: 15.4 us -> 0.36 us
    all_gather x4 -> x0, blocking collectives: 276 us -> none  [mixture(): gathered = lax.all_gather(normed, ('dev', 'head'), axis=0, tiled=True)]
    unnamed x4 -> x0, waiting for transfers between devices: 162 us -> none
    dot_general x24 -> x0, matrix products: 132 us -> none  [the longest x4 55.8 us: attend(): jnp.einsum('rhk,rhkv->rhv', query_rows, memory, precision=highest)]
    ppermute x0 -> x15, waiting for transfers between devices: none -> 36.5 us  [the longest x4 24 us: across(): lax.ppermute(x, 'dev', [(i, i ^ 2 << (j + i % 2) % bits) for i in range(w...]
    unnamed x72 -> x46, local copies, waits for them, and re-layouts: 1.39 us -> 22.3 us
    ppermute x0 -> x15, starting transfers between devices: none -> 20.8 us  [the longest x9 14.9 us: along(): return lax.ppermute(x, 'head', [(i, (i + k) % ring) for i in range(ring)])]
    pallas_call x0 -> x4, Pallas kernels: none -> 17.5 us  [the longest x1 8.24 us: attend(): pl.pallas_call(functools.partial(attend_kernel, blocks=blocks), out_shape...]
    select_n x12 -> x4, other arithmetic: 7.58 us -> 0.15 us  [the longest x2 0.08 us: shards(): jnp.take(picked, shares_of(spot ^ 1, 1 - core), axis=0).reshape(-1, 1)]
  transfers between devices with their start and end apart: 2 -> 15, of which waited for: 2 -> 13; matrix products, arithmetic and copies ran while one was open for 3% -> 6% of each run, Pallas kernels for 0% -> 3%
where the time goes in v1:
time: 106 us; the launch traced here: 105 us
  waiting for transfers between devices  36.5 us (34%)
  local copies, waits for them, and re-layouts  27.3 us (26%)
  starting transfers between devices  20.8 us (20%)
  Pallas kernels  17.5 us (17%)
  other arithmetic  2.82 us (3%)
    ppermute x4, waiting for transfers between devices, across(): lax.ppermute(x, 'dev', [(i, i ^ 2 << (j + i % 2) % bits) for i in range(w...  24 us
    unnamed x46, local copies, waits for them, and re-layouts  22.3 us
    ppermute x9, starting transfers between devices, along(): return lax.ppermute(x, 'head', [(i, (i + k) % ring) for i in range(ring)])  14.9 us
    ppermute x9, waiting for transfers between devices, along(): return lax.ppermute(x, 'head', [(i, (i + k) % ring) for i in range(ring)])  11.2 us
    pallas_call x1, Pallas kernels, attend(): pl.pallas_call(functools.partial(attend_kernel, blocks=blocks), out_shape...  8.24 us
    pallas_call x2, Pallas kernels, experts(): pl.pallas_call(experts_kernel, out_shape=jax.ShapeDtypeStruct(x.shape, dt...  7.52 us
    ppermute x4, starting transfers between devices, across(): lax.ppermute(x, 'dev', [(i, i ^ 2 << (j + i % 2) % bits) for i in range(w...  5.7 us
  transfers between devices with their start and end apart: 15, of which 13 were waited for; matrix products, arithmetic and copies ran while one was open for 6% of the time, Pallas kernels for 3%

profile of v1, /device:TPU:0, one launch (start us, length us, event | category | flops | bytes accessed | tf_op | source)
XLA Modules:
  0.0 105.4 jit_solution(15956882760266273941)
XLA Ops:
  0.0 0.8 copy.19.beta_ref
  0.8 0.8 copy.20.decay_ref
  1.6 3.4 %copy-done = f32[16,8,128,128]{3,2,1,0:T(8,128)S(1)} copy-done((f32[16,8,128,128]{3,2,1,0:T(8,128)S(1)}, f32[16,8,128,128]{3,2,1,0:T(8,128)}, u32[]{:S(2)}) %copy-start) | copy-done | bytes 8388632
  5.0 2.2 %copy-done.6 = bf16[1024,2048]{1,0:T(8,128)(2,1)S(1)} copy-done((bf16[1024,2048]{1,0:T(8,128)(2,1)S(1)}, bf16[1024,2048]{1,0:T(8,128)(2,1)}, u32[]{:S(2)}) %copy-start.6) | copy-done | bytes 4194328
  7.2 0.9 copy-done.7
  8.1 0.9 copy-done.8
  9.0 0.8 copy-done.10
  9.8 0.8 copy-done.11
  10.6 0.7 copy-done.12
  11.3 8.2 %attend.1 = (f32[16,2048]{1,0:T(8,128)S(1)}, bf16[16,2048]{1,0:T(8,128)(2,1)S(1)}, bf16[16,2048]{1,0:T(8,128)(2,1)S(1)}, bf16[16,2048]{1,0:T(8,128)(2,1)S(1)}) custom-call(s32[1]{0:T(128)} %bitcast.place, bf16[4,16,512]{2,1,0:T(8,128)(2,1)S(1)} %copy-done.10, bf16[4,16,512]{2,1,0:T(8,128)(2,1)S(1)} %copy-done.11, bf16[4,16,1024]{2,1,0:T(8,128)(2,1)S(1)} %copy-done.7, ...), custom_call_target="tpu_custom_call" | custom-call | tf_op jit(solution)/shard_map/attend/pallas_call | solution.py:130
  19.6 0.6 copy-done.9
  20.2 3.0 %collective-permute-start = (bf16[16,2048]{1,0:T(8,128)(2,1)S(1)}, bf16[16,2048]{1,0:T(8,128)(2,1)S(1)}, u32[]{:S(2)}, u32[]{:S(2)}) collective-permute-start(bf16[16,2048]{1,0:T(8,128)(2,1)S(1)} %get-tuple-element.13), channel_id=1, source_target_pairs={{0,1},{1,2},{2,3},{3,0},{4,5},{5,6},{6,7},{7,4},{8,9},{9,10},{10,1... | collective-permute-start | bytes 196616 | tf_op jit(solution)/shard_map/ppermute | solution.py:231
  23.2 2.6 %collective-permute-start.1 = (bf16[16,2048]{1,0:T(8,128)(2,1)S(1)}, bf16[16,2048]{1,0:T(8,128)(2,1)S(1)}, u32[]{:S(2)}, u32[]{:S(2)}) collective-permute-start(bf16[16,2048]{1,0:T(8,128)(2,1)S(1)} %get-tuple-element.14), channel_id=1, source_target_pairs={{0,2},{1,3},{2,0},{3,1},{4,6},{5,7},{6,4},{7,5},{8,10},{9,11},{10,... | collective-permute-start | bytes 196616 | tf_op jit(solution)/shard_map/ppermute | solution.py:231
  25.8 1.3 %collective-permute-start.2 = (bf16[16,2048]{1,0:T(8,128)(2,1)S(1)}, bf16[16,2048]{1,0:T(8,128)(2,1)S(1)}, u32[]{:S(2)}, u32[]{:S(2)}) collective-permute-start(bf16[16,2048]{1,0:T(8,128)(2,1)S(1)} %get-tuple-element.15), channel_id=1, source_target_pairs={{0,3},{1,0},{2,1},{3,2},{4,7},{5,4},{6,5},{7,6},{8,11},{9,8},{10,9... | collective-permute-start | bytes 196616 | tf_op jit(solution)/shard_map/ppermute | solution.py:231
  27.2 0.6 reshape.35.residual_ref
  27.8 2.5 %collective-permute-done.1.rest_1_ = bf16[16,2048]{1,0:T(8,128)(2,1)S(1)} collective-permute-done((bf16[16,2048]{1,0:T(8,128)(2,1)S(1)}, bf16[16,2048]{1,0:T(8,128)(2,1)S(1)}, u32[]{:S(2)}, u32[]{:S(2)}) %collective-permute-start.1) | collective-permute-done | bytes 65568 | tf_op jit(solution)/shard_map/ppermute | solution.py:231
  31.1 1.8 %norm.1 = (f32[16,2048]{1,0:T(8,128)}, bf16[16,2048]{1,0:T(8,128)(2,1)}) custom-call(f32[16,2048]{1,0:T(8,128)} %copy-done.9, bf16[16,2048]{1,0:T(8,128)(2,1)} %reshape.35.residual_ref, f32[1,2048]{1,0:T(1,128)} %bitcast.49, bf16[16,2048]{1,0:T(8,128)(2,1)} %copy-done.15, bf16[16,2048]{1,0:T(8,128)(2,1)} %copy-done.16, bf16[16,2048]{1,0:T(8,128)(2,1)} %copy-done.17), custom_call_target="tpu_custom_call" | custom-call | tf_op jit(solution)/shard_map/norm/pallas_call | solution.py:274
  32.9 1.6 %collective-permute-start.5 = (bf16[16,2048]{1,0:T(8,128)(2,1)}, bf16[16,2048]{1,0:T(8,128)(2,1)S(1)}, u32[]{:S(2)}, u32[]{:S(2)}) collective-permute-start(bf16[16,2048]{1,0:T(8,128)(2,1)} %get-tuple-element.17), channel_id=1, source_target_pairs={{0,1},{1,2},{2,3},{3,0},{4,5},{5,6},{6,7},{7,4},{8,9},{9,10},{10,1... | collective-permute-start | bytes 196616 | tf_op jit(solution)/shard_map/ppermute | solution.py:231
  34.5 2.0 %collective-permute-start.4 = (bf16[16,2048]{1,0:T(8,128)(2,1)}, bf16[16,2048]{1,0:T(8,128)(2,1)S(1)}, u32[]{:S(2)}, u32[]{:S(2)}) collective-permute-start(bf16[16,2048]{1,0:T(8,128)(2,1)} %get-tuple-element.17), channel_id=1, source_target_pairs={{0,2},{1,3},{2,0},{3,1},{4,6},{5,7},{6,4},{7,5},{8,10},{9,11},{10,... | collective-permute-start | bytes 196616 | tf_op jit(solution)/shard_map/ppermute | solution.py:231
  36.9 1.5 %constant_dynamic-update-slice_fusion.4 = (bf16[128,2048]{1,0:T(8,128)(2,1)}, bf16[256,2048]{1,0:T(8,128)(2,1)S(1)}) fusion(bf16[16,2048]{1,0:T(8,128)(2,1)} %get-tuple-element.17), kind=kLoop, calls=%fused_computation.17 | loop fusion | bytes 196608
  38.4 1.0 collective-permute-done.5
  39.5 2.0 %collective-permute-done.4 = bf16[16,2048]{1,0:T(8,128)(2,1)S(1)} collective-permute-done((bf16[16,2048]{1,0:T(8,128)(2,1)}, bf16[16,2048]{1,0:T(8,128)(2,1)S(1)}, u32[]{:S(2)}, u32[]{:S(2)}) %collective-permute-start.4) | collective-permute-done | bytes 65568 | tf_op jit(solution)/shard_map/ppermute | solution.py:231
  41.7 0.9 pad_maximum_fusion
  42.6 1.4 %collective-permute-start.6 = (bf16[64,2048]{1,0:T(8,128)(2,1)S(1)}, bf16[64,2048]{1,0:T(8,128)(2,1)S(1)}, u32[]{:S(2)}, u32[]{:S(2)}) collective-permute-start(bf16[64,2048]{1,0:T(8,128)(2,1)S(1)} %pad_maximum_fusion), channel_id=1, source_target_pairs={{0,8},{4,20},{8,0},{12,28},{16,24},{20,4},{24,16},{28,12},{1,9},{5... | collective-permute-start | bytes 786440 | tf_op jit(solution)/shard_map/ppermute | solution.py:234
  45.3 0.6 constant_dynamic-update-slice_fusion.1
  45.9 3.1 %collective-permute-done.6 = bf16[64,2048]{1,0:T(8,128)(2,1)S(1)} collective-permute-done((bf16[64,2048]{1,0:T(8,128)(2,1)S(1)}, bf16[64,2048]{1,0:T(8,128)(2,1)S(1)}, u32[]{:S(2)}, u32[]{:S(2)}) %collective-permute-start.6) | collective-permute-done | bytes 262176 | tf_op jit(solution)/shard_map/ppermute | solution.py:234
  49.0 0.7 constant_dynamic-update-slice_fusion
  49.8 1.4 %collective-permute-start.7 = (bf16[128,2048]{1,0:T(8,128)(2,1)}, bf16[128,2048]{1,0:T(8,128)(2,1)}, u32[]{:S(2)}, u32[]{:S(2)}) collective-permute-start(bf16[128,2048]{1,0:T(8,128)(2,1)} %get-tuple-element.23), channel_id=1, source_target_pairs={{0,16},{4,12},{8,24},{12,4},{16,0},{20,28},{24,8},{28,20},{1,17},{... | collective-permute-start | bytes 1572872 | tf_op jit(solution)/shard_map/ppermute | solution.py:234
  51.2 8.1 %collective-permute-done.7 = bf16[128,2048]{1,0:T(8,128)(2,1)} collective-permute-done((bf16[128,2048]{1,0:T(8,128)(2,1)}, bf16[128,2048]{1,0:T(8,128)(2,1)}, u32[]{:S(2)}, u32[]{:S(2)}) %collective-permute-start.7) | collective-permute-done | bytes 524320 | tf_op jit(solution)/shard_map/ppermute | solution.py:234
  59.3 1.1 %constant_dynamic-update-slice_fusion.5.x_ref = bf16[256,2048]{1,0:T(8,128)(2,1)S(1)} fusion(bf16[256,2048]{1,0:T(8,128)(2,1)S(1)} %get-tuple-element.24, bf16[128,2048]{1,0:T(8,128)(2,1)} %collective-permute-done.7), kind=kLoop, calls=%fused_computation.18 | loop fusion | bytes 1048576 | tf_op jit(solution)/shard_map/concatenate | solution.py:285
  61.9 1.3 %collective-permute-done.8.x_ref = bf16[256,2048]{1,0:T(8,128)(2,1)} collective-permute-done((bf16[256,2048]{1,0:T(8,128)(2,1)S(1)}, bf16[256,2048]{1,0:T(8,128)(2,1)}, u32[]{:S(2)}, u32[]{:S(2)}) %collective-permute-start.8) | collective-permute-done | bytes 1048608 | tf_op jit(solution)/shard_map/ppermute | solution.py:239
  63.2 1.6 %copy-done.2 = bf16[1,2048,512]{2,1,0:T(8,128)(2,1)S(1)} copy-done((bf16[1,2048,512]{2,1,0:T(8,128)(2,1)S(1)}, bf16[1,2048,512]{2,1,0:T(8,128)(2,1)}, u32[]{:S(2)}) %copy-start.2) | copy-done | bytes 2097176
  64.8 1.6 %copy-done.4 = bf16[1,512,2048]{2,1,0:T(8,128)(2,1)S(1)} copy-done((bf16[1,512,2048]{2,1,0:T(8,128)(2,1)S(1)}, bf16[1,512,2048]{2,1,0:T(8,128)(2,1)}, u32[]{:S(2)}) %copy-start.4) | copy-done | bytes 2097176
  66.4 4.9 %experts.3 = bf16[256,2048]{1,0:T(8,128)(2,1)} custom-call(bf16[256,2048]{1,0:T(8,128)(2,1)} %collective-permute-done.8.x_ref, f32[256,1]{1,0:T(8,128)S(1)} %reshape.65.share_ref, bf16[2048,512]{1,0:T(8,128)(2,1)S(1)} %bitcast.40, bf16[2048,512]{1,0:T(8,128)(2,1)S(1)} %bitcast.42, bf16[512,2048]{1,0:T(8,128)(2,1)S(1)} %bitcast.44), custom_call_target="tpu_custom_call" | custom-call | tf_op jit(solution)/shard_map/experts/pallas_call | solution.py:189
  72.2 1.6 %copy-done.3 = bf16[1,2048,512]{2,1,0:T(8,128)(2,1)S(1)} copy-done((bf16[1,2048,512]{2,1,0:T(8,128)(2,1)S(1)}, bf16[1,2048,512]{2,1,0:T(8,128)(2,1)}, u32[]{:S(2)}) %copy-start.3) | copy-done | bytes 2097176
  73.8 1.6 %copy-done.5 = bf16[1,512,2048]{2,1,0:T(8,128)(2,1)S(1)} copy-done((bf16[1,512,2048]{2,1,0:T(8,128)(2,1)S(1)}, bf16[1,512,2048]{2,1,0:T(8,128)(2,1)}, u32[]{:S(2)}) %copy-start.5) | copy-done | bytes 2097176
  75.4 2.7 %experts.2 = f32[256,2048]{1,0:T(8,128)S(1)} custom-call(bf16[256,2048]{1,0:T(8,128)(2,1)S(1)} %constant_dynamic-update-slice_fusion.5.x_ref, f32[256,1]{1,0:T(8,128)S(1)} %reshape.64.share_ref, bf16[2048,512]{1,0:T(8,128)(2,1)S(1)} %bitcast.41, bf16[2048,512]{1,0:T(8,128)(2,1)S(1)} %bitcast.43, bf16[512,2048]{1,0:T(8,128)(2,1)S(1)} %bitcast.45), custom_call_target="tpu_custom_call" | custom-call | tf_op jit(solution)/shard_map/experts/pallas_call | solution.py:189
  78.1 1.5 %convert_add_fusion = f32[256,2048]{1,0:T(8,128)S(1)} fusion(f32[256,2048]{1,0:T(8,128)S(1)} %experts.2, bf16[256,2048]{1,0:T(8,128)(2,1)} %collective-permute-done.9), kind=kLoop, calls=%fused_computation.2 | loop fusion | flops 1048576 | bytes 5242880 | tf_op jit(solution)/shard_map/add | solution.py:290
  79.7 1.5 %collective-permute-start.10 = (bf16[128,2048]{1,0:T(8,128)(2,1)S(1)}, bf16[128,2048]{1,0:T(8,128)(2,1)S(1)}, u32[]{:S(2)}, u32[]{:S(2)}) collective-permute-start(bf16[128,2048]{1,0:T(8,128)(2,1)S(1)} %slice.62), channel_id=1, source_target_pairs={{0,16},{4,12},{8,24},{12,4},{16,0},{20,28},{24,8},{28,20},{1,17},{... | collective-permute-start | bytes 1572872 | tf_op jit(solution)/shard_map/ppermute | solution.py:234
  81.1 7.8 %collective-permute-done.10 = bf16[128,2048]{1,0:T(8,128)(2,1)S(1)} collective-permute-done((bf16[128,2048]{1,0:T(8,128)(2,1)S(1)}, bf16[128,2048]{1,0:T(8,128)(2,1)S(1)}, u32[]{:S(2)}, u32[]{:S(2)}) %collective-permute-start.10) | collective-permute-done | bytes 524320 | tf_op jit(solution)/shard_map/ppermute | solution.py:234
  89.1 1.4 %collective-permute-start.11 = (bf16[64,2048]{1,0:T(8,128)(2,1)S(1)}, bf16[64,2048]{1,0:T(8,128)(2,1)S(1)}, u32[]{:S(2)}, u32[]{:S(2)}) collective-permute-start(bf16[64,2048]{1,0:T(8,128)(2,1)S(1)} %slice.63), channel_id=1, source_target_pairs={{0,8},{4,20},{8,0},{12,28},{16,24},{20,4},{24,16},{28,12},{1,9},{5... | collective-permute-start | bytes 786440 | tf_op jit(solution)/shard_map/ppermute | solution.py:234
  90.5 5.0 %collective-permute-done.11 = bf16[64,2048]{1,0:T(8,128)(2,1)S(1)} collective-permute-done((bf16[64,2048]{1,0:T(8,128)(2,1)S(1)}, bf16[64,2048]{1,0:T(8,128)(2,1)S(1)}, u32[]{:S(2)}, u32[]{:S(2)}) %collective-permute-start.11) | collective-permute-done | bytes 262176 | tf_op jit(solution)/shard_map/ppermute | solution.py:234
  95.6 1.6 %collective-permute-start.12 = (bf16[16,2048]{1,0:T(8,128)(2,1)S(1)}, bf16[16,2048]{1,0:T(8,128)(2,1)S(1)}, u32[]{:S(2)}, u32[]{:S(2)}) collective-permute-start(bf16[16,2048]{1,0:T(8,128)(2,1)S(1)} %get-tuple-element.20), channel_id=1, source_target_pairs={{0,1},{1,2},{2,3},{3,0},{4,5},{5,6},{6,7},{7,4},{8,9},{9,10},{10,1... | collective-permute-start | bytes 196616 | tf_op jit(solution)/shard_map/ppermute | solution.py:231
  97.3 2.3 %collective-permute-start.14 = (bf16[16,2048]{1,0:T(8,128)(2,1)S(1)}, bf16[16,2048]{1,0:T(8,128)(2,1)S(1)}, u32[]{:S(2)}, u32[]{:S(2)}) collective-permute-start(bf16[16,2048]{1,0:T(8,128)(2,1)S(1)} %get-tuple-element.21), channel_id=1, source_target_pairs={{0,3},{1,0},{2,1},{3,2},{4,7},{5,4},{6,5},{7,6},{8,11},{9,8},{10,9... | collective-permute-start | bytes 196616 | tf_op jit(solution)/shard_map/ppermute | solution.py:231
  99.5 2.4 %collective-permute-done.12 = bf16[16,2048]{1,0:T(8,128)(2,1)S(1)} collective-permute-done((bf16[16,2048]{1,0:T(8,128)(2,1)S(1)}, bf16[16,2048]{1,0:T(8,128)(2,1)S(1)}, u32[]{:S(2)}, u32[]{:S(2)}) %collective-permute-start.12) | collective-permute-done | bytes 65568 | tf_op jit(solution)/shard_map/ppermute | solution.py:231
  101.9 0.7 collective-permute-done.14
  102.6 2.0 %collective-permute-done.13 = bf16[16,2048]{1,0:T(8,128)(2,1)S(1)} collective-permute-done((bf16[16,2048]{1,0:T(8,128)(2,1)S(1)}, bf16[16,2048]{1,0:T(8,128)(2,1)S(1)}, u32[]{:S(2)}, u32[]{:S(2)}) %collective-permute-start.13) | collective-permute-done | bytes 65568 | tf_op jit(solution)/shard_map/ppermute | solution.py:231
  104.7 0.7 reshape.41
  (62 shorter events, 5.6 us)
Async XLA Ops:
  1.6 3.4 %copy-start = (f32[16,8,128,128]{3,2,1,0:T(8,128)S(1)}, f32[16,8,128,128]{3,2,1,0:T(8,128)}, u32[]{:S(2)}) copy-start(f32[16,8,128,128]{3,2,1,0:T(8,128)} %states_hbm.1) | copy-start | bytes 25165828
  5.0 2.2 %copy-start.6 = (bf16[1024,2048]{1,0:T(8,128)(2,1)S(1)}, bf16[1024,2048]{1,0:T(8,128)(2,1)}, u32[]{:S(2)}) copy-start(bf16[1024,2048]{1,0:T(8,128)(2,1)} %weight_hbm.1) | copy-start | bytes 12582916
  7.2 0.9 copy-start.7
  8.1 0.9 copy-start.8
  9.0 0.8 copy-start.10
  9.8 0.8 copy-start.11
  10.6 0.7 copy-start.12
  11.3 15.9 %copy-start.18 = (bf16[4,4,2048]{2,1,0:T(4,128)(2,1)S(1)}, bf16[4,4,2048]{2,1,0:T(4,128)(2,1)}, u32[]{:S(2)}) copy-start(bf16[4,4,2048]{2,1,0:T(4,128)(2,1)} %param.27) | copy-start | bytes 196612
  19.6 0.6 copy-start.9
  20.2 31.0 %copy-start.14 = (f32[4,128,10]{1,0,2:T(4,128)S(1)}, f32[4,128,10]{1,0,2:T(4,128)}, u32[]{:S(2)}) copy-start(f32[4,128,10]{1,0,2:T(4,128)} %param.30) | copy-start | bytes 61444
  20.2 40.3 %copy-start.19 = (s32[4,128,10]{1,0,2:T(4,128)S(1)}, s32[4,128,10]{1,0,2:T(4,128)}, u32[]{:S(2)}) copy-start(s32[4,128,10]{1,0,2:T(4,128)} %param.29) | copy-start | bytes 61444
  20.2 7.6 %collective-permute-start = (bf16[16,2048]{1,0:T(8,128)(2,1)S(1)}, bf16[16,2048]{1,0:T(8,128)(2,1)S(1)}, u32[]{:S(2)}, u32[]{:S(2)}) collective-permute-start(bf16[16,2048]{1,0:T(8,128)(2,1)S(1)} %get-tuple-element.13), channel_id=1, source_target_pairs={{0,1},{1,2},{2,3},{3,0},{4,5},{5,6},{6,7},{7,4},{8,9},{9,10},{10,1... | collective-permute-start | bytes 196616 | tf_op jit(solution)/shard_map/ppermute | solution.py:231
  23.2 7.1 %collective-permute-start.1 = (bf16[16,2048]{1,0:T(8,128)(2,1)S(1)}, bf16[16,2048]{1,0:T(8,128)(2,1)S(1)}, u32[]{:S(2)}, u32[]{:S(2)}) collective-permute-start(bf16[16,2048]{1,0:T(8,128)(2,1)S(1)} %get-tuple-element.14), channel_id=1, source_target_pairs={{0,2},{1,3},{2,0},{3,1},{4,6},{5,7},{6,4},{7,5},{8,10},{9,11},{10,... | collective-permute-start | bytes 196616 | tf_op jit(solution)/shard_map/ppermute | solution.py:231
  25.8 4.7 %collective-permute-start.2 = (bf16[16,2048]{1,0:T(8,128)(2,1)S(1)}, bf16[16,2048]{1,0:T(8,128)(2,1)S(1)}, u32[]{:S(2)}, u32[]{:S(2)}) collective-permute-start(bf16[16,2048]{1,0:T(8,128)(2,1)S(1)} %get-tuple-element.15), channel_id=1, source_target_pairs={{0,3},{1,0},{2,1},{3,2},{4,7},{5,4},{6,5},{7,6},{8,11},{9,8},{10,9... | collective-permute-start | bytes 196616 | tf_op jit(solution)/shard_map/ppermute | solution.py:231
  27.8 2.7 %copy-start.15 = (bf16[16,2048]{1,0:T(8,128)(2,1)}, bf16[16,2048]{1,0:T(8,128)(2,1)S(1)}, u32[]{:S(2)}) copy-start(bf16[16,2048]{1,0:T(8,128)(2,1)S(1)} %collective-permute-done.rest_0_) | copy-start | bytes 196612
  30.3 0.6 copy-start.16
  30.5 0.6 copy-start.17
  32.9 30.3 %copy-start.1 = (bf16[1,2048,512]{2,1,0:T(8,128)(2,1)S(1)}, bf16[1,2048,512]{2,1,0:T(8,128)(2,1)}, u32[]{:S(2)}) copy-start(bf16[1,2048,512]{2,1,0:T(8,128)(2,1)} %param.31) | copy-start | bytes 6291460
  32.9 6.5 %collective-permute-start.5 = (bf16[16,2048]{1,0:T(8,128)(2,1)}, bf16[16,2048]{1,0:T(8,128)(2,1)S(1)}, u32[]{:S(2)}, u32[]{:S(2)}) collective-permute-start(bf16[16,2048]{1,0:T(8,128)(2,1)} %get-tuple-element.17), channel_id=1, source_target_pairs={{0,1},{1,2},{2,3},{3,0},{4,5},{5,6},{6,7},{7,4},{8,9},{9,10},{10,1... | collective-permute-start | bytes 196616 | tf_op jit(solution)/shard_map/ppermute | solution.py:231
  34.5 6.9 %collective-permute-start.4 = (bf16[16,2048]{1,0:T(8,128)(2,1)}, bf16[16,2048]{1,0:T(8,128)(2,1)S(1)}, u32[]{:S(2)}, u32[]{:S(2)}) collective-permute-start(bf16[16,2048]{1,0:T(8,128)(2,1)} %get-tuple-element.17), channel_id=1, source_target_pairs={{0,2},{1,3},{2,0},{3,1},{4,6},{5,7},{6,4},{7,5},{8,10},{9,11},{10,... | collective-permute-start | bytes 196616 | tf_op jit(solution)/shard_map/ppermute | solution.py:231
  36.5 5.3 %collective-permute-start.3 = (bf16[16,2048]{1,0:T(8,128)(2,1)}, bf16[16,2048]{1,0:T(8,128)(2,1)S(1)}, u32[]{:S(2)}, u32[]{:S(2)}) collective-permute-start(bf16[16,2048]{1,0:T(8,128)(2,1)} %get-tuple-element.17), channel_id=1, source_target_pairs={{0,3},{1,0},{2,1},{3,2},{4,7},{5,4},{6,5},{7,6},{8,11},{9,8},{10,9... | collective-permute-start | bytes 196616 | tf_op jit(solution)/shard_map/ppermute | solution.py:231
  42.6 6.4 %collective-permute-start.6 = (bf16[64,2048]{1,0:T(8,128)(2,1)S(1)}, bf16[64,2048]{1,0:T(8,128)(2,1)S(1)}, u32[]{:S(2)}, u32[]{:S(2)}) collective-permute-start(bf16[64,2048]{1,0:T(8,128)(2,1)S(1)} %pad_maximum_fusion), channel_id=1, source_target_pairs={{0,8},{4,20},{8,0},{12,28},{16,24},{20,4},{24,16},{28,12},{1,9},{5... | collective-permute-start | bytes 786440 | tf_op jit(solution)/shard_map/ppermute | solution.py:234
  49.8 9.5 %collective-permute-start.7 = (bf16[128,2048]{1,0:T(8,128)(2,1)}, bf16[128,2048]{1,0:T(8,128)(2,1)}, u32[]{:S(2)}, u32[]{:S(2)}) collective-permute-start(bf16[128,2048]{1,0:T(8,128)(2,1)} %get-tuple-element.23), channel_id=1, source_target_pairs={{0,16},{4,12},{8,24},{12,4},{16,0},{20,28},{24,8},{28,20},{1,17},{... | collective-permute-start | bytes 1572872 | tf_op jit(solution)/shard_map/ppermute | solution.py:234
  60.4 2.9 %collective-permute-start.8 = (bf16[256,2048]{1,0:T(8,128)(2,1)S(1)}, bf16[256,2048]{1,0:T(8,128)(2,1)}, u32[]{:S(2)}, u32[]{:S(2)}) collective-permute-start(bf16[256,2048]{1,0:T(8,128)(2,1)S(1)} %constant_dynamic-update-slice_fusion.5.x_ref), channel_id=1, source_target_pairs={{0,4},{4,0},{8,12},{12,8},{16,20},{20,16},{24,28},{28,24},{1,5},{5... | collective-permute-start | bytes 3145736 | tf_op jit(solution)/shard_map/ppermute | solution.py:239
  63.2 1.6 %copy-start.2 = (bf16[1,2048,512]{2,1,0:T(8,128)(2,1)S(1)}, bf16[1,2048,512]{2,1,0:T(8,128)(2,1)}, u32[]{:S(2)}) copy-start(bf16[1,2048,512]{2,1,0:T(8,128)(2,1)} %param.32) | copy-start | bytes 6291460
  64.8 1.6 %copy-start.4 = (bf16[1,512,2048]{2,1,0:T(8,128)(2,1)S(1)}, bf16[1,512,2048]{2,1,0:T(8,128)(2,1)}, u32[]{:S(2)}) copy-start(bf16[1,512,2048]{2,1,0:T(8,128)(2,1)} %param.33) | copy-start | bytes 6291460
  71.3 6.8 %collective-permute-start.9 = (bf16[256,2048]{1,0:T(8,128)(2,1)}, bf16[256,2048]{1,0:T(8,128)(2,1)}, u32[]{:S(2)}, u32[]{:S(2)}) collective-permute-start(bf16[256,2048]{1,0:T(8,128)(2,1)} %experts.3), channel_id=1, source_target_pairs={{0,4},{4,0},{8,12},{12,8},{16,20},{20,16},{24,28},{28,24},{1,5},{5... | collective-permute-start | bytes 3145736 | tf_op jit(solution)/shard_map/ppermute | solution.py:239
  72.2 1.6 %copy-start.3 = (bf16[1,2048,512]{2,1,0:T(8,128)(2,1)S(1)}, bf16[1,2048,512]{2,1,0:T(8,128)(2,1)}, u32[]{:S(2)}) copy-start(bf16[1,2048,512]{2,1,0:T(8,128)(2,1)} %param.32) | copy-start | bytes 6291460
  73.8 1.6 %copy-start.5 = (bf16[1,512,2048]{2,1,0:T(8,128)(2,1)S(1)}, bf16[1,512,2048]{2,1,0:T(8,128)(2,1)}, u32[]{:S(2)}) copy-start(bf16[1,512,2048]{2,1,0:T(8,128)(2,1)} %param.33) | copy-start | bytes 6291460
  79.7 25.0 %copy-start.13 = (f32[16,2048]{1,0:T(8,128)S(1)}, f32[16,2048]{1,0:T(8,128)}, u32[]{:S(2)}) copy-start(f32[16,2048]{1,0:T(8,128)} %get-tuple-element.16) | copy-start | bytes 393220
  79.7 9.2 %collective-permute-start.10 = (bf16[128,2048]{1,0:T(8,128)(2,1)S(1)}, bf16[128,2048]{1,0:T(8,128)(2,1)S(1)}, u32[]{:S(2)}, u32[]{:S(2)}) collective-permute-start(bf16[128,2048]{1,0:T(8,128)(2,1)S(1)} %slice.62), channel_id=1, source_target_pairs={{0,16},{4,12},{8,24},{12,4},{16,0},{20,28},{24,8},{28,20},{1,17},{... | collective-permute-start | bytes 1572872 | tf_op jit(solution)/shard_map/ppermute | solution.py:234
  89.1 6.4 %collective-permute-start.11 = (bf16[64,2048]{1,0:T(8,128)(2,1)S(1)}, bf16[64,2048]{1,0:T(8,128)(2,1)S(1)}, u32[]{:S(2)}, u32[]{:S(2)}) collective-permute-start(bf16[64,2048]{1,0:T(8,128)(2,1)S(1)} %slice.63), channel_id=1, source_target_pairs={{0,8},{4,20},{8,0},{12,28},{16,24},{20,4},{24,16},{28,12},{1,9},{5... | collective-permute-start | bytes 786440 | tf_op jit(solution)/shard_map/ppermute | solution.py:234
  95.6 6.3 %collective-permute-start.12 = (bf16[16,2048]{1,0:T(8,128)(2,1)S(1)}, bf16[16,2048]{1,0:T(8,128)(2,1)S(1)}, u32[]{:S(2)}, u32[]{:S(2)}) collective-permute-start(bf16[16,2048]{1,0:T(8,128)(2,1)S(1)} %get-tuple-element.20), channel_id=1, source_target_pairs={{0,1},{1,2},{2,3},{3,0},{4,5},{5,6},{6,7},{7,4},{8,9},{9,10},{10,1... | collective-permute-start | bytes 196616 | tf_op jit(solution)/shard_map/ppermute | solution.py:231
  97.3 5.4 %collective-permute-start.14 = (bf16[16,2048]{1,0:T(8,128)(2,1)S(1)}, bf16[16,2048]{1,0:T(8,128)(2,1)S(1)}, u32[]{:S(2)}, u32[]{:S(2)}) collective-permute-start(bf16[16,2048]{1,0:T(8,128)(2,1)S(1)} %get-tuple-element.21), channel_id=1, source_target_pairs={{0,3},{1,0},{2,1},{3,2},{4,7},{5,4},{6,5},{7,6},{8,11},{9,8},{10,9... | collective-permute-start | bytes 196616 | tf_op jit(solution)/shard_map/ppermute | solution.py:231
  99.5 5.2 %collective-permute-start.13 = (bf16[16,2048]{1,0:T(8,128)(2,1)S(1)}, bf16[16,2048]{1,0:T(8,128)(2,1)S(1)}, u32[]{:S(2)}, u32[]{:S(2)}) collective-permute-start(bf16[16,2048]{1,0:T(8,128)(2,1)S(1)} %get-tuple-element.22), channel_id=1, source_target_pairs={{0,2},{1,3},{2,0},{3,1},{4,6},{5,7},{6,4},{7,5},{8,10},{9,11},{10,... | collective-permute-start | bytes 196616 | tf_op jit(solution)/shard_map/ppermute | solution.py:231

commit v2 on v1

v2 whole, which is shorter than its diff:
```python
import functools

import jax
import jax.numpy as jnp
from jax import lax
from jax.experimental import pallas as pl
from jax.experimental.pallas import tpu as pltpu
from jax.sharding import PartitionSpec as P

HK = 128
HV = 128
EPS = 1e-06


def attend_kernel(place, spot, *refs, blocks):
    q_hbm, k_hbm, v_hbm, gate_hbm, beta_hbm, decay_hbm, gain_hbm, states_hbm, weight_hbm = refs[:9]
    expert_hbm, refs = refs[9:12], refs[12:]
    own_ref, send_refs, expert_refs = refs[0], refs[1:blocks], refs[blocks : blocks + 3]
    (q_ref, k_ref, v_ref, gate_ref, beta_ref, decay_ref, gain_ref, state, weight) = refs[
        blocks + 3 : blocks + 12
    ]
    rows, reads, gated, small_sems, state_sems, weight_sems = refs[blocks + 12 :]
    steps, requests, _ = q_ref.shape
    heads = v_ref.shape[2] // HV
    pairs = q_ref.shape[2] // HK
    repeat = heads // pairs
    each = requests // blocks
    vectors = 2 * steps

    small = [
        pltpu.make_async_copy(src, dst, small_sems.at[i])
        for i, (src, dst) in enumerate(
            (
                (q_hbm, q_ref),
                (k_hbm, k_ref),
                (v_hbm, v_ref),
                (gate_hbm, gate_ref),
                (beta_hbm, beta_ref),
                (decay_hbm, decay_ref),
                (gain_hbm, gain_ref),
            )
        )
    ]
    large = [
        pltpu.make_async_copy(src, dst, weight_sems.at[i])
        for i, (src, dst) in enumerate(
            [(weight_hbm, weight)]
            + [(src.at[0], dst) for src, dst in zip(expert_hbm, expert_refs)]
        )
    ]
    for copy in small:
        copy.start()
    for r in range(requests):
        pltpu.make_async_copy(states_hbm.at[r], state.at[r], state_sems.at[r]).start()
    for copy in large:
        copy.start()
    for copy in small:
        copy.wait()

    unit_q, unit_k = {}, {}
    for g in range(pairs):
        lanes = slice(g * HK, (g + 1) * HK)
        for t in range(steps):
            q = q_ref[t, :, lanes].astype(jnp.float32)
            k = k_ref[t, :, lanes].astype(jnp.float32)
            q = q * lax.rsqrt(jnp.sum(q * q, axis=-1, keepdims=True) + EPS) * HK ** (-0.5)
            k = k * lax.rsqrt(jnp.sum(k * k, axis=-1, keepdims=True) + EPS)
            for i, value in ((t, q), (steps + t, k)):
                high = value.astype(jnp.bfloat16).astype(jnp.float32)
                rows[g, pl.ds(i, requests, stride=2 * vectors), :] = high
                rows[g, pl.ds(vectors + i, requests, stride=2 * vectors), :] = value - high
            unit_q[g, t], unit_k[g, t] = q, k

    def read_states(r, carry):
        pltpu.make_async_copy(states_hbm.at[r], state.at[r], state_sems.at[r]).wait()
        both = pl.ds(pl.multiple_of(r * 2 * vectors, 2 * vectors), 2 * vectors)
        at = pl.ds(pl.multiple_of(r * vectors, vectors), vectors)
        for g in range(pairs):
            left = rows[g, both, :].astype(jnp.bfloat16)
            for h in range(g * repeat, (g + 1) * repeat):
                read = jnp.dot(
                    left, state[r, h].astype(jnp.bfloat16), preferred_element_type=jnp.float32
                )
                reads[h, at, :] = read[:vectors] + read[vectors:]
        return carry

    lax.fori_loop(0, requests, read_states, 0)

    betas = jax.nn.sigmoid(beta_ref[...].reshape(steps * heads, requests).T)
    decays = decay_ref[...].reshape(steps * heads, requests).T
    for g in range(pairs):
        kk, qk = {}, {}
        for t in range(steps):
            for s in range(t + 1):
                qk[t, s] = jnp.sum(unit_q[g, t] * unit_k[g, s], axis=-1, keepdims=True)
                if s < t:
                    kk[t, s] = jnp.sum(unit_k[g, t] * unit_k[g, s], axis=-1, keepdims=True)
        for h in range(g * repeat, (g + 1) * repeat):
            lanes = slice(h * HV, (h + 1) * HV)
            decay = [decays[:, t * heads + h : t * heads + h + 1] for t in range(steps)]
            span = {}
            for t in range(steps):
                span[t, t] = None
                for s in range(t - 1, -2, -1):
                    last = span[t, s + 1]
                    span[t, s] = decay[s + 1] if last is None else last * decay[s + 1]
            deltas = []
            for t in range(steps):
                start_q = reads[h, pl.ds(t, requests, stride=vectors), :]
                start_k = reads[h, pl.ds(steps + t, requests, stride=vectors), :]
                recalled = span[t, -1] * start_k
                for s in range(t):
                    recalled = recalled + (span[t, s] * kk[t, s]) * deltas[s]
                beta = betas[:, t * heads + h : t * heads + h + 1]
                deltas.append((v_ref[t, :, lanes].astype(jnp.float32) - recalled) * beta)
                read = span[t, -1] * start_q
                for s in range(t + 1):
                    factor = qk[t, s] if s == t else span[t, s] * qk[t, s]
                    read = read + factor * deltas[s]
                scale = lax.rsqrt(jnp.mean(read * read, axis=-1, keepdims=True) + EPS)
                gate = gate_ref[t, :, lanes].astype(jnp.float32)
                value = read * scale * gain_ref[...] * jax.nn.silu(gate)
                gated[pl.ds(t * requests, requests), lanes] = value.astype(jnp.bfloat16)

    total = steps * requests
    new = lax.broadcasted_iota(jnp.int32, (total, total), 0)
    old = lax.broadcasted_iota(jnp.int32, (total, total), 1)
    block = new // (steps * each) + place[0]
    block = jnp.where(block >= blocks, block - blocks, block)
    within = new % (steps * each)
    source = (within // each) * requests + block * each + within % each
    chosen = jnp.where(source == old, 1.0, 0.0).astype(jnp.bfloat16)
    ordered = jnp.dot(chosen, gated[...], preferred_element_type=jnp.float32).astype(jnp.bfloat16)

    for copy in large:
        copy.wait()
    size = steps * each
    columns = weight.shape[1]
    tile = min(512, columns)
    for c in range(0, columns, tile):
        part = jnp.dot(ordered, weight[:, c : c + tile], preferred_element_type=jnp.float32)
        own_ref[:, c : c + tile] = part[:size]
        for k in range(1, blocks):
            send_refs[k - 1][:, c : c + tile] = part[k * size : (k + 1) * size].astype(jnp.bfloat16)


def attend(place, spot, queries, keys_in, values_in, out_gate, beta, decay, gain, states, weight, mats, blocks):
    steps, requests, _ = queries.shape
    heads = values_in.shape[2] // HV
    pairs = queries.shape[2] // HK
    size = steps * requests // blocks
    columns = weight.shape[1]
    whole = pl.BlockSpec(memory_space=pltpu.VMEM)
    far = pl.BlockSpec(memory_space=pltpu.HBM)
    small = (queries, keys_in, values_in, out_gate, beta, decay, gain)
    return pl.pallas_call(
        functools.partial(attend_kernel, blocks=blocks),
        out_shape=[jax.ShapeDtypeStruct((size, columns), jnp.float32)]
        + [jax.ShapeDtypeStruct((size, columns), jnp.bfloat16)] * (blocks - 1)
        + [pltpu.VMEM(mat.shape[1:], mat.dtype) for mat in mats],
        in_specs=[pl.BlockSpec(memory_space=pltpu.SMEM)] * 2 + [far] * 12,
        out_specs=[whole] * (blocks + 3),
        scratch_shapes=[pltpu.VMEM(x.shape, x.dtype) for x in small]
        + [
            pltpu.VMEM(states.shape, jnp.float32),
            pltpu.VMEM(weight.shape, jnp.bfloat16),
            pltpu.VMEM((pairs, requests * 4 * steps, HK), jnp.float32),
            pltpu.VMEM((heads, requests * 2 * steps, HV), jnp.float32),
            pltpu.VMEM((steps * requests, heads * HV), jnp.bfloat16),
            pltpu.SemaphoreType.DMA((len(small),)),
            pltpu.SemaphoreType.DMA((requests,)),
            pltpu.SemaphoreType.DMA((4,)),
        ],
        compiler_params=pltpu.CompilerParams(vmem_limit_bytes=32 << 20),
        name="attend",
    )(place, spot, *[pltpu.with_memory_space_constraint(x, pltpu.HBM) for x in (*small, states, weight, *mats)])


def local(kernel, out_shape, *operands, name):
    whole = pl.BlockSpec(memory_space=pltpu.VMEM)
    scalars = [x.ndim == 1 for x in operands]
    return pl.pallas_call(
        kernel,
        out_shape=out_shape,
        in_specs=[pl.BlockSpec(memory_space=pltpu.SMEM) if one else whole for one in scalars],
        out_specs=jax.tree.map(lambda _: whole, out_shape),
        compiler_params=pltpu.CompilerParams(vmem_limit_bytes=12 << 20),
        name=name,
    )(*operands)


def norm_kernel(own_ref, residual_ref, gain_ref, *rest):
    arrived, (stream_ref, normed_ref) = rest[:-2], rest[-2:]
    steps, each, _ = residual_ref.shape
    for t in range(steps):
        at = slice(t * each, (t + 1) * each)
        stream_ref[at, :] = residual_ref[t].astype(jnp.float32)
    stream = stream_ref[...] + own_ref[...]
    for ref in arrived:
        stream = stream + ref[...].astype(jnp.float32)
    stream_ref[...] = stream
    scale = lax.rsqrt(jnp.mean(stream * stream, axis=-1, keepdims=True) + EPS)
    normed_ref[...] = (stream * scale * gain_ref[...]).astype(jnp.bfloat16)


def join_kernel(*refs):
    at = 0
    for ref in refs[:-1]:
        refs[-1][pl.ds(at, ref.shape[0]), :] = ref[...]
        at += ref.shape[0]


def join(*parts):
    rows = sum(x.shape[0] for x in parts)
    shape = jax.ShapeDtypeStruct((rows, parts[0].shape[1]), parts[0].dtype)
    return local(join_kernel, shape, *parts, name="join")


def add_kernel(first_ref, second_ref, *outs):
    total = first_ref[...].astype(jnp.float32) + second_ref[...].astype(jnp.float32)
    at = 0
    for out in outs:
        out[...] = total[at : at + out.shape[0]].astype(out.dtype)
        at += out.shape[0]


def add(first, second, *outs):
    shapes = [jax.ShapeDtypeStruct((rows, first.shape[1]), dtype) for rows, dtype in outs]
    return local(add_kernel, shapes, first, second, name="add")


def finish_kernel(stream_ref, own_ref, *rest):
    arrived, out_ref = rest[:-1], rest[-1]
    total = stream_ref[...] + own_ref[...]
    for ref in arrived:
        total = total + ref[...].astype(jnp.float32)
    steps, each, _ = out_ref.shape
    for t in range(steps):
        out_ref[t] = total[t * each : (t + 1) * each].astype(jnp.bfloat16)


def experts_kernel(place, spot, ids_ref, route_ref, gate, up, down, *refs, plan):
    count = len(plan)
    ring, width, bits = plan[0][:3]
    top, steps, requests = ids_ref.shape
    each = requests // (ring * width)
    routes = [route_ref[k] for k in range(top)]
    norm = functools.reduce(jnp.add, routes)
    own = spot[0] * ring + place[0]
    picked = jnp.zeros((steps, requests), jnp.float32)
    for k in range(top):
        picked = picked + jnp.where(ids_ref[k] == own, routes[k] / norm, 0.0)

    for (_, _, _, flip, skip), x_ref, out_ref in zip(plan, refs[:count], refs[count:]):
        rows = x_ref.shape[0]
        row = lax.broadcasted_iota(jnp.int32, (rows, requests), 0) + skip
        column = lax.broadcasted_iota(jnp.int32, (rows, requests), 1)
        size = steps * each
        block = row // size
        k, m = block % ring, block // ring
        device = jnp.bitwise_xor(spot[0], flip)
        core = device % 2
        mask = jnp.zeros_like(row)
        for j in range(bits):
            mask = mask + ((m >> j) & 1) * (jnp.int32(2) << ((j + core) % bits))
        far = place[0] + k
        far = jnp.where(far >= ring, far - ring, far)
        owner = jnp.bitwise_xor(device, mask) * ring + far
        moment = (row % size) // each
        request = owner * each + row % each
        share = jnp.zeros((rows, requests), jnp.float32)
        for t in range(steps):
            share = jnp.where(moment == t, jnp.broadcast_to(picked[t : t + 1], (rows, requests)), share)
        share = jnp.sum(jnp.where(request == column, share, 0.0), axis=-1, keepdims=True)

        x = x_ref[...]
        gated = jnp.dot(x, gate[...], preferred_element_type=jnp.float32)
        lifted = jnp.dot(x, up[...], preferred_element_type=jnp.float32)
        hidden = (jax.nn.silu(gated) * lifted).astype(jnp.bfloat16)
        served = jnp.dot(hidden, down[...], preferred_element_type=jnp.float32)
        served = served.astype(jnp.bfloat16).astype(jnp.float32) * share
        out_ref[...] = served.astype(out_ref.dtype)


def shards(
    queries,
    keys_in,
    values_in,
    out_gate,
    beta_logit,
    decay_rate,
    states,
    out_weight,
    head_gain,
    residual,
    post_gain,
    expert_ids,
    route_weight,
    expert_gate,
    expert_up,
    expert_down,
):
    ring, width = lax.axis_size("head"), lax.axis_size("dev")
    place = lax.axis_index("head").astype(jnp.int32).reshape(1)
    spot = lax.axis_index("dev").astype(jnp.int32).reshape(1)
    steps, each, columns = residual.shape
    size = steps * each
    bits = (width // 2).bit_length() - 1

    def along(x, k):
        return lax.ppermute(x, "head", [(i, (i + k) % ring) for i in range(ring)])

    def across(x, j):
        return lax.ppermute(
            x, "dev", [(i, i ^ (2 << ((j + i % 2) % bits))) for i in range(width)]
        )

    def other(x):
        return lax.ppermute(x, "dev", [(i, i ^ 1) for i in range(width)])

    parts = attend(
        place,
        spot,
        queries,
        keys_in,
        values_in,
        out_gate,
        beta_logit.transpose(0, 2, 1),
        decay_rate.transpose(0, 2, 1),
        head_gain.reshape(1, HV),
        states,
        out_weight,
        (expert_gate, expert_up, expert_down),
        ring,
    )
    arrived = [along(parts[k], k) for k in range(1, ring)]
    stream, normed = local(
        norm_kernel,
        [
            jax.ShapeDtypeStruct((size, columns), jnp.float32),
            jax.ShapeDtypeStruct((size, columns), jnp.bfloat16),
        ],
        parts[0],
        residual,
        post_gain.reshape(1, columns),
        *arrived,
        name="norm",
    )

    ids, route = expert_ids.transpose(2, 0, 1), route_weight.transpose(2, 0, 1)

    def experts(*pieces):
        return local(
            functools.partial(
                experts_kernel,
                plan=tuple((ring, width, bits, flip, skip) for _, _, flip, skip in pieces),
            ),
            [jax.ShapeDtypeStruct(x.shape, dtype) for x, dtype, _, _ in pieces],
            place,
            spot,
            ids,
            route,
            *parts[ring:],
            *[x for x, _, _, _ in pieces],
            name="experts",
        )

    rows = join(normed, *[along(normed, ring - k) for k in range(1, ring)])
    for j in range(bits - 1):
        rows = join(rows, across(rows, j))
    half = rows.shape[0]
    late = across(rows, bits - 1)
    served, peer_served = experts(
        (rows, jnp.float32, 0, 0), (other(rows), jnp.bfloat16, 1, 0)
    )
    peer_served, late = lax.optimization_barrier((peer_served, late))
    total = add(served, other(peer_served), (half, jnp.float32))[0]
    late_served = experts((late, jnp.float32, 0, half))[0]
    peer_late = experts((other(late), jnp.bfloat16, 1, half))[0]
    send = add(late_served, other(peer_late), (half, jnp.bfloat16))[0]
    for j in reversed(range(bits)):
        came = across(send, j)
        if j > 0:
            half //= 2
            total, send = add(total, came, (half, jnp.float32), (half, jnp.bfloat16))
    total, *blocks = add(
        total, came, (size, jnp.float32), *[(size, jnp.bfloat16)] * (ring - 1)
    )
    return local(
        finish_kernel,
        jax.ShapeDtypeStruct((steps, each, columns), jnp.bfloat16),
        stream,
        total,
        *[along(x, k + 1) for k, x in enumerate(blocks)],
        name="finish",
    )


def solution(mesh):
    return jax.shard_map(
        shards,
        mesh=mesh,
        in_specs=(
            P(None, ("groups", "dev"), "head"),
            P(None, ("groups", "dev"), "head"),
            P(None, ("groups", "dev"), "head"),
            P(None, ("groups", "dev"), "head"),
            P(None, ("groups", "dev"), "head"),
            P(None, ("groups", "dev"), "head"),
            P(("groups", "dev"), "head", None, None),
            P("head", None),
            P(),
            P(None, ("groups", "dev", "head"), None),
            P(),
            P(None, "groups", None),
            P(None, "groups", None),
            P(("dev", "head"), None, None),
            P(("dev", "head"), None, None),
            P(("dev", "head"), None, None),
        ),
        out_specs=P(None, ("groups", "dev", "head"), None),
        check_vma=False,
    )
```

time: 106 us -> 77 us (0.73)
  local copies, waits for them, and re-layouts: 27.3 us -> 0.01 us
  other arithmetic: 2.82 us -> 0 us
    unnamed x46 -> x8, local copies, waits for them, and re-layouts: 22.3 us -> 0.01 us
    pallas_call x1, Pallas kernels: 8.24 us -> 12.2 us  [attend(): pl.pallas_call(functools.partial(attend_kernel, blocks=blocks), out_shape...]
    pallas_call x3 -> x11, Pallas kernels: 9.3 us -> 5.53 us  [local(): pl.pallas_call(kernel, out_shape=out_shape, in_specs=[pl.BlockSpec(memory...]
    concatenate x2 -> x0, local copies, waits for them, and re-layouts: 1.82 us -> none  [shards(): rows = jnp.concatenate([rows, across(rows, j)])]
    reshape x6 -> x0, local copies, waits for them, and re-layouts: 1.69 us -> none  [the longest x1 0.66 us: shards(): return routed.astype(jnp.bfloat16).reshape(steps, each, columns)]
    add x2 -> x0, other arithmetic: 1.62 us -> none  [the longest x1 1.49 us: shards(): total = served + other(peer_served).astype(jnp.float32)]
    ppermute x2 -> x4, waiting for transfers between devices: 1.34 us -> 2.58 us  [other(): return lax.ppermute(x, 'dev', [(i, i ^ 1) for i in range(width)])]
    gather x2 -> x0, local copies, waits for them, and re-layouts: 1.12 us -> none  [the longest x1 0.56 us: shards(): jnp.take(picked, shares_of(spot ^ 1, 1 - core), axis=0).reshape(-1, 1)]
  transfers between devices with their start and end apart: 15 -> 17, of which waited for: 13 -> 15; matrix products, arithmetic and copies ran while one was open for 6% -> 0% of each run, Pallas kernels for 3% -> 4%
where the time goes in v2:
time: 77 us; the launch traced here: 76.9 us
  waiting for transfers between devices  37.5 us (49%)
  starting transfers between devices  21.5 us (28%)
  Pallas kernels  17.8 us (23%)
    ppermute x4, waiting for transfers between devices, across(): lax.ppermute(x, 'dev', [(i, i ^ 2 << (j + i % 2) % bits) for i in range(w...  23.1 us
    ppermute x9, starting transfers between devices, along(): return lax.ppermute(x, 'head', [(i, (i + k) % ring) for i in range(ring)])  15.1 us
    pallas_call x1, Pallas kernels, attend(): pl.pallas_call(functools.partial(attend_kernel, blocks=blocks), out_shape...  12.2 us
    ppermute x9, waiting for transfers between devices, along(): return lax.ppermute(x, 'head', [(i, (i + k) % ring) for i in range(ring)])  11.8 us
    ppermute x4, starting transfers between devices, across(): lax.ppermute(x, 'dev', [(i, i ^ 2 << (j + i % 2) % bits) for i in range(w...  5.63 us
    pallas_call x11, Pallas kernels, local(): pl.pallas_call(kernel, out_shape=out_shape, in_specs=[pl.BlockSpec(memory...  5.53 us
    ppermute x4, waiting for transfers between devices, other(): return lax.ppermute(x, 'dev', [(i, i ^ 1) for i in range(width)])  2.58 us
  transfers between devices with their start and end apart: 17, of which 15 were waited for; matrix products, arithmetic and copies ran while one was open for 0% of the time, Pallas kernels for 4%

profile of v2, /device:TPU:0, one launch (start us, length us, event | category | flops | bytes accessed | tf_op | source)
XLA Modules:
  0.0 76.9 jit_solution(1264639875175849187)
XLA Ops:
  0.0 0.0 copy-start.2
  0.0 12.2 %attend.1 = (f32[16,2048]{1,0:T(8,128)S(1)}, bf16[16,2048]{1,0:T(8,128)(2,1)S(1)}, bf16[16,2048]{1,0:T(8,128)(2,1)S(1)}, bf16[16,2048]{1,0:T(8,128)(2,1)S(1)}, b...) custom-call(s32[1]{0:T(128)} %bitcast.place, s32[1]{0:T(128)} %bitcast.1.spot, ...), custom_call_target="tpu_custom_call" | custom-call | tf_op jit(solution)/shard_map/attend/pallas_call | solution.py:156
  12.3 3.1 %collective-permute-start = (bf16[16,2048]{1,0:T(8,128)(2,1)S(1)}, bf16[16,2048]{1,0:T(8,128)(2,1)S(1)}, u32[]{:S(2)}, u32[]{:S(2)}) collective-permute-start(bf16[16,2048]{1,0:T(8,128)(2,1)S(1)} %get-tuple-element.25), channel_id=1, source_target_pairs={{0,1},{1,2},{2,3},{3,0},{4,5},{5,6},{6,7},{7,4},{8,9},{9,10},{10,1... | collective-permute-start | bytes 196616 | tf_op jit(solution)/shard_map/ppermute | solution.py:311
  15.4 2.6 %collective-permute-start.1 = (bf16[16,2048]{1,0:T(8,128)(2,1)S(1)}, bf16[16,2048]{1,0:T(8,128)(2,1)S(1)}, u32[]{:S(2)}, u32[]{:S(2)}) collective-permute-start(bf16[16,2048]{1,0:T(8,128)(2,1)S(1)} %get-tuple-element.26), channel_id=1, source_target_pairs={{0,2},{1,3},{2,0},{3,1},{4,6},{5,7},{6,4},{7,5},{8,10},{9,11},{10,... | collective-permute-start | bytes 196616 | tf_op jit(solution)/shard_map/ppermute | solution.py:311
  18.0 1.3 %collective-permute-start.2 = (bf16[16,2048]{1,0:T(8,128)(2,1)S(1)}, bf16[16,2048]{1,0:T(8,128)(2,1)S(1)}, u32[]{:S(2)}, u32[]{:S(2)}) collective-permute-start(bf16[16,2048]{1,0:T(8,128)(2,1)S(1)} %get-tuple-element.27), channel_id=1, source_target_pairs={{0,3},{1,0},{2,1},{3,2},{4,7},{5,4},{6,5},{7,6},{8,11},{9,8},{10,9... | collective-permute-start | bytes 196616 | tf_op jit(solution)/shard_map/ppermute | solution.py:311
  19.3 0.6 collective-permute-done.rest_0_
  19.9 2.5 %collective-permute-done.1.rest_1_ = bf16[16,2048]{1,0:T(8,128)(2,1)S(1)} collective-permute-done((bf16[16,2048]{1,0:T(8,128)(2,1)S(1)}, bf16[16,2048]{1,0:T(8,128)(2,1)S(1)}, u32[]{:S(2)}, u32[]{:S(2)}) %collective-permute-start.1) | collective-permute-done | bytes 65568 | tf_op jit(solution)/shard_map/ppermute | solution.py:311
  22.5 0.2 collective-permute-done.2.rest_2_
  22.7 0.0 copy-done.2
  22.7 0.0 copy-done.3
  22.7 0.2 norm.1
  22.8 1.6 %collective-permute-start.5 = (bf16[16,2048]{1,0:T(8,128)(2,1)S(1)}, bf16[16,2048]{1,0:T(8,128)(2,1)S(1)}, u32[]{:S(2)}, u32[]{:S(2)}) collective-permute-start(bf16[16,2048]{1,0:T(8,128)(2,1)S(1)} %get-tuple-element.32.refs_0_), channel_id=1, source_target_pairs={{0,1},{1,2},{2,3},{3,0},{4,5},{5,6},{6,7},{7,4},{8,9},{9,10},{10,1... | collective-permute-start | bytes 196616 | tf_op jit(solution)/shard_map/ppermute | solution.py:311
  24.5 2.0 %collective-permute-start.4 = (bf16[16,2048]{1,0:T(8,128)(2,1)S(1)}, bf16[16,2048]{1,0:T(8,128)(2,1)S(1)}, u32[]{:S(2)}, u32[]{:S(2)}) collective-permute-start(bf16[16,2048]{1,0:T(8,128)(2,1)S(1)} %get-tuple-element.32.refs_0_), channel_id=1, source_target_pairs={{0,2},{1,3},{2,0},{3,1},{4,6},{5,7},{6,4},{7,5},{8,10},{9,11},{10,... | collective-permute-start | bytes 196616 | tf_op jit(solution)/shard_map/ppermute | solution.py:311
  26.5 0.4 collective-permute-start.3
  26.9 2.3 %collective-permute-done.5.refs_3_ = bf16[16,2048]{1,0:T(8,128)(2,1)S(1)} collective-permute-done((bf16[16,2048]{1,0:T(8,128)(2,1)S(1)}, bf16[16,2048]{1,0:T(8,128)(2,1)S(1)}, u32[]{:S(2)}, u32[]{:S(2)}) %collective-permute-start.5) | collective-permute-done | bytes 65568 | tf_op jit(solution)/shard_map/ppermute | solution.py:311
  29.2 2.0 %collective-permute-done.4.refs_2_ = bf16[16,2048]{1,0:T(8,128)(2,1)S(1)} collective-permute-done((bf16[16,2048]{1,0:T(8,128)(2,1)S(1)}, bf16[16,2048]{1,0:T(8,128)(2,1)S(1)}, u32[]{:S(2)}, u32[]{:S(2)}) %collective-permute-start.4) | collective-permute-done | bytes 65568 | tf_op jit(solution)/shard_map/ppermute | solution.py:311
  31.2 0.4 collective-permute-done.3.refs_1_
  31.6 1.4 %collective-permute-start.6 = (bf16[64,2048]{1,0:T(8,128)(2,1)S(1)}, bf16[64,2048]{1,0:T(8,128)(2,1)S(1)}, u32[]{:S(2)}, u32[]{:S(2)}) collective-permute-start(bf16[64,2048]{1,0:T(8,128)(2,1)S(1)} %join.2.refs_0_), channel_id=1, source_target_pairs={{0,8},{4,20},{8,0},{12,28},{16,24},{20,4},{24,16},{28,12},{1,9},{5... | collective-permute-start | bytes 786440 | tf_op jit(solution)/shard_map/ppermute | solution.py:314
  33.0 5.0 %collective-permute-done.6.refs_1_ = bf16[64,2048]{1,0:T(8,128)(2,1)S(1)} collective-permute-done((bf16[64,2048]{1,0:T(8,128)(2,1)S(1)}, bf16[64,2048]{1,0:T(8,128)(2,1)S(1)}, u32[]{:S(2)}, u32[]{:S(2)}) %collective-permute-start.6) | collective-permute-done | bytes 262176 | tf_op jit(solution)/shard_map/ppermute | solution.py:314
  38.0 0.1 collective-permute-start.7
  38.1 1.4 %collective-permute-start.8 = (bf16[128,2048]{1,0:T(8,128)(2,1)S(1)}, bf16[128,2048]{1,0:T(8,128)(2,1)S(1)}, u32[]{:S(2)}, u32[]{:S(2)}) collective-permute-start(bf16[128,2048]{1,0:T(8,128)(2,1)S(1)} %join.3.refs_0_), channel_id=1, source_target_pairs={{0,16},{4,12},{8,24},{12,4},{16,0},{20,28},{24,8},{28,20},{1,17},{... | collective-permute-start | bytes 1572872 | tf_op jit(solution)/shard_map/ppermute | solution.py:314
  39.5 0.5 collective-permute-done.7.refs_1_
  40.0 0.0 copy-done
  40.0 0.0 copy-done.1
  40.0 2.1 %experts.3 = (f32[128,2048]{1,0:T(8,128)S(1)}, bf16[128,2048]{1,0:T(8,128)(2,1)S(1)}) custom-call(s32[1]{0:T(128)} %bitcast.place, s32[1]{0:T(128)} %bitcast.1.spot, s32[10,4,128]{2,1,0:T(4,128)S(1)} %bitcast.8, f32[10,4,128]{2,1,0:T(4,128)S(1)} %bitcast.11, bf16[2048,512]{1,0:T(8,128)(2,1)S(1)} %get-tuple-element.29.gate, ...), custom_call_target="tpu_custom_call" | custom-call | tf_op jit(solution)/shard_map/experts/pallas_call | solution.py:182
  42.1 5.3 %collective-permute-done.8.refs_0_ = bf16[128,2048]{1,0:T(8,128)(2,1)S(1)} collective-permute-done((bf16[128,2048]{1,0:T(8,128)(2,1)S(1)}, bf16[128,2048]{1,0:T(8,128)(2,1)S(1)}, u32[]{:S(2)}, u32[]{:S(2)}) %collective-permute-start.8) | collective-permute-done | bytes 524320 | tf_op jit(solution)/shard_map/ppermute | solution.py:314
  47.4 0.0 collective-permute-start.10
  47.4 1.9 %collective-permute-done.10.refs_0_ = bf16[128,2048]{1,0:T(8,128)(2,1)S(1)} collective-permute-done((bf16[128,2048]{1,0:T(8,128)(2,1)S(1)}, bf16[128,2048]{1,0:T(8,128)(2,1)S(1)}, u32[]{:S(2)}, u32[]{:S(2)}) %collective-permute-start.10) | collective-permute-done | bytes 524320 | tf_op jit(solution)/shard_map/ppermute | solution.py:319
  49.3 1.1 %experts.5 = bf16[128,2048]{1,0:T(8,128)(2,1)S(1)} custom-call(s32[1]{0:T(128)} %bitcast.place, s32[1]{0:T(128)} %bitcast.1.spot, s32[10,4,128]{2,1,0:T(4,128)S(1)} %bitcast.9, f32[10,4,128]{2,1,0:T(4,128)S(1)} %bitcast.12, bf16[2048,512]{1,0:T(8,128)(2,1)S(1)} %get-tuple-element.29.gate, bf16[2048,512]{1,0:T(8,128)(2,1)S(1)} %get-tuple-element.30.up, ...), custom_call_target="tpu_custom_call" | custom-call | tf_op jit(solution)/shard_map/experts/pallas_call | solution.py:182
  50.4 0.2 collective-permute-start.11
  50.6 1.1 %experts.4.first_ref = f32[128,2048]{1,0:T(8,128)S(1)} custom-call(s32[1]{0:T(128)} %bitcast.place, s32[1]{0:T(128)} %bitcast.1.spot, s32[10,4,128]{2,1,0:T(4,128)S(1)} %bitcast.10, f32[10,4,128]{2,1,0:T(4,128)S(1)} %bitcast.13, bf16[2048,512]{1,0:T(8,128)(2,1)S(1)} %get-tuple-element.29.gate, bf16[2048,512]{1,0:T(8,128)(2,1)S(1)} %get-tuple-element.30.up, ...), custom_call_target="tpu_custom_call" | custom-call | tf_op jit(solution)/shard_map/experts/pallas_call | solution.py:182
  51.8 0.4 collective-permute-start.9
  52.2 0.2 collective-permute-done.11.second_ref
  52.4 0.1 add.5
  52.5 1.4 %collective-permute-start.12 = (bf16[128,2048]{1,0:T(8,128)(2,1)S(1)}, bf16[128,2048]{1,0:T(8,128)(2,1)S(1)}, u32[]{:S(2)}, u32[]{:S(2)}) collective-permute-start(bf16[128,2048]{1,0:T(8,128)(2,1)S(1)} %add.5), channel_id=1, source_target_pairs={{0,16},{4,12},{8,24},{12,4},{16,0},{20,28},{24,8},{28,20},{1,17},{... | collective-permute-start | bytes 1572872 | tf_op jit(solution)/shard_map/ppermute | solution.py:314
  53.9 0.0 collective-permute-done.9.second_ref
  53.9 0.1 add.4.first_ref
  54.0 7.7 %collective-permute-done.12.second_ref = bf16[128,2048]{1,0:T(8,128)(2,1)S(1)} collective-permute-done((bf16[128,2048]{1,0:T(8,128)(2,1)S(1)}, bf16[128,2048]{1,0:T(8,128)(2,1)S(1)}, u32[]{:S(2)}, u32[]{:S(2)}) %collective-permute-start.12) | collective-permute-done | bytes 524320 | tf_op jit(solution)/shard_map/ppermute | solution.py:314
  61.7 0.1 add.6
  61.8 1.4 %collective-permute-start.13 = (bf16[64,2048]{1,0:T(8,128)(2,1)S(1)}, bf16[64,2048]{1,0:T(8,128)(2,1)S(1)}, u32[]{:S(2)}, u32[]{:S(2)}) collective-permute-start(bf16[64,2048]{1,0:T(8,128)(2,1)S(1)} %get-tuple-element.38), channel_id=1, source_target_pairs={{0,8},{4,20},{8,0},{12,28},{16,24},{20,4},{24,16},{28,12},{1,9},{5... | collective-permute-start | bytes 786440 | tf_op jit(solution)/shard_map/ppermute | solution.py:314
  63.2 5.0 %collective-permute-done.13.second_ref = bf16[64,2048]{1,0:T(8,128)(2,1)S(1)} collective-permute-done((bf16[64,2048]{1,0:T(8,128)(2,1)S(1)}, bf16[64,2048]{1,0:T(8,128)(2,1)S(1)}, u32[]{:S(2)}, u32[]{:S(2)}) %collective-permute-start.13) | collective-permute-done | bytes 262176 | tf_op jit(solution)/shard_map/ppermute | solution.py:314
  68.3 1.6 %collective-permute-start.14 = (bf16[16,2048]{1,0:T(8,128)(2,1)S(1)}, bf16[16,2048]{1,0:T(8,128)(2,1)S(1)}, u32[]{:S(2)}, u32[]{:S(2)}) collective-permute-start(bf16[16,2048]{1,0:T(8,128)(2,1)S(1)} %get-tuple-element.40), channel_id=1, source_target_pairs={{0,1},{1,2},{2,3},{3,0},{4,5},{5,6},{6,7},{7,4},{8,9},{9,10},{10,1... | collective-permute-start | bytes 196616 | tf_op jit(solution)/shard_map/ppermute | solution.py:311
  69.9 1.3 %collective-permute-start.15 = (bf16[16,2048]{1,0:T(8,128)(2,1)S(1)}, bf16[16,2048]{1,0:T(8,128)(2,1)S(1)}, u32[]{:S(2)}, u32[]{:S(2)}) collective-permute-start(bf16[16,2048]{1,0:T(8,128)(2,1)S(1)} %get-tuple-element.41), channel_id=1, source_target_pairs={{0,2},{1,3},{2,0},{3,1},{4,6},{5,7},{6,4},{7,5},{8,10},{9,11},{10,... | collective-permute-start | bytes 196616 | tf_op jit(solution)/shard_map/ppermute | solution.py:311
  71.2 1.1 %collective-permute-start.16 = (bf16[16,2048]{1,0:T(8,128)(2,1)S(1)}, bf16[16,2048]{1,0:T(8,128)(2,1)S(1)}, u32[]{:S(2)}, u32[]{:S(2)}) collective-permute-start(bf16[16,2048]{1,0:T(8,128)(2,1)S(1)} %get-tuple-element.42), channel_id=1, source_target_pairs={{0,3},{1,0},{2,1},{3,2},{4,7},{5,4},{6,5},{7,6},{8,11},{9,8},{10,9... | collective-permute-start | bytes 196616 | tf_op jit(solution)/shard_map/ppermute | solution.py:311
  72.3 2.2 %collective-permute-done.14.rest_0_ = bf16[16,2048]{1,0:T(8,128)(2,1)S(1)} collective-permute-done((bf16[16,2048]{1,0:T(8,128)(2,1)S(1)}, bf16[16,2048]{1,0:T(8,128)(2,1)S(1)}, u32[]{:S(2)}, u32[]{:S(2)}) %collective-permute-start.14) | collective-permute-done | bytes 65568 | tf_op jit(solution)/shard_map/ppermute | solution.py:311
  74.5 1.7 %collective-permute-done.15.rest_1_ = bf16[16,2048]{1,0:T(8,128)(2,1)S(1)} collective-permute-done((bf16[16,2048]{1,0:T(8,128)(2,1)S(1)}, bf16[16,2048]{1,0:T(8,128)(2,1)S(1)}, u32[]{:S(2)}, u32[]{:S(2)}) %collective-permute-start.15) | collective-permute-done | bytes 65568 | tf_op jit(solution)/shard_map/ppermute | solution.py:311
  76.2 0.0 collective-permute-done.16.rest_2_
  76.2 0.7 finish.1
  (6 shorter events, 0.1 us)
Async XLA Ops:
  0.0 22.7 %copy-start.2 = (bf16[4,4,2048]{2,1,0:T(4,128)(2,1)S(1)}, bf16[4,4,2048]{2,1,0:T(4,128)(2,1)}, u32[]{:S(2)}) copy-start(bf16[4,4,2048]{2,1,0:T(4,128)(2,1)} %residual_ref.1) | copy-start | bytes 196612
  0.0 22.7 %copy-start.3 = (f32[2048]{0:T(1024)S(1)}, f32[2048]{0:T(1024)}, u32[]{:S(2)}) copy-start(f32[2048]{0:T(1024)} %param.26) | copy-start | bytes 24580
  0.0 40.0 %copy-start = (s32[4,128,10]{1,0,2:T(4,128)S(1)}, s32[4,128,10]{1,0,2:T(4,128)}, u32[]{:S(2)}) copy-start(s32[4,128,10]{1,0,2:T(4,128)} %param.27) | copy-start | bytes 61444
  0.0 40.0 %copy-start.1 = (f32[4,128,10]{1,0,2:T(4,128)S(1)}, f32[4,128,10]{1,0,2:T(4,128)}, u32[]{:S(2)}) copy-start(f32[4,128,10]{1,0,2:T(4,128)} %param.28) | copy-start | bytes 61444
  12.3 7.7 %collective-permute-start = (bf16[16,2048]{1,0:T(8,128)(2,1)S(1)}, bf16[16,2048]{1,0:T(8,128)(2,1)S(1)}, u32[]{:S(2)}, u32[]{:S(2)}) collective-permute-start(bf16[16,2048]{1,0:T(8,128)(2,1)S(1)} %get-tuple-element.25), channel_id=1, source_target_pairs={{0,1},{1,2},{2,3},{3,0},{4,5},{5,6},{6,7},{7,4},{8,9},{9,10},{10,1... | collective-permute-start | bytes 196616 | tf_op jit(solution)/shard_map/ppermute | solution.py:311
  15.4 7.1 %collective-permute-start.1 = (bf16[16,2048]{1,0:T(8,128)(2,1)S(1)}, bf16[16,2048]{1,0:T(8,128)(2,1)S(1)}, u32[]{:S(2)}, u32[]{:S(2)}) collective-permute-start(bf16[16,2048]{1,0:T(8,128)(2,1)S(1)} %get-tuple-element.26), channel_id=1, source_target_pairs={{0,2},{1,3},{2,0},{3,1},{4,6},{5,7},{6,4},{7,5},{8,10},{9,11},{10,... | collective-permute-start | bytes 196616 | tf_op jit(solution)/shard_map/ppermute | solution.py:311
  18.0 4.7 %collective-permute-start.2 = (bf16[16,2048]{1,0:T(8,128)(2,1)S(1)}, bf16[16,2048]{1,0:T(8,128)(2,1)S(1)}, u32[]{:S(2)}, u32[]{:S(2)}) collective-permute-start(bf16[16,2048]{1,0:T(8,128)(2,1)S(1)} %get-tuple-element.27), channel_id=1, source_target_pairs={{0,3},{1,0},{2,1},{3,2},{4,7},{5,4},{6,5},{7,6},{8,11},{9,8},{10,9... | collective-permute-start | bytes 196616 | tf_op jit(solution)/shard_map/ppermute | solution.py:311
  22.8 6.3 %collective-permute-start.5 = (bf16[16,2048]{1,0:T(8,128)(2,1)S(1)}, bf16[16,2048]{1,0:T(8,128)(2,1)S(1)}, u32[]{:S(2)}, u32[]{:S(2)}) collective-permute-start(bf16[16,2048]{1,0:T(8,128)(2,1)S(1)} %get-tuple-element.32.refs_0_), channel_id=1, source_target_pairs={{0,1},{1,2},{2,3},{3,0},{4,5},{5,6},{6,7},{7,4},{8,9},{9,10},{10,1... | collective-permute-start | bytes 196616 | tf_op jit(solution)/shard_map/ppermute | solution.py:311
  24.5 6.7 %collective-permute-start.4 = (bf16[16,2048]{1,0:T(8,128)(2,1)S(1)}, bf16[16,2048]{1,0:T(8,128)(2,1)S(1)}, u32[]{:S(2)}, u32[]{:S(2)}) collective-permute-start(bf16[16,2048]{1,0:T(8,128)(2,1)S(1)} %get-tuple-element.32.refs_0_), channel_id=1, source_target_pairs={{0,2},{1,3},{2,0},{3,1},{4,6},{5,7},{6,4},{7,5},{8,10},{9,11},{10,... | collective-permute-start | bytes 196616 | tf_op jit(solution)/shard_map/ppermute | solution.py:311
  26.5 5.0 %collective-permute-start.3 = (bf16[16,2048]{1,0:T(8,128)(2,1)S(1)}, bf16[16,2048]{1,0:T(8,128)(2,1)S(1)}, u32[]{:S(2)}, u32[]{:S(2)}) collective-permute-start(bf16[16,2048]{1,0:T(8,128)(2,1)S(1)} %get-tuple-element.32.refs_0_), channel_id=1, source_target_pairs={{0,3},{1,0},{2,1},{3,2},{4,7},{5,4},{6,5},{7,6},{8,11},{9,8},{10,9... | collective-permute-start | bytes 196616 | tf_op jit(solution)/shard_map/ppermute | solution.py:311
  31.6 6.4 %collective-permute-start.6 = (bf16[64,2048]{1,0:T(8,128)(2,1)S(1)}, bf16[64,2048]{1,0:T(8,128)(2,1)S(1)}, u32[]{:S(2)}, u32[]{:S(2)}) collective-permute-start(bf16[64,2048]{1,0:T(8,128)(2,1)S(1)} %join.2.refs_0_), channel_id=1, source_target_pairs={{0,8},{4,20},{8,0},{12,28},{16,24},{20,4},{24,16},{28,12},{1,9},{5... | collective-permute-start | bytes 786440 | tf_op jit(solution)/shard_map/ppermute | solution.py:314
  38.0 2.0 %collective-permute-start.7 = (bf16[128,2048]{1,0:T(8,128)(2,1)S(1)}, bf16[128,2048]{1,0:T(8,128)(2,1)S(1)}, u32[]{:S(2)}, u32[]{:S(2)}) collective-permute-start(bf16[128,2048]{1,0:T(8,128)(2,1)S(1)} %join.3.refs_0_), channel_id=1, source_target_pairs={{0,4},{4,0},{8,12},{12,8},{16,20},{20,16},{24,28},{28,24},{1,5},{5... | collective-permute-start | bytes 1572872 | tf_op jit(solution)/shard_map/ppermute | solution.py:319
  38.1 9.2 %collective-permute-start.8 = (bf16[128,2048]{1,0:T(8,128)(2,1)S(1)}, bf16[128,2048]{1,0:T(8,128)(2,1)S(1)}, u32[]{:S(2)}, u32[]{:S(2)}) collective-permute-start(bf16[128,2048]{1,0:T(8,128)(2,1)S(1)} %join.3.refs_0_), channel_id=1, source_target_pairs={{0,16},{4,12},{8,24},{12,4},{16,0},{20,28},{24,8},{28,20},{1,17},{... | collective-permute-start | bytes 1572872 | tf_op jit(solution)/shard_map/ppermute | solution.py:314
  47.4 1.9 %collective-permute-start.10 = (bf16[128,2048]{1,0:T(8,128)(2,1)S(1)}, bf16[128,2048]{1,0:T(8,128)(2,1)S(1)}, u32[]{:S(2)}, u32[]{:S(2)}) collective-permute-start(bf16[128,2048]{1,0:T(8,128)(2,1)S(1)} %collective-permute-done.8.refs_0_), channel_id=1, source_target_pairs={{0,4},{4,0},{8,12},{12,8},{16,20},{20,16},{24,28},{28,24},{1,5},{5... | collective-permute-start | bytes 1572872 | tf_op jit(solution)/shard_map/ppermute | solution.py:319
  50.4 2.0 %collective-permute-start.11 = (bf16[128,2048]{1,0:T(8,128)(2,1)S(1)}, bf16[128,2048]{1,0:T(8,128)(2,1)S(1)}, u32[]{:S(2)}, u32[]{:S(2)}) collective-permute-start(bf16[128,2048]{1,0:T(8,128)(2,1)S(1)} %experts.5), channel_id=1, source_target_pairs={{0,4},{4,0},{8,12},{12,8},{16,20},{20,16},{24,28},{28,24},{1,5},{5... | collective-permute-start | bytes 1572872 | tf_op jit(solution)/shard_map/ppermute | solution.py:319
  51.8 2.2 %collective-permute-start.9 = (bf16[128,2048]{1,0:T(8,128)(2,1)S(1)}, bf16[128,2048]{1,0:T(8,128)(2,1)S(1)}, u32[]{:S(2)}, u32[]{:S(2)}) collective-permute-start(bf16[128,2048]{1,0:T(8,128)(2,1)S(1)} %get-tuple-element.35), channel_id=1, source_target_pairs={{0,4},{4,0},{8,12},{12,8},{16,20},{20,16},{24,28},{28,24},{1,5},{5... | collective-permute-start | bytes 1572872 | tf_op jit(solution)/shard_map/ppermute | solution.py:319
  52.5 9.2 %collective-permute-start.12 = (bf16[128,2048]{1,0:T(8,128)(2,1)S(1)}, bf16[128,2048]{1,0:T(8,128)(2,1)S(1)}, u32[]{:S(2)}, u32[]{:S(2)}) collective-permute-start(bf16[128,2048]{1,0:T(8,128)(2,1)S(1)} %add.5), channel_id=1, source_target_pairs={{0,16},{4,12},{8,24},{12,4},{16,0},{20,28},{24,8},{28,20},{1,17},{... | collective-permute-start | bytes 1572872 | tf_op jit(solution)/shard_map/ppermute | solution.py:314
  61.8 6.4 %collective-permute-start.13 = (bf16[64,2048]{1,0:T(8,128)(2,1)S(1)}, bf16[64,2048]{1,0:T(8,128)(2,1)S(1)}, u32[]{:S(2)}, u32[]{:S(2)}) collective-permute-start(bf16[64,2048]{1,0:T(8,128)(2,1)S(1)} %get-tuple-element.38), channel_id=1, source_target_pairs={{0,8},{4,20},{8,0},{12,28},{16,24},{20,4},{24,16},{28,12},{1,9},{5... | collective-permute-start | bytes 786440 | tf_op jit(solution)/shard_map/ppermute | solution.py:314
  68.3 6.2 %collective-permute-start.14 = (bf16[16,2048]{1,0:T(8,128)(2,1)S(1)}, bf16[16,2048]{1,0:T(8,128)(2,1)S(1)}, u32[]{:S(2)}, u32[]{:S(2)}) collective-permute-start(bf16[16,2048]{1,0:T(8,128)(2,1)S(1)} %get-tuple-element.40), channel_id=1, source_target_pairs={{0,1},{1,2},{2,3},{3,0},{4,5},{5,6},{6,7},{7,4},{8,9},{9,10},{10,1... | collective-permute-start | bytes 196616 | tf_op jit(solution)/shard_map/ppermute | solution.py:311
  69.9 6.3 %collective-permute-start.15 = (bf16[16,2048]{1,0:T(8,128)(2,1)S(1)}, bf16[16,2048]{1,0:T(8,128)(2,1)S(1)}, u32[]{:S(2)}, u32[]{:S(2)}) collective-permute-start(bf16[16,2048]{1,0:T(8,128)(2,1)S(1)} %get-tuple-element.41), channel_id=1, source_target_pairs={{0,2},{1,3},{2,0},{3,1},{4,6},{5,7},{6,4},{7,5},{8,10},{9,11},{10,... | collective-permute-start | bytes 196616 | tf_op jit(solution)/shard_map/ppermute | solution.py:311
  71.2 5.0 %collective-permute-start.16 = (bf16[16,2048]{1,0:T(8,128)(2,1)S(1)}, bf16[16,2048]{1,0:T(8,128)(2,1)S(1)}, u32[]{:S(2)}, u32[]{:S(2)}) collective-permute-start(bf16[16,2048]{1,0:T(8,128)(2,1)S(1)} %get-tuple-element.42), channel_id=1, source_target_pairs={{0,3},{1,0},{2,1},{3,2},{4,7},{5,4},{6,5},{7,6},{8,11},{9,8},{10,9... | collective-permute-start | bytes 196616 | tf_op jit(solution)/shard_map/ppermute | solution.py:311

commit v3 on v2

--- a/solution.py
+++ b/solution.py
@@ -14,12 +14,12 @@
 
 def attend_kernel(place, spot, *refs, blocks):
     q_hbm, k_hbm, v_hbm, gate_hbm, beta_hbm, decay_hbm, gain_hbm, states_hbm, weight_hbm = refs[:9]
-    expert_hbm, refs = refs[9:12], refs[12:]
-    own_ref, send_refs, expert_refs = refs[0], refs[1:blocks], refs[blocks : blocks + 3]
+    refs = refs[9:]
+    own_ref, send_refs = refs[0], refs[1:blocks]
     (q_ref, k_ref, v_ref, gate_ref, beta_ref, decay_ref, gain_ref, state, weight) = refs[
-        blocks + 3 : blocks + 12
+        blocks : blocks + 9
     ]
-    rows, reads, gated, small_sems, state_sems, weight_sems = refs[blocks + 12 :]
+    rows, reads, gated, small_sems, state_sems, weight_sems = refs[blocks + 9 :]
     steps, requests, _ = q_ref.shape
     heads = v_ref.shape[2] // HV
     pairs = q_ref.shape[2] // HK
@@ -41,19 +41,11 @@
             )
         )
     ]
-    large = [
-        pltpu.make_async_copy(src, dst, weight_sems.at[i])
-        for i, (src, dst) in enumerate(
-            [(weight_hbm, weight)]
-            + [(src.at[0], dst) for src, dst in zip(expert_hbm, expert_refs)]
-        )
-    ]
+    large = pltpu.make_async_copy(weight_hbm, weight, weight_sems.at[0])
     for copy in small:
         copy.start()
     for r in range(requests):
         pltpu.make_async_copy(states_hbm.at[r], state.at[r], state_sems.at[r]).start()
-    for copy in large:
-        copy.start()
     for copy in small:
         copy.wait()
 
@@ -77,14 +69,16 @@
         at = pl.ds(pl.multiple_of(r * vectors, vectors), vectors)
         for g in range(pairs):
             left = rows[g, both, :].astype(jnp.bfloat16)
-            for h in range(g * repeat, (g + 1) * repeat):
-                read = jnp.dot(
-                    left, state[r, h].astype(jnp.bfloat16), preferred_element_type=jnp.float32
-                )
-                reads[h, at, :] = read[:vectors] + read[vectors:]
+            right = [state[r, g * repeat + i].astype(jnp.bfloat16) for i in range(repeat)]
+            read = jnp.dot(left, jnp.concatenate(right, axis=1), preferred_element_type=jnp.float32)
+            read = read[:vectors] + read[vectors:]
+            for i in range(repeat):
+                reads[g * repeat + i, at, :] = read[:, i * HV : (i + 1) * HV]
         return carry
 
-    lax.fori_loop(0, requests, read_states, 0)
+    lax.fori_loop(0, requests // 2, read_states, 0)
+    large.start()
+    lax.fori_loop(requests // 2, requests, read_states, 0)
 
     betas = jax.nn.sigmoid(beta_ref[...].reshape(steps * heads, requests).T)
     decays = decay_ref[...].reshape(steps * heads, requests).T
@@ -132,8 +126,7 @@
     chosen = jnp.where(source == old, 1.0, 0.0).astype(jnp.bfloat16)
     ordered = jnp.dot(chosen, gated[...], preferred_element_type=jnp.float32).astype(jnp.bfloat16)
 
-    for copy in large:
-        copy.wait()
+    large.wait()
     size = steps * each
     columns = weight.shape[1]
     tile = min(512, columns)
@@ -144,7 +137,7 @@
             send_refs[k - 1][:, c : c + tile] = part[k * size : (k + 1) * size].astype(jnp.bfloat16)
 
 
-def attend(place, spot, queries, keys_in, values_in, out_gate, beta, decay, gain, states, weight, mats, blocks):
+def attend(place, spot, queries, keys_in, values_in, out_gate, beta, decay, gain, states, weight, blocks):
     steps, requests, _ = queries.shape
     heads = values_in.shape[2] // HV
     pairs = queries.shape[2] // HK
@@ -156,10 +149,9 @@
     return pl.pallas_call(
         functools.partial(attend_kernel, blocks=blocks),
         out_shape=[jax.ShapeDtypeStruct((size, columns), jnp.float32)]
-        + [jax.ShapeDtypeStruct((size, columns), jnp.bfloat16)] * (blocks - 1)
-        + [pltpu.VMEM(mat.shape[1:], mat.dtype) for mat in mats],
-        in_specs=[pl.BlockSpec(memory_space=pltpu.SMEM)] * 2 + [far] * 12,
-        out_specs=[whole] * (blocks + 3),
+        + [jax.ShapeDtypeStruct((size, columns), jnp.bfloat16)] * (blocks - 1),
+        in_specs=[pl.BlockSpec(memory_space=pltpu.SMEM)] * 2 + [far] * 9,
+        out_specs=[whole] * blocks,
         scratch_shapes=[pltpu.VMEM(x.shape, x.dtype) for x in small]
         + [
             pltpu.VMEM(states.shape, jnp.float32),
@@ -169,14 +161,14 @@
             pltpu.VMEM((steps * requests, heads * HV), jnp.bfloat16),
             pltpu.SemaphoreType.DMA((len(small),)),
             pltpu.SemaphoreType.DMA((requests,)),
-            pltpu.SemaphoreType.DMA((4,)),
+            pltpu.SemaphoreType.DMA((1,)),
         ],
         compiler_params=pltpu.CompilerParams(vmem_limit_bytes=32 << 20),
         name="attend",
-    )(place, spot, *[pltpu.with_memory_space_constraint(x, pltpu.HBM) for x in (*small, states, weight, *mats)])
-
-
-def local(kernel, out_shape, *operands, name):
+    )(place, spot, *[pltpu.with_memory_space_constraint(x, pltpu.HBM) for x in (*small, states, weight)])
+
+
+def local(kernel, out_shape, *operands, name, scratch=()):
     whole = pl.BlockSpec(memory_space=pltpu.VMEM)
     scalars = [x.ndim == 1 for x in operands]
     return pl.pallas_call(
@@ -185,6 +177,7 @@
         in_specs=[pl.BlockSpec(memory_space=pltpu.SMEM) if one else whole for one in scalars],
         out_specs=jax.tree.map(lambda _: whole, out_shape),
         compiler_params=pltpu.CompilerParams(vmem_limit_bytes=12 << 20),
+        scratch_shapes=scratch,
         name=name,
     )(*operands)
 
@@ -203,6 +196,30 @@
     normed_ref[...] = (stream * scale * gain_ref[...]).astype(jnp.bfloat16)
 
 
+def load_kernel(*refs):
+    count = len(refs) // 2
+    copies = [
+        pltpu.make_async_copy(src.at[0], dst, refs[-1].at[i])
+        for i, (src, dst) in enumerate(zip(refs[:count], refs[count:-1]))
+    ]
+    for copy in copies:
+        copy.start()
+    for copy in copies:
+        copy.wait()
+
+
+def load(*mats):
+    return pl.pallas_call(
+        load_kernel,
+        out_shape=[jax.ShapeDtypeStruct(mat.shape[1:], mat.dtype) for mat in mats],
+        in_specs=[pl.BlockSpec(memory_space=pltpu.HBM)] * len(mats),
+        out_specs=[pl.BlockSpec(memory_space=pltpu.VMEM)] * len(mats),
+        scratch_shapes=[pltpu.SemaphoreType.DMA((len(mats),))],
+        compiler_params=pltpu.CompilerParams(vmem_limit_bytes=8 << 20),
+        name="load",
+    )(*[pltpu.with_memory_space_constraint(mat, pltpu.HBM) for mat in mats])
+
+
 def join_kernel(*refs):
     at = 0
     for ref in refs[:-1]:
@@ -216,17 +233,20 @@
     return local(join_kernel, shape, *parts, name="join")
 
 
-def add_kernel(first_ref, second_ref, *outs):
-    total = first_ref[...].astype(jnp.float32) + second_ref[...].astype(jnp.float32)
+def add_kernel(*refs, count):
+    total = refs[0][...].astype(jnp.float32)
+    for ref in refs[1:count]:
+        total = total + ref[...].astype(jnp.float32)
     at = 0
-    for out in outs:
+    for out in refs[count:]:
         out[...] = total[at : at + out.shape[0]].astype(out.dtype)
         at += out.shape[0]
 
 
-def add(first, second, *outs):
-    shapes = [jax.ShapeDtypeStruct((rows, first.shape[1]), dtype) for rows, dtype in outs]
-    return local(add_kernel, shapes, first, second, name="add")
+def add(operands, *outs):
+    shapes = [jax.ShapeDtypeStruct((rows, operands[0].shape[1]), dtype) for rows, dtype in outs]
+    kernel = functools.partial(add_kernel, count=len(operands))
+    return local(kernel, shapes, *operands, name="add")
 
 
 def finish_kernel(stream_ref, own_ref, *rest):
@@ -244,6 +264,7 @@
     ring, width, bits = plan[0][:3]
     top, steps, requests = ids_ref.shape
     each = requests // (ring * width)
+    size = steps * each
     routes = [route_ref[k] for k in range(top)]
     norm = functools.reduce(jnp.add, routes)
     own = spot[0] * ring + place[0]
@@ -251,11 +272,15 @@
     for k in range(top):
         picked = picked + jnp.where(ids_ref[k] == own, routes[k] / norm, 0.0)
 
-    for (_, _, _, flip, skip), x_ref, out_ref in zip(plan, refs[:count], refs[count:]):
+    rows_ref = refs[-1]
+    at = 0
+    shares = []
+    for (_, _, _, flip, skip), x_ref in zip(plan, refs[:count]):
         rows = x_ref.shape[0]
+        rows_ref[pl.ds(at, rows), :] = x_ref[...]
+        at += rows
         row = lax.broadcasted_iota(jnp.int32, (rows, requests), 0) + skip
         column = lax.broadcasted_iota(jnp.int32, (rows, requests), 1)
-        size = steps * each
         block = row // size
         k, m = block % ring, block // ring
         device = jnp.bitwise_xor(spot[0], flip)
@@ -271,15 +296,19 @@
         share = jnp.zeros((rows, requests), jnp.float32)
         for t in range(steps):
             share = jnp.where(moment == t, jnp.broadcast_to(picked[t : t + 1], (rows, requests)), share)
-        share = jnp.sum(jnp.where(request == column, share, 0.0), axis=-1, keepdims=True)
-
-        x = x_ref[...]
-        gated = jnp.dot(x, gate[...], preferred_element_type=jnp.float32)
-        lifted = jnp.dot(x, up[...], preferred_element_type=jnp.float32)
-        hidden = (jax.nn.silu(gated) * lifted).astype(jnp.bfloat16)
-        served = jnp.dot(hidden, down[...], preferred_element_type=jnp.float32)
-        served = served.astype(jnp.bfloat16).astype(jnp.float32) * share
-        out_ref[...] = served.astype(out_ref.dtype)
+        shares.append(jnp.sum(jnp.where(request == column, share, 0.0), axis=-1, keepdims=True))
+
+    x = rows_ref[...]
+    gated = jnp.dot(x, gate[...], preferred_element_type=jnp.float32)
+    lifted = jnp.dot(x, up[...], preferred_element_type=jnp.float32)
+    hidden = (jax.nn.silu(gated) * lifted).astype(jnp.bfloat16)
+    served = jnp.dot(hidden, down[...], preferred_element_type=jnp.float32)
+    served = served.astype(jnp.bfloat16).astype(jnp.float32)
+    at = 0
+    for share, out_ref in zip(shares, refs[count : 2 * count]):
+        rows = out_ref.shape[0]
+        out_ref[...] = (served[at : at + rows] * share).astype(out_ref.dtype)
+        at += rows
 
 
 def shards(
@@ -330,10 +359,12 @@
         head_gain.reshape(1, HV),
         states,
         out_weight,
-        (expert_gate, expert_up, expert_down),
         ring,
     )
     arrived = [along(parts[k], k) for k in range(1, ring)]
+    arrived, weights = lax.optimization_barrier(
+        (arrived, load(expert_gate, expert_up, expert_down))
+    )
     stream, normed = local(
         norm_kernel,
         [
@@ -360,31 +391,57 @@
             spot,
             ids,
             route,
-            *parts[ring:],
+            *weights,
             *[x for x, _, _, _ in pieces],
             name="experts",
+            scratch=[pltpu.VMEM((sum(x.shape[0] for x, _, _, _ in pieces), columns), jnp.bfloat16)],
         )
 
-    rows = join(normed, *[along(normed, ring - k) for k in range(1, ring)])
-    for j in range(bits - 1):
-        rows = join(rows, across(rows, j))
-    half = rows.shape[0]
-    late = across(rows, bits - 1)
-    served, peer_served = experts(
-        (rows, jnp.float32, 0, 0), (other(rows), jnp.bfloat16, 1, 0)
-    )
-    peer_served, late = lax.optimization_barrier((peer_served, late))
-    total = add(served, other(peer_served), (half, jnp.float32))[0]
-    late_served = experts((late, jnp.float32, 0, half))[0]
-    peer_late = experts((other(late), jnp.bfloat16, 1, half))[0]
-    send = add(late_served, other(peer_late), (half, jnp.bfloat16))[0]
+    first = join(normed, *[along(normed, ring - k) for k in range(1, ring)])
+    held = first.shape[0]
+    last = (1 << bits) - 1
+    sets, served, totals = {0: first}, {}, {}
+    later = first
+    for depth in range(bits + 1):
+        group = [m for m in range(last + 1) if m.bit_count() == depth]
+        for m in group:
+            if m:
+                j = m.bit_length() - 1
+                sets[m] = across(later if m == 1 << j and j else sets[m - (1 << j)], j)
+        if depth:
+            before = [m for m in served if m.bit_count() == depth - 1]
+            done, got = lax.optimization_barrier(
+                ([served[m] for m in before], [sets[m] for m in group])
+            )
+            served.update(zip(before, done))
+            sets.update(zip(group, got))
+        for m in group:
+            served[m] = experts(
+                (sets[m], jnp.float32, 0, m * held), (other(sets[m]), jnp.bfloat16, 1, m * held)
+            )
+        if depth == 0:
+            later, served[0] = lax.optimization_barrier((first, served[0]))
+    for m in range(last + 1):
+        leaves = m >> (bits - 1)
+        totals[m] = add(
+            (served[m][0], other(served[m][1])), (held, jnp.bfloat16 if leaves else jnp.float32)
+        )[0]
+    came = {}
     for j in reversed(range(bits)):
-        came = across(send, j)
-        if j > 0:
-            half //= 2
-            total, send = add(total, came, (half, jnp.float32), (half, jnp.bfloat16))
+        top = 1 << j
+        for m in reversed(range(1, top)):
+            leaves = m >> (j - 1)
+            totals[m] = add(
+                (totals[m], across(totals[m + top], j)),
+                (held, jnp.bfloat16 if leaves else jnp.float32),
+            )[0]
+        if top > 1:
+            totals[top], totals[0] = lax.optimization_barrier((totals[top], totals[0]))
+        came[j] = across(totals[top], j)
     total, *blocks = add(
-        total, came, (size, jnp.float32), *[(size, jnp.bfloat16)] * (ring - 1)
+        (totals[0], *[came[j] for j in reversed(range(bits))]),
+        (size, jnp.float32),
+        *[(size, jnp.bfloat16)] * (ring - 1),
     )
     return local(
         finish_kernel,

time: 77 us -> 71.9 us (0.934)
  waiting for transfers between devices: 37.5 us -> 28.2 us
  starting transfers between devices: 21.5 us -> 24.9 us
    ppermute x4 -> x6, waiting for transfers between devices: 23.1 us -> 16.6 us  [across(): lax.ppermute(x, 'dev', [(i, i ^ 2 << (j + i % 2) % bits) for i in range(w...]
    pallas_call x0 -> x1, Pallas kernels: none -> 2.88 us  [load(): pl.pallas_call(load_kernel, out_shape=[jax.ShapeDtypeStruct(mat.shape[1:]...]
    ppermute x4 -> x6, starting transfers between devices: 5.63 us -> 8.05 us  [across(): lax.ppermute(x, 'dev', [(i, i ^ 2 << (j + i % 2) % bits) for i in range(w...]
    pallas_call x1, Pallas kernels: 12.2 us -> 9.89 us  [attend(): pl.pallas_call(functools.partial(attend_kernel, blocks=blocks), out_shape...]
    ppermute x9, waiting for transfers between devices: 11.8 us -> 9.54 us  [along(): return lax.ppermute(x, 'head', [(i, (i + k) % ring) for i in range(ring)])]
    ppermute x4 -> x8, starting transfers between devices: 0.71 us -> 1.67 us  [other(): return lax.ppermute(x, 'dev', [(i, i ^ 1) for i in range(width)])]
    ppermute x4 -> x8, waiting for transfers between devices: 2.58 us -> 2.13 us  [other(): return lax.ppermute(x, 'dev', [(i, i ^ 1) for i in range(width)])]
    pallas_call x11 -> x13, Pallas kernels: 5.53 us -> 5.75 us  [local(): pl.pallas_call(kernel, out_shape=out_shape, in_specs=[pl.BlockSpec(memory...]
  transfers between devices with their start and end apart: 17 -> 23, of which waited for: 15 -> 16; matrix products, arithmetic and copies ran while one was open for 0% -> 0% of each run, Pallas kernels for 4% -> 9%
where the time goes in v3:
time: 71.9 us; the launch traced here: 71.8 us
  waiting for transfers between devices  28.2 us (39%)
  starting transfers between devices  24.9 us (35%)
  Pallas kernels  18.5 us (26%)
    ppermute x6, waiting for transfers between devices, across(): lax.ppermute(x, 'dev', [(i, i ^ 2 << (j + i % 2) % bits) for i in range(w...  16.6 us
    ppermute x9, starting transfers between devices, along(): return lax.ppermute(x, 'head', [(i, (i + k) % ring) for i in range(ring)])  15.2 us
    pallas_call x1, Pallas kernels, attend(): pl.pallas_call(functools.partial(attend_kernel, blocks=blocks), out_shape...  9.89 us
    ppermute x9, waiting for transfers between devices, along(): return lax.ppermute(x, 'head', [(i, (i + k) % ring) for i in range(ring)])  9.54 us
    ppermute x6, starting transfers between devices, across(): lax.ppermute(x, 'dev', [(i, i ^ 2 << (j + i % 2) % bits) for i in range(w...  8.05 us
    pallas_call x13, Pallas kernels, local(): pl.pallas_call(kernel, out_shape=out_shape, in_specs=[pl.BlockSpec(memory...  5.75 us
    pallas_call x1, Pallas kernels, load(): pl.pallas_call(load_kernel, out_shape=[jax.ShapeDtypeStruct(mat.shape[1:]...  2.88 us
    ppermute x8, waiting for transfers between devices, other(): return lax.ppermute(x, 'dev', [(i, i ^ 1) for i in range(width)])  2.13 us
  transfers between devices with their start and end apart: 23, of which 16 were waited for; matrix products, arithmetic and copies ran while one was open for 0% of the time, Pallas kernels for 9%

profile of v3, /device:TPU:0, one launch (start us, length us, event | category | flops | bytes accessed | tf_op | source)
XLA Modules:
  0.0 71.8 jit_solution(14952629111292432498)
XLA Ops:
  0.0 9.9 %attend.1 = (f32[16,2048]{1,0:T(8,128)S(1)}, bf16[16,2048]{1,0:T(8,128)(2,1)S(1)}, bf16[16,2048]{1,0:T(8,128)(2,1)S(1)}, bf16[16,2048]{1,0:T(8,128)(2,1)S(1)}) custom-call(s32[1]{0:T(128)} %bitcast.place, s32[1]{0:T(128)} %bitcast.1.spot, bf16[4,16,512]{2,1,0:T(8,128)(2,1)} %refs_0_.2, bf16[4,16,512]{2,1,0:T(8,128)(2,1)} %refs_1_.2, ...), custom_call_target="tpu_custom_call" | custom-call | tf_op jit(solution)/shard_map/attend/pallas_call | solution.py:149
  9.9 3.1 %collective-permute-start = (bf16[16,2048]{1,0:T(8,128)(2,1)S(1)}, bf16[16,2048]{1,0:T(8,128)(2,1)S(1)}, u32[]{:S(2)}, u32[]{:S(2)}) collective-permute-start(bf16[16,2048]{1,0:T(8,128)(2,1)S(1)} %get-tuple-element.47), channel_id=1, source_target_pairs={{0,1},{1,2},{2,3},{3,0},{4,5},{5,6},{6,7},{7,4},{8,9},{9,10},{10,1... | collective-permute-start | bytes 196616 | tf_op jit(solution)/shard_map/ppermute | solution.py:340
  13.0 2.6 %collective-permute-start.1 = (bf16[16,2048]{1,0:T(8,128)(2,1)S(1)}, bf16[16,2048]{1,0:T(8,128)(2,1)S(1)}, u32[]{:S(2)}, u32[]{:S(2)}) collective-permute-start(bf16[16,2048]{1,0:T(8,128)(2,1)S(1)} %get-tuple-element.48), channel_id=1, source_target_pairs={{0,2},{1,3},{2,0},{3,1},{4,6},{5,7},{6,4},{7,5},{8,10},{9,11},{10,... | collective-permute-start | bytes 196616 | tf_op jit(solution)/shard_map/ppermute | solution.py:340
  15.6 1.4 %collective-permute-start.2 = (bf16[16,2048]{1,0:T(8,128)(2,1)S(1)}, bf16[16,2048]{1,0:T(8,128)(2,1)S(1)}, u32[]{:S(2)}, u32[]{:S(2)}) collective-permute-start(bf16[16,2048]{1,0:T(8,128)(2,1)S(1)} %get-tuple-element.49), channel_id=1, source_target_pairs={{0,3},{1,0},{2,1},{3,2},{4,7},{5,4},{6,5},{7,6},{8,11},{9,8},{10,9... | collective-permute-start | bytes 196616 | tf_op jit(solution)/shard_map/ppermute | solution.py:340
  17.0 2.9 %load.1 = (bf16[2048,512]{1,0:T(8,128)(2,1)S(1)}, bf16[2048,512]{1,0:T(8,128)(2,1)S(1)}, bf16[512,2048]{1,0:T(8,128)(2,1)S(1)}) custom-call(bf16[1,2048,512]{2,1,0:T(8,128)(2,1)} %refs_0_.3, bf16[1,2048,512]{2,1,0:T(8,128)(2,1)} %refs_1_.3, bf16[1,512,2048]{2,1,0:T(8,128)(2,1)} %refs_2_.3), custom_call_target="tpu_custom_call" | custom-call | tf_op jit(solution)/shard_map/load/pallas_call | solution.py:212
  19.9 0.2 collective-permute-done.1.rest_1_
  20.1 0.3 collective-permute-done.2.rest_2_
  20.3 0.2 norm.1
  20.5 1.6 %collective-permute-start.5 = (bf16[16,2048]{1,0:T(8,128)(2,1)S(1)}, bf16[16,2048]{1,0:T(8,128)(2,1)S(1)}, u32[]{:S(2)}, u32[]{:S(2)}) collective-permute-start(bf16[16,2048]{1,0:T(8,128)(2,1)S(1)} %get-tuple-element.60.refs_0_), channel_id=1, source_target_pairs={{0,1},{1,2},{2,3},{3,0},{4,5},{5,6},{6,7},{7,4},{8,9},{9,10},{10,1... | collective-permute-start | bytes 196616 | tf_op jit(solution)/shard_map/ppermute | solution.py:340
  22.1 2.0 %collective-permute-start.4 = (bf16[16,2048]{1,0:T(8,128)(2,1)S(1)}, bf16[16,2048]{1,0:T(8,128)(2,1)S(1)}, u32[]{:S(2)}, u32[]{:S(2)}) collective-permute-start(bf16[16,2048]{1,0:T(8,128)(2,1)S(1)} %get-tuple-element.60.refs_0_), channel_id=1, source_target_pairs={{0,2},{1,3},{2,0},{3,1},{4,6},{5,7},{6,4},{7,5},{8,10},{9,11},{10,... | collective-permute-start | bytes 196616 | tf_op jit(solution)/shard_map/ppermute | solution.py:340
  24.1 0.4 collective-permute-start.3
  24.5 2.3 %collective-permute-done.5.refs_3_ = bf16[16,2048]{1,0:T(8,128)(2,1)S(1)} collective-permute-done((bf16[16,2048]{1,0:T(8,128)(2,1)S(1)}, bf16[16,2048]{1,0:T(8,128)(2,1)S(1)}, u32[]{:S(2)}, u32[]{:S(2)}) %collective-permute-start.5) | collective-permute-done | bytes 65568 | tf_op jit(solution)/shard_map/ppermute | solution.py:340
  26.9 1.9 %collective-permute-done.4.refs_2_ = bf16[16,2048]{1,0:T(8,128)(2,1)S(1)} collective-permute-done((bf16[16,2048]{1,0:T(8,128)(2,1)S(1)}, bf16[16,2048]{1,0:T(8,128)(2,1)S(1)}, u32[]{:S(2)}, u32[]{:S(2)}) %collective-permute-start.4) | collective-permute-done | bytes 65568 | tf_op jit(solution)/shard_map/ppermute | solution.py:340
  28.8 0.3 collective-permute-done.3.refs_1_
  29.1 0.1 collective-permute-start.6
  29.2 1.5 %collective-permute-start.7 = (bf16[64,2048]{1,0:T(8,128)(2,1)S(1)}, bf16[64,2048]{1,0:T(8,128)(2,1)S(1)}, u32[]{:S(2)}, u32[]{:S(2)}) collective-permute-start(bf16[64,2048]{1,0:T(8,128)(2,1)S(1)} %join.1.refs_0_), channel_id=1, source_target_pairs={{0,8},{4,20},{8,0},{12,28},{16,24},{20,4},{24,16},{28,12},{1,9},{5... | collective-permute-start | bytes 786440 | tf_op jit(solution)/shard_map/ppermute | solution.py:343
  30.6 0.1 collective-permute-done.6.refs_1_
  30.7 1.1 %experts.4 = (f32[64,2048]{1,0:T(8,128)S(1)}, bf16[64,2048]{1,0:T(8,128)(2,1)S(1)}) custom-call(s32[1]{0:T(128)} %bitcast.place, s32[1]{0:T(128)} %bitcast.1.spot, s32[10,4,128]{2,1,0:T(4,128)S(1)} %bitcast.8, f32[10,4,128]{2,1,0:T(4,128)S(1)} %bitcast.12, bf16[2048,512]{1,0:T(8,128)(2,1)S(1)} %get-tuple-element.57.gate, ...), custom_call_target="tpu_custom_call" | custom-call | tf_op jit(solution)/shard_map/experts/pallas_call | solution.py:174
  31.8 1.5 %collective-permute-start.8 = (bf16[64,2048]{1,0:T(8,128)(2,1)S(1)}, bf16[64,2048]{1,0:T(8,128)(2,1)S(1)}, u32[]{:S(2)}, u32[]{:S(2)}) collective-permute-start(bf16[64,2048]{1,0:T(8,128)(2,1)S(1)} %join.1.refs_0_), channel_id=1, source_target_pairs={{0,16},{4,12},{8,24},{12,4},{16,0},{20,28},{24,8},{28,20},{1,17},{... | collective-permute-start | bytes 786440 | tf_op jit(solution)/shard_map/ppermute | solution.py:343
  33.4 3.2 %collective-permute-done.7.refs_0_ = bf16[64,2048]{1,0:T(8,128)(2,1)S(1)} collective-permute-done((bf16[64,2048]{1,0:T(8,128)(2,1)S(1)}, bf16[64,2048]{1,0:T(8,128)(2,1)S(1)}, u32[]{:S(2)}, u32[]{:S(2)}) %collective-permute-start.7) | collective-permute-done | bytes 262176 | tf_op jit(solution)/shard_map/ppermute | solution.py:343
  36.5 1.7 %collective-permute-done.8.refs_0_ = bf16[64,2048]{1,0:T(8,128)(2,1)S(1)} collective-permute-done((bf16[64,2048]{1,0:T(8,128)(2,1)S(1)}, bf16[64,2048]{1,0:T(8,128)(2,1)S(1)}, u32[]{:S(2)}, u32[]{:S(2)}) %collective-permute-start.8) | collective-permute-done | bytes 262176 | tf_op jit(solution)/shard_map/ppermute | solution.py:343
  38.3 0.1 collective-permute-start.10
  38.4 0.4 collective-permute-start.9
  38.8 1.5 %collective-permute-start.11 = (bf16[64,2048]{1,0:T(8,128)(2,1)S(1)}, bf16[64,2048]{1,0:T(8,128)(2,1)S(1)}, u32[]{:S(2)}, u32[]{:S(2)}) collective-permute-start(bf16[64,2048]{1,0:T(8,128)(2,1)S(1)} %collective-permute-done.7.refs_0_), channel_id=1, source_target_pairs={{0,16},{4,12},{8,24},{12,4},{16,0},{20,28},{24,8},{28,20},{1,17},{... | collective-permute-start | bytes 786440 | tf_op jit(solution)/shard_map/ppermute | solution.py:343
  40.3 1.1 %experts.6 = (f32[64,2048]{1,0:T(8,128)S(1)}, bf16[64,2048]{1,0:T(8,128)(2,1)S(1)}) custom-call(s32[1]{0:T(128)} %bitcast.place, s32[1]{0:T(128)} %bitcast.1.spot, s32[10,4,128]{2,1,0:T(4,128)S(1)} %bitcast.9, f32[10,4,128]{2,1,0:T(4,128)S(1)} %bitcast.13, bf16[2048,512]{1,0:T(8,128)(2,1)S(1)} %get-tuple-element.57.gate, ...), custom_call_target="tpu_custom_call" | custom-call | tf_op jit(solution)/shard_map/experts/pallas_call | solution.py:174
  41.4 1.1 %experts.5 = (f32[64,2048]{1,0:T(8,128)S(1)}, bf16[64,2048]{1,0:T(8,128)(2,1)S(1)}) custom-call(s32[1]{0:T(128)} %bitcast.place, s32[1]{0:T(128)} %bitcast.1.spot, s32[10,4,128]{2,1,0:T(4,128)S(1)} %bitcast.10, f32[10,4,128]{2,1,0:T(4,128)S(1)} %bitcast.14, bf16[2048,512]{1,0:T(8,128)(2,1)S(1)} %get-tuple-element.57.gate, ...), custom_call_target="tpu_custom_call" | custom-call | tf_op jit(solution)/shard_map/experts/pallas_call | solution.py:174
  42.5 2.6 %collective-permute-done.11.refs_0_ = bf16[64,2048]{1,0:T(8,128)(2,1)S(1)} collective-permute-done((bf16[64,2048]{1,0:T(8,128)(2,1)S(1)}, bf16[64,2048]{1,0:T(8,128)(2,1)S(1)}, u32[]{:S(2)}, u32[]{:S(2)}) %collective-permute-start.11) | collective-permute-done | bytes 262176 | tf_op jit(solution)/shard_map/ppermute | solution.py:343
  45.2 1.5 %collective-permute-done.16.refs_1_ = bf16[64,2048]{1,0:T(8,128)(2,1)S(1)} collective-permute-done((bf16[64,2048]{1,0:T(8,128)(2,1)S(1)}, bf16[64,2048]{1,0:T(8,128)(2,1)S(1)}, u32[]{:S(2)}, u32[]{:S(2)}) %collective-permute-start.16) | collective-permute-done | bytes 262176 | tf_op jit(solution)/shard_map/ppermute | solution.py:348
  46.7 1.1 %experts.7 = (f32[64,2048]{1,0:T(8,128)S(1)}, bf16[64,2048]{1,0:T(8,128)(2,1)S(1)}) custom-call(s32[1]{0:T(128)} %bitcast.place, s32[1]{0:T(128)} %bitcast.1.spot, s32[10,4,128]{2,1,0:T(4,128)S(1)} %bitcast.11, f32[10,4,128]{2,1,0:T(4,128)S(1)} %bitcast.15, bf16[2048,512]{1,0:T(8,128)(2,1)S(1)} %get-tuple-element.57.gate, ...), custom_call_target="tpu_custom_call" | custom-call | tf_op jit(solution)/shard_map/experts/pallas_call | solution.py:174
  47.8 0.2 collective-permute-start.17
  48.0 0.4 collective-permute-start.13
  48.4 0.1 collective-permute-start.12
  48.6 0.4 collective-permute-start.15
  48.9 0.5 collective-permute-done.17.refs_1_
  49.5 1.5 %collective-permute-start.18 = (bf16[64,2048]{1,0:T(8,128)(2,1)S(1)}, bf16[64,2048]{1,0:T(8,128)(2,1)S(1)}, u32[]{:S(2)}, u32[]{:S(2)}) collective-permute-start(bf16[64,2048]{1,0:T(8,128)(2,1)S(1)} %add.9), channel_id=1, source_target_pairs={{0,16},{4,12},{8,24},{12,4},{16,0},{20,28},{24,8},{28,20},{1,17},{... | collective-permute-start | bytes 786440 | tf_op jit(solution)/shard_map/ppermute | solution.py:343
  51.0 0.1 add.7.refs_0_
  51.2 0.6 collective-permute-start.14
  51.9 4.1 %collective-permute-done.18.refs_1_ = bf16[64,2048]{1,0:T(8,128)(2,1)S(1)} collective-permute-done((bf16[64,2048]{1,0:T(8,128)(2,1)S(1)}, bf16[64,2048]{1,0:T(8,128)(2,1)S(1)}, u32[]{:S(2)}, u32[]{:S(2)}) %collective-permute-start.18) | collective-permute-done | bytes 262176 | tf_op jit(solution)/shard_map/ppermute | solution.py:343
  56.0 1.5 %collective-permute-start.19 = (bf16[64,2048]{1,0:T(8,128)(2,1)S(1)}, bf16[64,2048]{1,0:T(8,128)(2,1)S(1)}, u32[]{:S(2)}, u32[]{:S(2)}) collective-permute-start(bf16[64,2048]{1,0:T(8,128)(2,1)S(1)} %add.10), channel_id=1, source_target_pairs={{0,8},{4,20},{8,0},{12,28},{16,24},{20,4},{24,16},{28,12},{1,9},{5... | collective-permute-start | bytes 786440 | tf_op jit(solution)/shard_map/ppermute | solution.py:343
  57.5 2.0 %collective-permute-done.14.refs_1_ = bf16[64,2048]{1,0:T(8,128)(2,1)S(1)} collective-permute-done((bf16[64,2048]{1,0:T(8,128)(2,1)S(1)}, bf16[64,2048]{1,0:T(8,128)(2,1)S(1)}, u32[]{:S(2)}, u32[]{:S(2)}) %collective-permute-start.14) | collective-permute-done | bytes 262176 | tf_op jit(solution)/shard_map/ppermute | solution.py:343
  59.5 3.0 %collective-permute-done.19.refs_2_ = bf16[64,2048]{1,0:T(8,128)(2,1)S(1)} collective-permute-done((bf16[64,2048]{1,0:T(8,128)(2,1)S(1)}, bf16[64,2048]{1,0:T(8,128)(2,1)S(1)}, u32[]{:S(2)}, u32[]{:S(2)}) %collective-permute-start.19) | collective-permute-done | bytes 262176 | tf_op jit(solution)/shard_map/ppermute | solution.py:343
  62.4 0.1 add.11
  62.5 1.6 %collective-permute-start.20 = (bf16[16,2048]{1,0:T(8,128)(2,1)S(1)}, bf16[16,2048]{1,0:T(8,128)(2,1)S(1)}, u32[]{:S(2)}, u32[]{:S(2)}) collective-permute-start(bf16[16,2048]{1,0:T(8,128)(2,1)S(1)} %get-tuple-element.84), channel_id=1, source_target_pairs={{0,1},{1,2},{2,3},{3,0},{4,5},{5,6},{6,7},{7,4},{8,9},{9,10},{10,1... | collective-permute-start | bytes 196616 | tf_op jit(solution)/shard_map/ppermute | solution.py:340
  64.1 1.3 %collective-permute-start.21 = (bf16[16,2048]{1,0:T(8,128)(2,1)S(1)}, bf16[16,2048]{1,0:T(8,128)(2,1)S(1)}, u32[]{:S(2)}, u32[]{:S(2)}) collective-permute-start(bf16[16,2048]{1,0:T(8,128)(2,1)S(1)} %get-tuple-element.85), channel_id=1, source_target_pairs={{0,2},{1,3},{2,0},{3,1},{4,6},{5,7},{6,4},{7,5},{8,10},{9,11},{10,... | collective-permute-start | bytes 196616 | tf_op jit(solution)/shard_map/ppermute | solution.py:340
  65.5 1.1 %collective-permute-start.22 = (bf16[16,2048]{1,0:T(8,128)(2,1)S(1)}, bf16[16,2048]{1,0:T(8,128)(2,1)S(1)}, u32[]{:S(2)}, u32[]{:S(2)}) collective-permute-start(bf16[16,2048]{1,0:T(8,128)(2,1)S(1)} %get-tuple-element.86), channel_id=1, source_target_pairs={{0,3},{1,0},{2,1},{3,2},{4,7},{5,4},{6,5},{7,6},{8,11},{9,8},{10,9... | collective-permute-start | bytes 196616 | tf_op jit(solution)/shard_map/ppermute | solution.py:340
  66.6 2.6 %collective-permute-done.20.rest_0_ = bf16[16,2048]{1,0:T(8,128)(2,1)S(1)} collective-permute-done((bf16[16,2048]{1,0:T(8,128)(2,1)S(1)}, bf16[16,2048]{1,0:T(8,128)(2,1)S(1)}, u32[]{:S(2)}, u32[]{:S(2)}) %collective-permute-start.20) | collective-permute-done | bytes 65568 | tf_op jit(solution)/shard_map/ppermute | solution.py:340
  69.2 1.9 %collective-permute-done.21.rest_1_ = bf16[16,2048]{1,0:T(8,128)(2,1)S(1)} collective-permute-done((bf16[16,2048]{1,0:T(8,128)(2,1)S(1)}, bf16[16,2048]{1,0:T(8,128)(2,1)S(1)}, u32[]{:S(2)}, u32[]{:S(2)}) %collective-permute-start.21) | collective-permute-done | bytes 65568 | tf_op jit(solution)/shard_map/ppermute | solution.py:340
  71.1 0.7 finish.1
  (21 shorter events, 0.3 us)
Async XLA Ops:
  9.9 10.0 %collective-permute-start = (bf16[16,2048]{1,0:T(8,128)(2,1)S(1)}, bf16[16,2048]{1,0:T(8,128)(2,1)S(1)}, u32[]{:S(2)}, u32[]{:S(2)}) collective-permute-start(bf16[16,2048]{1,0:T(8,128)(2,1)S(1)} %get-tuple-element.47), channel_id=1, source_target_pairs={{0,1},{1,2},{2,3},{3,0},{4,5},{5,6},{6,7},{7,4},{8,9},{9,10},{10,1... | collective-permute-start | bytes 196616 | tf_op jit(solution)/shard_map/ppermute | solution.py:340
  13.0 7.1 %collective-permute-start.1 = (bf16[16,2048]{1,0:T(8,128)(2,1)S(1)}, bf16[16,2048]{1,0:T(8,128)(2,1)S(1)}, u32[]{:S(2)}, u32[]{:S(2)}) collective-permute-start(bf16[16,2048]{1,0:T(8,128)(2,1)S(1)} %get-tuple-element.48), channel_id=1, source_target_pairs={{0,2},{1,3},{2,0},{3,1},{4,6},{5,7},{6,4},{7,5},{8,10},{9,11},{10,... | collective-permute-start | bytes 196616 | tf_op jit(solution)/shard_map/ppermute | solution.py:340
  15.6 4.8 %copy-start.2 = (bf16[4,4,2048]{2,1,0:T(4,128)(2,1)S(1)}, bf16[4,4,2048]{2,1,0:T(4,128)(2,1)}, u32[]{:S(2)}) copy-start(bf16[4,4,2048]{2,1,0:T(4,128)(2,1)} %residual_ref.1) | copy-start | bytes 196612
  15.6 4.8 %copy-start.3 = (f32[2048]{0:T(1024)S(1)}, f32[2048]{0:T(1024)}, u32[]{:S(2)}) copy-start(f32[2048]{0:T(1024)} %param.26) | copy-start | bytes 24580
  15.6 15.1 %copy-start = (s32[4,128,10]{1,0,2:T(4,128)S(1)}, s32[4,128,10]{1,0,2:T(4,128)}, u32[]{:S(2)}) copy-start(s32[4,128,10]{1,0,2:T(4,128)} %param.27) | copy-start | bytes 61444
  15.6 15.1 %copy-start.1 = (f32[4,128,10]{1,0,2:T(4,128)S(1)}, f32[4,128,10]{1,0,2:T(4,128)}, u32[]{:S(2)}) copy-start(f32[4,128,10]{1,0,2:T(4,128)} %param.28) | copy-start | bytes 61444
  15.6 4.8 %collective-permute-start.2 = (bf16[16,2048]{1,0:T(8,128)(2,1)S(1)}, bf16[16,2048]{1,0:T(8,128)(2,1)S(1)}, u32[]{:S(2)}, u32[]{:S(2)}) collective-permute-start(bf16[16,2048]{1,0:T(8,128)(2,1)S(1)} %get-tuple-element.49), channel_id=1, source_target_pairs={{0,3},{1,0},{2,1},{3,2},{4,7},{5,4},{6,5},{7,6},{8,11},{9,8},{10,9... | collective-permute-start | bytes 196616 | tf_op jit(solution)/shard_map/ppermute | solution.py:340
  20.5 6.4 %collective-permute-start.5 = (bf16[16,2048]{1,0:T(8,128)(2,1)S(1)}, bf16[16,2048]{1,0:T(8,128)(2,1)S(1)}, u32[]{:S(2)}, u32[]{:S(2)}) collective-permute-start(bf16[16,2048]{1,0:T(8,128)(2,1)S(1)} %get-tuple-element.60.refs_0_), channel_id=1, source_target_pairs={{0,1},{1,2},{2,3},{3,0},{4,5},{5,6},{6,7},{7,4},{8,9},{9,10},{10,1... | collective-permute-start | bytes 196616 | tf_op jit(solution)/shard_map/ppermute | solution.py:340
  22.1 6.7 %collective-permute-start.4 = (bf16[16,2048]{1,0:T(8,128)(2,1)S(1)}, bf16[16,2048]{1,0:T(8,128)(2,1)S(1)}, u32[]{:S(2)}, u32[]{:S(2)}) collective-permute-start(bf16[16,2048]{1,0:T(8,128)(2,1)S(1)} %get-tuple-element.60.refs_0_), channel_id=1, source_target_pairs={{0,2},{1,3},{2,0},{3,1},{4,6},{5,7},{6,4},{7,5},{8,10},{9,11},{10,... | collective-permute-start | bytes 196616 | tf_op jit(solution)/shard_map/ppermute | solution.py:340
  24.1 5.0 %collective-permute-start.3 = (bf16[16,2048]{1,0:T(8,128)(2,1)S(1)}, bf16[16,2048]{1,0:T(8,128)(2,1)S(1)}, u32[]{:S(2)}, u32[]{:S(2)}) collective-permute-start(bf16[16,2048]{1,0:T(8,128)(2,1)S(1)} %get-tuple-element.60.refs_0_), channel_id=1, source_target_pairs={{0,3},{1,0},{2,1},{3,2},{4,7},{5,4},{6,5},{7,6},{8,11},{9,8},{10,9... | collective-permute-start | bytes 196616 | tf_op jit(solution)/shard_map/ppermute | solution.py:340
  29.1 1.6 %collective-permute-start.6 = (bf16[64,2048]{1,0:T(8,128)(2,1)S(1)}, bf16[64,2048]{1,0:T(8,128)(2,1)S(1)}, u32[]{:S(2)}, u32[]{:S(2)}) collective-permute-start(bf16[64,2048]{1,0:T(8,128)(2,1)S(1)} %join.1.refs_0_), channel_id=1, source_target_pairs={{0,4},{4,0},{8,12},{12,8},{16,20},{20,16},{24,28},{28,24},{1,5},{5... | collective-permute-start | bytes 786440 | tf_op jit(solution)/shard_map/ppermute | solution.py:348
  29.2 7.4 %collective-permute-start.7 = (bf16[64,2048]{1,0:T(8,128)(2,1)S(1)}, bf16[64,2048]{1,0:T(8,128)(2,1)S(1)}, u32[]{:S(2)}, u32[]{:S(2)}) collective-permute-start(bf16[64,2048]{1,0:T(8,128)(2,1)S(1)} %join.1.refs_0_), channel_id=1, source_target_pairs={{0,8},{4,20},{8,0},{12,28},{16,24},{20,4},{24,16},{28,12},{1,9},{5... | collective-permute-start | bytes 786440 | tf_op jit(solution)/shard_map/ppermute | solution.py:343
  31.8 6.4 %collective-permute-start.8 = (bf16[64,2048]{1,0:T(8,128)(2,1)S(1)}, bf16[64,2048]{1,0:T(8,128)(2,1)S(1)}, u32[]{:S(2)}, u32[]{:S(2)}) collective-permute-start(bf16[64,2048]{1,0:T(8,128)(2,1)S(1)} %join.1.refs_0_), channel_id=1, source_target_pairs={{0,16},{4,12},{8,24},{12,4},{16,0},{20,28},{24,8},{28,20},{1,17},{... | collective-permute-start | bytes 786440 | tf_op jit(solution)/shard_map/ppermute | solution.py:343
  38.3 2.0 %collective-permute-start.10 = (bf16[64,2048]{1,0:T(8,128)(2,1)S(1)}, bf16[64,2048]{1,0:T(8,128)(2,1)S(1)}, u32[]{:S(2)}, u32[]{:S(2)}) collective-permute-start(bf16[64,2048]{1,0:T(8,128)(2,1)S(1)} %collective-permute-done.8.refs_0_), channel_id=1, source_target_pairs={{0,4},{4,0},{8,12},{12,8},{16,20},{20,16},{24,28},{28,24},{1,5},{5... | collective-permute-start | bytes 786440 | tf_op jit(solution)/shard_map/ppermute | solution.py:348
  38.4 3.0 %collective-permute-start.9 = (bf16[64,2048]{1,0:T(8,128)(2,1)S(1)}, bf16[64,2048]{1,0:T(8,128)(2,1)S(1)}, u32[]{:S(2)}, u32[]{:S(2)}) collective-permute-start(bf16[64,2048]{1,0:T(8,128)(2,1)S(1)} %collective-permute-done.7.refs_0_), channel_id=1, source_target_pairs={{0,4},{4,0},{8,12},{12,8},{16,20},{20,16},{24,28},{28,24},{1,5},{5... | collective-permute-start | bytes 786440 | tf_op jit(solution)/shard_map/ppermute | solution.py:348
  38.8 6.4 %collective-permute-start.11 = (bf16[64,2048]{1,0:T(8,128)(2,1)S(1)}, bf16[64,2048]{1,0:T(8,128)(2,1)S(1)}, u32[]{:S(2)}, u32[]{:S(2)}) collective-permute-start(bf16[64,2048]{1,0:T(8,128)(2,1)S(1)} %collective-permute-done.7.refs_0_), channel_id=1, source_target_pairs={{0,16},{4,12},{8,24},{12,4},{16,0},{20,28},{24,8},{28,20},{1,17},{... | collective-permute-start | bytes 786440 | tf_op jit(solution)/shard_map/ppermute | solution.py:343
  45.2 1.5 %collective-permute-start.16 = (bf16[64,2048]{1,0:T(8,128)(2,1)S(1)}, bf16[64,2048]{1,0:T(8,128)(2,1)S(1)}, u32[]{:S(2)}, u32[]{:S(2)}) collective-permute-start(bf16[64,2048]{1,0:T(8,128)(2,1)S(1)} %collective-permute-done.11.refs_0_), channel_id=1, source_target_pairs={{0,4},{4,0},{8,12},{12,8},{16,20},{20,16},{24,28},{28,24},{1,5},{5... | collective-permute-start | bytes 786440 | tf_op jit(solution)/shard_map/ppermute | solution.py:348
  47.8 1.6 %collective-permute-start.17 = (bf16[64,2048]{1,0:T(8,128)(2,1)S(1)}, bf16[64,2048]{1,0:T(8,128)(2,1)S(1)}, u32[]{:S(2)}, u32[]{:S(2)}) collective-permute-start(bf16[64,2048]{1,0:T(8,128)(2,1)S(1)} %get-tuple-element.82), channel_id=1, source_target_pairs={{0,4},{4,0},{8,12},{12,8},{16,20},{20,16},{24,28},{28,24},{1,5},{5... | collective-permute-start | bytes 786440 | tf_op jit(solution)/shard_map/ppermute | solution.py:348
  48.0 3.0 %collective-permute-start.13 = (bf16[64,2048]{1,0:T(8,128)(2,1)S(1)}, bf16[64,2048]{1,0:T(8,128)(2,1)S(1)}, u32[]{:S(2)}, u32[]{:S(2)}) collective-permute-start(bf16[64,2048]{1,0:T(8,128)(2,1)S(1)} %get-tuple-element.75), channel_id=1, source_target_pairs={{0,4},{4,0},{8,12},{12,8},{16,20},{20,16},{24,28},{28,24},{1,5},{5... | collective-permute-start | bytes 786440 | tf_op jit(solution)/shard_map/ppermute | solution.py:348
  48.4 2.7 %collective-permute-start.12 = (bf16[64,2048]{1,0:T(8,128)(2,1)S(1)}, bf16[64,2048]{1,0:T(8,128)(2,1)S(1)}, u32[]{:S(2)}, u32[]{:S(2)}) collective-permute-start(bf16[64,2048]{1,0:T(8,128)(2,1)S(1)} %get-tuple-element.73), channel_id=1, source_target_pairs={{0,4},{4,0},{8,12},{12,8},{16,20},{20,16},{24,28},{28,24},{1,5},{5... | collective-permute-start | bytes 786440 | tf_op jit(solution)/shard_map/ppermute | solution.py:348
  48.6 3.2 %collective-permute-start.15 = (bf16[64,2048]{1,0:T(8,128)(2,1)S(1)}, bf16[64,2048]{1,0:T(8,128)(2,1)S(1)}, u32[]{:S(2)}, u32[]{:S(2)}) collective-permute-start(bf16[64,2048]{1,0:T(8,128)(2,1)S(1)} %get-tuple-element.79), channel_id=1, source_target_pairs={{0,4},{4,0},{8,12},{12,8},{16,20},{20,16},{24,28},{28,24},{1,5},{5... | collective-permute-start | bytes 786440 | tf_op jit(solution)/shard_map/ppermute | solution.py:348
  49.5 6.4 %collective-permute-start.18 = (bf16[64,2048]{1,0:T(8,128)(2,1)S(1)}, bf16[64,2048]{1,0:T(8,128)(2,1)S(1)}, u32[]{:S(2)}, u32[]{:S(2)}) collective-permute-start(bf16[64,2048]{1,0:T(8,128)(2,1)S(1)} %add.9), channel_id=1, source_target_pairs={{0,16},{4,12},{8,24},{12,4},{16,0},{20,28},{24,8},{28,20},{1,17},{... | collective-permute-start | bytes 786440 | tf_op jit(solution)/shard_map/ppermute | solution.py:343
  51.2 8.3 %collective-permute-start.14 = (bf16[64,2048]{1,0:T(8,128)(2,1)S(1)}, bf16[64,2048]{1,0:T(8,128)(2,1)S(1)}, u32[]{:S(2)}, u32[]{:S(2)}) collective-permute-start(bf16[64,2048]{1,0:T(8,128)(2,1)S(1)} %add.6), channel_id=1, source_target_pairs={{0,16},{4,12},{8,24},{12,4},{16,0},{20,28},{24,8},{28,20},{1,17},{... | collective-permute-start | bytes 786440 | tf_op jit(solution)/shard_map/ppermute | solution.py:343
  56.0 6.4 %collective-permute-start.19 = (bf16[64,2048]{1,0:T(8,128)(2,1)S(1)}, bf16[64,2048]{1,0:T(8,128)(2,1)S(1)}, u32[]{:S(2)}, u32[]{:S(2)}) collective-permute-start(bf16[64,2048]{1,0:T(8,128)(2,1)S(1)} %add.10), channel_id=1, source_target_pairs={{0,8},{4,20},{8,0},{12,28},{16,24},{20,4},{24,16},{28,12},{1,9},{5... | collective-permute-start | bytes 786440 | tf_op jit(solution)/shard_map/ppermute | solution.py:343
  62.5 6.7 %collective-permute-start.20 = (bf16[16,2048]{1,0:T(8,128)(2,1)S(1)}, bf16[16,2048]{1,0:T(8,128)(2,1)S(1)}, u32[]{:S(2)}, u32[]{:S(2)}) collective-permute-start(bf16[16,2048]{1,0:T(8,128)(2,1)S(1)} %get-tuple-element.84), channel_id=1, source_target_pairs={{0,1},{1,2},{2,3},{3,0},{4,5},{5,6},{6,7},{7,4},{8,9},{9,10},{10,1... | collective-permute-start | bytes 196616 | tf_op jit(solution)/shard_map/ppermute | solution.py:340
  64.1 7.0 %collective-permute-start.21 = (bf16[16,2048]{1,0:T(8,128)(2,1)S(1)}, bf16[16,2048]{1,0:T(8,128)(2,1)S(1)}, u32[]{:S(2)}, u32[]{:S(2)}) collective-permute-start(bf16[16,2048]{1,0:T(8,128)(2,1)S(1)} %get-tuple-element.85), channel_id=1, source_target_pairs={{0,2},{1,3},{2,0},{3,1},{4,6},{5,7},{6,4},{7,5},{8,10},{9,11},{10,... | collective-permute-start | bytes 196616 | tf_op jit(solution)/shard_map/ppermute | solution.py:340
  65.5 5.6 %collective-permute-start.22 = (bf16[16,2048]{1,0:T(8,128)(2,1)S(1)}, bf16[16,2048]{1,0:T(8,128)(2,1)S(1)}, u32[]{:S(2)}, u32[]{:S(2)}) collective-permute-start(bf16[16,2048]{1,0:T(8,128)(2,1)S(1)} %get-tuple-element.86), channel_id=1, source_target_pairs={{0,3},{1,0},{2,1},{3,2},{4,7},{5,4},{6,5},{7,6},{8,11},{9,8},{10,9... | collective-permute-start | bytes 196616 | tf_op jit(solution)/shard_map/ppermute | solution.py:340

commit v4 on v3

--- a/solution.py
+++ b/solution.py
@@ -42,11 +42,13 @@
         )
     ]
     large = pltpu.make_async_copy(weight_hbm, weight, weight_sems.at[0])
-    for copy in small:
+    for copy in small[:2]:
         copy.start()
-    for r in range(requests):
+    for r in range(requests // 2):
         pltpu.make_async_copy(states_hbm.at[r], state.at[r], state_sems.at[r]).start()
-    for copy in small:
+    for copy in small[2:]:
+        copy.start()
+    for copy in small[:2]:
         copy.wait()
 
     unit_q, unit_k = {}, {}
@@ -65,6 +67,14 @@
 
     def read_states(r, carry):
         pltpu.make_async_copy(states_hbm.at[r], state.at[r], state_sems.at[r]).wait()
+
+        @pl.when(r < requests // 2)
+        def _():
+            after = r + requests // 2
+            pltpu.make_async_copy(
+                states_hbm.at[after], state.at[after], state_sems.at[after]
+            ).start()
+
         both = pl.ds(pl.multiple_of(r * 2 * vectors, 2 * vectors), 2 * vectors)
         at = pl.ds(pl.multiple_of(r * vectors, vectors), vectors)
         for g in range(pairs):
@@ -76,10 +86,13 @@
                 reads[g * repeat + i, at, :] = read[:, i * HV : (i + 1) * HV]
         return carry
 
-    lax.fori_loop(0, requests // 2, read_states, 0)
+    early = requests * 3 // 4
+    lax.fori_loop(0, early, read_states, 0)
     large.start()
-    lax.fori_loop(requests // 2, requests, read_states, 0)
-
+    lax.fori_loop(early, requests, read_states, 0)
+
+    for copy in small[2:]:
+        copy.wait()
     betas = jax.nn.sigmoid(beta_ref[...].reshape(steps * heads, requests).T)
     decays = decay_ref[...].reshape(steps * heads, requests).T
     for g in range(pairs):
@@ -397,30 +410,40 @@
             scratch=[pltpu.VMEM((sum(x.shape[0] for x, _, _, _ in pieces), columns), jnp.bfloat16)],
         )
 
-    first = join(normed, *[along(normed, ring - k) for k in range(1, ring)])
+    blocks = [normed] + [along(normed, ring - k) for k in range(1, ring)]
+    firsts = [join(*blocks[: ring // 2]), join(*blocks[ring // 2 :])]
+    first = join(*firsts)
     held = first.shape[0]
     last = (1 << bits) - 1
-    sets, served, totals = {0: first}, {}, {}
+    sets, parts, served, totals = {0: first}, {0: firsts}, {}, {}
+
+    def serve(m, peers):
+        served[m] = experts((sets[m], jnp.float32, 0, m * held), (peers, jnp.bfloat16, 1, m * held))
+
     later = first
-    for depth in range(bits + 1):
-        group = [m for m in range(last + 1) if m.bit_count() == depth]
-        for m in group:
-            if m:
-                j = m.bit_length() - 1
-                sets[m] = across(later if m == 1 << j and j else sets[m - (1 << j)], j)
-        if depth:
-            before = [m for m in served if m.bit_count() == depth - 1]
-            done, got = lax.optimization_barrier(
-                ([served[m] for m in before], [sets[m] for m in group])
-            )
-            served.update(zip(before, done))
-            sets.update(zip(group, got))
-        for m in group:
-            served[m] = experts(
-                (sets[m], jnp.float32, 0, m * held), (other(sets[m]), jnp.bfloat16, 1, m * held)
-            )
-        if depth == 0:
-            later, served[0] = lax.optimization_barrier((first, served[0]))
+    for j in range(bits):
+        top = 1 << j
+        if j < bits - 1 or j == 0:
+            parts[top] = [across(x, j) for x in parts[0]]
+        else:
+            sets[top] = across(later, j)
+        if j == 0:
+            serve(0, other(first))
+            later, served[0], parts[1] = lax.optimization_barrier((first, served[0], parts[1]))
+            later = first
+        for m in range(1, top):
+            parts[m + top] = [across(x, j) for x in parts[m]]
+            if m not in served:
+                serve(m, other(sets[m]))
+                parts[m + top], served[m] = lax.optimization_barrier((parts[m + top], served[m]))
+        for m in range(1, 2 * top):
+            if m not in sets:
+                sets[m] = join(*parts[m])
+    for m in range(1 << (bits - 1), last + 1):
+        peers = other(sets[m])
+        if m > 1 and m - 1 in served:
+            peers, served[m - 1] = lax.optimization_barrier((peers, served[m - 1]))
+        serve(m, peers)
     for m in range(last + 1):
         leaves = m >> (bits - 1)
         totals[m] = add(

time: 71.9 us -> 69.6 us (0.968)
  Pallas kernels: 18.5 us -> 16.7 us
  waiting for transfers between devices: 28.2 us -> 27 us
    pallas_call x1, Pallas kernels: 9.89 us -> 8.03 us  [attend(): pl.pallas_call(functools.partial(attend_kernel, blocks=blocks), out_shape...]
    ppermute x6 -> x8, starting transfers between devices: 8.05 us -> 9.66 us  [across(): lax.ppermute(x, 'dev', [(i, i ^ 2 << (j + i % 2) % bits) for i in range(w...]
    ppermute x8, waiting for transfers between devices: 2.13 us -> 0.9 us  [other(): return lax.ppermute(x, 'dev', [(i, i ^ 1) for i in range(width)])]
    ppermute x6 -> x8, waiting for transfers between devices: 16.6 us -> 15.5 us  [across(): lax.ppermute(x, 'dev', [(i, i ^ 2 << (j + i % 2) % bits) for i in range(w...]
    ppermute x9, waiting for transfers between devices: 9.54 us -> 10.6 us  [along(): return lax.ppermute(x, 'head', [(i, (i + k) % ring) for i in range(ring)])]
    pallas_call x13 -> x17, Pallas kernels: 5.75 us -> 5.79 us  [local(): pl.pallas_call(kernel, out_shape=out_shape, in_specs=[pl.BlockSpec(memory...]
  transfers between devices with their start and end apart: 23 -> 25, of which waited for: 16 -> 15; matrix products, arithmetic and copies ran while one was open for 0% -> 0% of each run, Pallas kernels for 9% -> 10%
where the time goes in v4:
time: 69.6 us; the launch traced here: 69.5 us
  waiting for transfers between devices  27 us (39%)
  starting transfers between devices  25.6 us (37%)
  Pallas kernels  16.7 us (24%)
    ppermute x8, waiting for transfers between devices, across(): lax.ppermute(x, 'dev', [(i, i ^ 2 << (j + i % 2) % bits) for i in range(w...  15.5 us
    ppermute x9, starting transfers between devices, along(): return lax.ppermute(x, 'head', [(i, (i + k) % ring) for i in range(ring)])  14.6 us
    ppermute x9, waiting for transfers between devices, along(): return lax.ppermute(x, 'head', [(i, (i + k) % ring) for i in range(ring)])  10.6 us
    ppermute x8, starting transfers between devices, across(): lax.ppermute(x, 'dev', [(i, i ^ 2 << (j + i % 2) % bits) for i in range(w...  9.66 us
    pallas_call x1, Pallas kernels, attend(): pl.pallas_call(functools.partial(attend_kernel, blocks=blocks), out_shape...  8.03 us
    pallas_call x17, Pallas kernels, local(): pl.pallas_call(kernel, out_shape=out_shape, in_specs=[pl.BlockSpec(memory...  5.79 us
    pallas_call x1, Pallas kernels, load(): pl.pallas_call(load_kernel, out_shape=[jax.ShapeDtypeStruct(mat.shape[1:]...  2.88 us
  transfers between devices with their start and end apart: 25, of which 15 were waited for; matrix products, arithmetic and copies ran while one was open for 0% of the time, Pallas kernels for 10%

profile of v4, /device:TPU:0, one launch (start us, length us, event | category | flops | bytes accessed | tf_op | source)
XLA Modules:
  0.0 69.5 jit_solution(3858255941641657970)
XLA Ops:
  0.0 8.0 %attend.1 = (f32[16,2048]{1,0:T(8,128)S(1)}, bf16[16,2048]{1,0:T(8,128)(2,1)S(1)}, bf16[16,2048]{1,0:T(8,128)(2,1)S(1)}, bf16[16,2048]{1,0:T(8,128)(2,1)S(1)}) custom-call(s32[1]{0:T(128)} %bitcast.place, s32[1]{0:T(128)} %bitcast.1.spot, bf16[4,16,512]{2,1,0:T(8,128)(2,1)} %refs_0_.2, bf16[4,16,512]{2,1,0:T(8,128)(2,1)} %refs_1_.2, ...), custom_call_target="tpu_custom_call" | custom-call | tf_op jit(solution)/shard_map/attend/pallas_call | solution.py:162
  8.0 3.1 %collective-permute-start = (bf16[16,2048]{1,0:T(8,128)(2,1)S(1)}, bf16[16,2048]{1,0:T(8,128)(2,1)S(1)}, u32[]{:S(2)}, u32[]{:S(2)}) collective-permute-start(bf16[16,2048]{1,0:T(8,128)(2,1)S(1)} %get-tuple-element.49), channel_id=1, source_target_pairs={{0,1},{1,2},{2,3},{3,0},{4,5},{5,6},{6,7},{7,4},{8,9},{9,10},{10,1... | collective-permute-start | bytes 196616 | tf_op jit(solution)/shard_map/ppermute | solution.py:353
  11.1 2.6 %collective-permute-start.1 = (bf16[16,2048]{1,0:T(8,128)(2,1)S(1)}, bf16[16,2048]{1,0:T(8,128)(2,1)S(1)}, u32[]{:S(2)}, u32[]{:S(2)}) collective-permute-start(bf16[16,2048]{1,0:T(8,128)(2,1)S(1)} %get-tuple-element.50), channel_id=1, source_target_pairs={{0,2},{1,3},{2,0},{3,1},{4,6},{5,7},{6,4},{7,5},{8,10},{9,11},{10,... | collective-permute-start | bytes 196616 | tf_op jit(solution)/shard_map/ppermute | solution.py:353
  13.7 1.4 %collective-permute-start.2 = (bf16[16,2048]{1,0:T(8,128)(2,1)S(1)}, bf16[16,2048]{1,0:T(8,128)(2,1)S(1)}, u32[]{:S(2)}, u32[]{:S(2)}) collective-permute-start(bf16[16,2048]{1,0:T(8,128)(2,1)S(1)} %get-tuple-element.51), channel_id=1, source_target_pairs={{0,3},{1,0},{2,1},{3,2},{4,7},{5,4},{6,5},{7,6},{8,11},{9,8},{10,9... | collective-permute-start | bytes 196616 | tf_op jit(solution)/shard_map/ppermute | solution.py:353
  15.1 2.9 %load.1 = (bf16[2048,512]{1,0:T(8,128)(2,1)S(1)}, bf16[2048,512]{1,0:T(8,128)(2,1)S(1)}, bf16[512,2048]{1,0:T(8,128)(2,1)S(1)}) custom-call(bf16[1,2048,512]{2,1,0:T(8,128)(2,1)} %refs_0_.3, bf16[1,2048,512]{2,1,0:T(8,128)(2,1)} %refs_1_.3, bf16[1,512,2048]{2,1,0:T(8,128)(2,1)} %refs_2_.3), custom_call_target="tpu_custom_call" | custom-call | tf_op jit(solution)/shard_map/load/pallas_call | solution.py:225
  18.0 0.2 collective-permute-done.1.rest_1_
  18.2 0.3 collective-permute-done.2.rest_2_
  18.5 0.2 norm.1
  18.7 3.0 %collective-permute-start.3 = (bf16[16,2048]{1,0:T(8,128)(2,1)S(1)}, bf16[16,2048]{1,0:T(8,128)(2,1)S(1)}, u32[]{:S(2)}, u32[]{:S(2)}) collective-permute-start(bf16[16,2048]{1,0:T(8,128)(2,1)S(1)} %get-tuple-element.59.refs_0_), channel_id=1, source_target_pairs={{0,3},{1,0},{2,1},{3,2},{4,7},{5,4},{6,5},{7,6},{8,11},{9,8},{10,9... | collective-permute-start | bytes 196616 | tf_op jit(solution)/shard_map/ppermute | solution.py:353
  21.7 0.6 collective-permute-start.4
  22.3 1.3 %collective-permute-done.3.refs_1_ = bf16[16,2048]{1,0:T(8,128)(2,1)S(1)} collective-permute-done((bf16[16,2048]{1,0:T(8,128)(2,1)S(1)}, bf16[16,2048]{1,0:T(8,128)(2,1)S(1)}, u32[]{:S(2)}, u32[]{:S(2)}) %collective-permute-start.3) | collective-permute-done | bytes 65568 | tf_op jit(solution)/shard_map/ppermute | solution.py:353
  23.6 4.1 %collective-permute-done.5.refs_1_ = bf16[16,2048]{1,0:T(8,128)(2,1)S(1)} collective-permute-done((bf16[16,2048]{1,0:T(8,128)(2,1)S(1)}, bf16[16,2048]{1,0:T(8,128)(2,1)S(1)}, u32[]{:S(2)}, u32[]{:S(2)}) %collective-permute-start.5) | collective-permute-done | bytes 65568 | tf_op jit(solution)/shard_map/ppermute | solution.py:353
  27.8 0.1 collective-permute-start.6
  27.9 1.6 %collective-permute-start.7 = (bf16[32,2048]{1,0:T(8,128)(2,1)S(1)}, bf16[32,2048]{1,0:T(8,128)(2,1)S(1)}, u32[]{:S(2)}, u32[]{:S(2)}) collective-permute-start(bf16[32,2048]{1,0:T(8,128)(2,1)S(1)} %join.5.refs_0_), channel_id=1, source_target_pairs={{0,8},{4,20},{8,0},{12,28},{16,24},{20,4},{24,16},{28,12},{1,9},{5... | collective-permute-start | bytes 393224 | tf_op jit(solution)/shard_map/ppermute | solution.py:356
  29.4 0.5 collective-permute-start.8
  30.0 1.5 %collective-permute-start.13 = (bf16[64,2048]{1,0:T(8,128)(2,1)S(1)}, bf16[64,2048]{1,0:T(8,128)(2,1)S(1)}, u32[]{:S(2)}, u32[]{:S(2)}) collective-permute-start(bf16[64,2048]{1,0:T(8,128)(2,1)S(1)} %join.7.refs_0_), channel_id=1, source_target_pairs={{0,16},{4,12},{8,24},{12,4},{16,0},{20,28},{24,8},{28,20},{1,17},{... | collective-permute-start | bytes 786440 | tf_op jit(solution)/shard_map/ppermute | solution.py:356
  31.5 1.1 %experts.4 = (f32[64,2048]{1,0:T(8,128)S(1)}, bf16[64,2048]{1,0:T(8,128)(2,1)S(1)}) custom-call(s32[1]{0:T(128)} %bitcast.place, s32[1]{0:T(128)} %bitcast.1.spot, s32[10,4,128]{2,1,0:T(4,128)S(1)} %bitcast.8, f32[10,4,128]{2,1,0:T(4,128)S(1)} %bitcast.12, bf16[2048,512]{1,0:T(8,128)(2,1)S(1)} %get-tuple-element.60.gate, ...), custom_call_target="tpu_custom_call" | custom-call | tf_op jit(solution)/shard_map/experts/pallas_call | solution.py:187
  32.6 0.7 %collective-permute-done.7.refs_0_ = bf16[32,2048]{1,0:T(8,128)(2,1)S(1)} collective-permute-done((bf16[32,2048]{1,0:T(8,128)(2,1)S(1)}, bf16[32,2048]{1,0:T(8,128)(2,1)S(1)}, u32[]{:S(2)}, u32[]{:S(2)}) %collective-permute-start.7) | collective-permute-done | bytes 131104 | tf_op jit(solution)/shard_map/ppermute | solution.py:356
  33.4 2.8 %collective-permute-done.8.refs_1_ = bf16[32,2048]{1,0:T(8,128)(2,1)S(1)} collective-permute-done((bf16[32,2048]{1,0:T(8,128)(2,1)S(1)}, bf16[32,2048]{1,0:T(8,128)(2,1)S(1)}, u32[]{:S(2)}, u32[]{:S(2)}) %collective-permute-start.8) | collective-permute-done | bytes 131104 | tf_op jit(solution)/shard_map/ppermute | solution.py:356
  36.2 0.1 collective-permute-start.11
  36.3 1.6 %collective-permute-start.9 = (bf16[32,2048]{1,0:T(8,128)(2,1)S(1)}, bf16[32,2048]{1,0:T(8,128)(2,1)S(1)}, u32[]{:S(2)}, u32[]{:S(2)}) collective-permute-start(bf16[32,2048]{1,0:T(8,128)(2,1)S(1)} %collective-permute-done.7.refs_0_), channel_id=1, source_target_pairs={{0,16},{4,12},{8,24},{12,4},{16,0},{20,28},{24,8},{28,20},{1,17},{... | collective-permute-start | bytes 393224 | tf_op jit(solution)/shard_map/ppermute | solution.py:356
  37.9 0.5 collective-permute-start.10
  38.4 1.1 %experts.5 = (f32[64,2048]{1,0:T(8,128)S(1)}, bf16[64,2048]{1,0:T(8,128)(2,1)S(1)}) custom-call(s32[1]{0:T(128)} %bitcast.place, s32[1]{0:T(128)} %bitcast.1.spot, s32[10,4,128]{2,1,0:T(4,128)S(1)} %bitcast.9, f32[10,4,128]{2,1,0:T(4,128)S(1)} %bitcast.13, bf16[2048,512]{1,0:T(8,128)(2,1)S(1)} %get-tuple-element.60.gate, ...), custom_call_target="tpu_custom_call" | custom-call | tf_op jit(solution)/shard_map/experts/pallas_call | solution.py:187
  39.5 1.8 %collective-permute-done.9.refs_0_ = bf16[32,2048]{1,0:T(8,128)(2,1)S(1)} collective-permute-done((bf16[32,2048]{1,0:T(8,128)(2,1)S(1)}, bf16[32,2048]{1,0:T(8,128)(2,1)S(1)}, u32[]{:S(2)}, u32[]{:S(2)}) %collective-permute-start.9) | collective-permute-done | bytes 131104 | tf_op jit(solution)/shard_map/ppermute | solution.py:356
  41.3 1.5 %collective-permute-done.10.refs_1_ = bf16[32,2048]{1,0:T(8,128)(2,1)S(1)} collective-permute-done((bf16[32,2048]{1,0:T(8,128)(2,1)S(1)}, bf16[32,2048]{1,0:T(8,128)(2,1)S(1)}, u32[]{:S(2)}, u32[]{:S(2)}) %collective-permute-start.10) | collective-permute-done | bytes 131104 | tf_op jit(solution)/shard_map/ppermute | solution.py:356
  42.9 0.1 collective-permute-start.12
  42.9 1.1 %experts.6 = (f32[64,2048]{1,0:T(8,128)S(1)}, bf16[64,2048]{1,0:T(8,128)(2,1)S(1)}) custom-call(s32[1]{0:T(128)} %bitcast.place, s32[1]{0:T(128)} %bitcast.1.spot, s32[10,4,128]{2,1,0:T(4,128)S(1)} %bitcast.10, f32[10,4,128]{2,1,0:T(4,128)S(1)} %bitcast.14, bf16[2048,512]{1,0:T(8,128)(2,1)S(1)} %get-tuple-element.60.gate, ...), custom_call_target="tpu_custom_call" | custom-call | tf_op jit(solution)/shard_map/experts/pallas_call | solution.py:187
  44.1 0.4 collective-permute-done.12.refs_1_
  44.5 1.1 %experts.7 = (f32[64,2048]{1,0:T(8,128)S(1)}, bf16[64,2048]{1,0:T(8,128)(2,1)S(1)}) custom-call(s32[1]{0:T(128)} %bitcast.place, s32[1]{0:T(128)} %bitcast.1.spot, s32[10,4,128]{2,1,0:T(4,128)S(1)} %bitcast.11, f32[10,4,128]{2,1,0:T(4,128)S(1)} %bitcast.15, bf16[2048,512]{1,0:T(8,128)(2,1)S(1)} %get-tuple-element.60.gate, ...), custom_call_target="tpu_custom_call" | custom-call | tf_op jit(solution)/shard_map/experts/pallas_call | solution.py:187
  45.6 0.2 collective-permute-start.19
  45.8 0.4 collective-permute-start.16
  46.2 0.1 collective-permute-start.18
  46.3 0.4 collective-permute-start.15
  46.7 0.5 collective-permute-done.19.refs_1_
  47.2 1.5 %collective-permute-start.20 = (bf16[64,2048]{1,0:T(8,128)(2,1)S(1)}, bf16[64,2048]{1,0:T(8,128)(2,1)S(1)}, u32[]{:S(2)}, u32[]{:S(2)}) collective-permute-start(bf16[64,2048]{1,0:T(8,128)(2,1)S(1)} %add.9), channel_id=1, source_target_pairs={{0,16},{4,12},{8,24},{12,4},{16,0},{20,28},{24,8},{28,20},{1,17},{... | collective-permute-start | bytes 786440 | tf_op jit(solution)/shard_map/ppermute | solution.py:356
  48.8 0.1 add.8.refs_0_
  48.9 0.9 %collective-permute-start.17 = (bf16[64,2048]{1,0:T(8,128)(2,1)S(1)}, bf16[64,2048]{1,0:T(8,128)(2,1)S(1)}, u32[]{:S(2)}, u32[]{:S(2)}) collective-permute-start(bf16[64,2048]{1,0:T(8,128)(2,1)S(1)} %add.6), channel_id=1, source_target_pairs={{0,16},{4,12},{8,24},{12,4},{16,0},{20,28},{24,8},{28,20},{1,17},{... | collective-permute-start | bytes 786440 | tf_op jit(solution)/shard_map/ppermute | solution.py:356
  49.9 3.8 %collective-permute-done.20.refs_1_ = bf16[64,2048]{1,0:T(8,128)(2,1)S(1)} collective-permute-done((bf16[64,2048]{1,0:T(8,128)(2,1)S(1)}, bf16[64,2048]{1,0:T(8,128)(2,1)S(1)}, u32[]{:S(2)}, u32[]{:S(2)}) %collective-permute-start.20) | collective-permute-done | bytes 262176 | tf_op jit(solution)/shard_map/ppermute | solution.py:356
  53.7 1.6 %collective-permute-start.21 = (bf16[64,2048]{1,0:T(8,128)(2,1)S(1)}, bf16[64,2048]{1,0:T(8,128)(2,1)S(1)}, u32[]{:S(2)}, u32[]{:S(2)}) collective-permute-start(bf16[64,2048]{1,0:T(8,128)(2,1)S(1)} %add.10), channel_id=1, source_target_pairs={{0,8},{4,20},{8,0},{12,28},{16,24},{20,4},{24,16},{28,12},{1,9},{5... | collective-permute-start | bytes 786440 | tf_op jit(solution)/shard_map/ppermute | solution.py:356
  55.3 1.9 %collective-permute-done.17.refs_1_ = bf16[64,2048]{1,0:T(8,128)(2,1)S(1)} collective-permute-done((bf16[64,2048]{1,0:T(8,128)(2,1)S(1)}, bf16[64,2048]{1,0:T(8,128)(2,1)S(1)}, u32[]{:S(2)}, u32[]{:S(2)}) %collective-permute-start.17) | collective-permute-done | bytes 262176 | tf_op jit(solution)/shard_map/ppermute | solution.py:356
  57.2 2.9 %collective-permute-done.21.refs_2_ = bf16[64,2048]{1,0:T(8,128)(2,1)S(1)} collective-permute-done((bf16[64,2048]{1,0:T(8,128)(2,1)S(1)}, bf16[64,2048]{1,0:T(8,128)(2,1)S(1)}, u32[]{:S(2)}, u32[]{:S(2)}) %collective-permute-start.21) | collective-permute-done | bytes 262176 | tf_op jit(solution)/shard_map/ppermute | solution.py:356
  60.2 0.1 add.11
  60.3 1.3 %collective-permute-start.22 = (bf16[16,2048]{1,0:T(8,128)(2,1)S(1)}, bf16[16,2048]{1,0:T(8,128)(2,1)S(1)}, u32[]{:S(2)}, u32[]{:S(2)}) collective-permute-start(bf16[16,2048]{1,0:T(8,128)(2,1)S(1)} %get-tuple-element.88), channel_id=1, source_target_pairs={{0,1},{1,2},{2,3},{3,0},{4,5},{5,6},{6,7},{7,4},{8,9},{9,10},{10,1... | collective-permute-start | bytes 196616 | tf_op jit(solution)/shard_map/ppermute | solution.py:353
  61.6 2.2 %collective-permute-start.23 = (bf16[16,2048]{1,0:T(8,128)(2,1)S(1)}, bf16[16,2048]{1,0:T(8,128)(2,1)S(1)}, u32[]{:S(2)}, u32[]{:S(2)}) collective-permute-start(bf16[16,2048]{1,0:T(8,128)(2,1)S(1)} %get-tuple-element.89), channel_id=1, source_target_pairs={{0,2},{1,3},{2,0},{3,1},{4,6},{5,7},{6,4},{7,5},{8,10},{9,11},{10,... | collective-permute-start | bytes 196616 | tf_op jit(solution)/shard_map/ppermute | solution.py:353
  63.8 0.3 collective-permute-start.24
  64.1 2.7 %collective-permute-done.22.rest_0_ = bf16[16,2048]{1,0:T(8,128)(2,1)S(1)} collective-permute-done((bf16[16,2048]{1,0:T(8,128)(2,1)S(1)}, bf16[16,2048]{1,0:T(8,128)(2,1)S(1)}, u32[]{:S(2)}, u32[]{:S(2)}) %collective-permute-start.22) | collective-permute-done | bytes 65568 | tf_op jit(solution)/shard_map/ppermute | solution.py:353
  66.9 1.9 %collective-permute-done.23.rest_1_ = bf16[16,2048]{1,0:T(8,128)(2,1)S(1)} collective-permute-done((bf16[16,2048]{1,0:T(8,128)(2,1)S(1)}, bf16[16,2048]{1,0:T(8,128)(2,1)S(1)}, u32[]{:S(2)}, u32[]{:S(2)}) %collective-permute-start.23) | collective-permute-done | bytes 65568 | tf_op jit(solution)/shard_map/ppermute | solution.py:353
  68.8 0.7 finish.1
  (29 shorter events, 0.3 us)
Async XLA Ops:
  8.0 10.0 %collective-permute-start = (bf16[16,2048]{1,0:T(8,128)(2,1)S(1)}, bf16[16,2048]{1,0:T(8,128)(2,1)S(1)}, u32[]{:S(2)}, u32[]{:S(2)}) collective-permute-start(bf16[16,2048]{1,0:T(8,128)(2,1)S(1)} %get-tuple-element.49), channel_id=1, source_target_pairs={{0,1},{1,2},{2,3},{3,0},{4,5},{5,6},{6,7},{7,4},{8,9},{9,10},{10,1... | collective-permute-start | bytes 196616 | tf_op jit(solution)/shard_map/ppermute | solution.py:353
  11.1 7.1 %collective-permute-start.1 = (bf16[16,2048]{1,0:T(8,128)(2,1)S(1)}, bf16[16,2048]{1,0:T(8,128)(2,1)S(1)}, u32[]{:S(2)}, u32[]{:S(2)}) collective-permute-start(bf16[16,2048]{1,0:T(8,128)(2,1)S(1)} %get-tuple-element.50), channel_id=1, source_target_pairs={{0,2},{1,3},{2,0},{3,1},{4,6},{5,7},{6,4},{7,5},{8,10},{9,11},{10,... | collective-permute-start | bytes 196616 | tf_op jit(solution)/shard_map/ppermute | solution.py:353
  13.7 4.8 %copy-start.2 = (bf16[4,4,2048]{2,1,0:T(4,128)(2,1)S(1)}, bf16[4,4,2048]{2,1,0:T(4,128)(2,1)}, u32[]{:S(2)}) copy-start(bf16[4,4,2048]{2,1,0:T(4,128)(2,1)} %residual_ref.1) | copy-start | bytes 196612
  13.7 4.8 %copy-start.3 = (f32[2048]{0:T(1024)S(1)}, f32[2048]{0:T(1024)}, u32[]{:S(2)}) copy-start(f32[2048]{0:T(1024)} %param.26) | copy-start | bytes 24580
  13.7 17.8 %copy-start = (s32[4,128,10]{1,0,2:T(4,128)S(1)}, s32[4,128,10]{1,0,2:T(4,128)}, u32[]{:S(2)}) copy-start(s32[4,128,10]{1,0,2:T(4,128)} %param.27) | copy-start | bytes 61444
  13.7 17.8 %copy-start.1 = (f32[4,128,10]{1,0,2:T(4,128)S(1)}, f32[4,128,10]{1,0,2:T(4,128)}, u32[]{:S(2)}) copy-start(f32[4,128,10]{1,0,2:T(4,128)} %param.28) | copy-start | bytes 61444
  13.7 4.8 %collective-permute-start.2 = (bf16[16,2048]{1,0:T(8,128)(2,1)S(1)}, bf16[16,2048]{1,0:T(8,128)(2,1)S(1)}, u32[]{:S(2)}, u32[]{:S(2)}) collective-permute-start(bf16[16,2048]{1,0:T(8,128)(2,1)S(1)} %get-tuple-element.51), channel_id=1, source_target_pairs={{0,3},{1,0},{2,1},{3,2},{4,7},{5,4},{6,5},{7,6},{8,11},{9,8},{10,9... | collective-permute-start | bytes 196616 | tf_op jit(solution)/shard_map/ppermute | solution.py:353
  18.7 4.9 %collective-permute-start.3 = (bf16[16,2048]{1,0:T(8,128)(2,1)S(1)}, bf16[16,2048]{1,0:T(8,128)(2,1)S(1)}, u32[]{:S(2)}, u32[]{:S(2)}) collective-permute-start(bf16[16,2048]{1,0:T(8,128)(2,1)S(1)} %get-tuple-element.59.refs_0_), channel_id=1, source_target_pairs={{0,3},{1,0},{2,1},{3,2},{4,7},{5,4},{6,5},{7,6},{8,11},{9,8},{10,9... | collective-permute-start | bytes 196616 | tf_op jit(solution)/shard_map/ppermute | solution.py:353
  21.7 6.1 %collective-permute-start.5 = (bf16[16,2048]{1,0:T(8,128)(2,1)S(1)}, bf16[16,2048]{1,0:T(8,128)(2,1)S(1)}, u32[]{:S(2)}, u32[]{:S(2)}) collective-permute-start(bf16[16,2048]{1,0:T(8,128)(2,1)S(1)} %get-tuple-element.59.refs_0_), channel_id=1, source_target_pairs={{0,1},{1,2},{2,3},{3,0},{4,5},{5,6},{6,7},{7,4},{8,9},{9,10},{10,1... | collective-permute-start | bytes 196616 | tf_op jit(solution)/shard_map/ppermute | solution.py:353
  21.7 6.1 %collective-permute-start.4 = (bf16[16,2048]{1,0:T(8,128)(2,1)S(1)}, bf16[16,2048]{1,0:T(8,128)(2,1)S(1)}, u32[]{:S(2)}, u32[]{:S(2)}) collective-permute-start(bf16[16,2048]{1,0:T(8,128)(2,1)S(1)} %get-tuple-element.59.refs_0_), channel_id=1, source_target_pairs={{0,2},{1,3},{2,0},{3,1},{4,6},{5,7},{6,4},{7,5},{8,10},{9,11},{10,... | collective-permute-start | bytes 196616 | tf_op jit(solution)/shard_map/ppermute | solution.py:353
  27.8 3.7 %collective-permute-start.6 = (bf16[64,2048]{1,0:T(8,128)(2,1)S(1)}, bf16[64,2048]{1,0:T(8,128)(2,1)S(1)}, u32[]{:S(2)}, u32[]{:S(2)}) collective-permute-start(bf16[64,2048]{1,0:T(8,128)(2,1)S(1)} %join.7.refs_0_), channel_id=1, source_target_pairs={{0,4},{4,0},{8,12},{12,8},{16,20},{20,16},{24,28},{28,24},{1,5},{5... | collective-permute-start | bytes 786440 | tf_op jit(solution)/shard_map/ppermute | solution.py:361
  27.9 5.5 %collective-permute-start.7 = (bf16[32,2048]{1,0:T(8,128)(2,1)S(1)}, bf16[32,2048]{1,0:T(8,128)(2,1)S(1)}, u32[]{:S(2)}, u32[]{:S(2)}) collective-permute-start(bf16[32,2048]{1,0:T(8,128)(2,1)S(1)} %join.5.refs_0_), channel_id=1, source_target_pairs={{0,8},{4,20},{8,0},{12,28},{16,24},{20,4},{24,16},{28,12},{1,9},{5... | collective-permute-start | bytes 393224 | tf_op jit(solution)/shard_map/ppermute | solution.py:356
  29.4 6.7 %collective-permute-start.8 = (bf16[32,2048]{1,0:T(8,128)(2,1)S(1)}, bf16[32,2048]{1,0:T(8,128)(2,1)S(1)}, u32[]{:S(2)}, u32[]{:S(2)}) collective-permute-start(bf16[32,2048]{1,0:T(8,128)(2,1)S(1)} %join.6.refs_1_), channel_id=1, source_target_pairs={{0,8},{4,20},{8,0},{12,28},{16,24},{20,4},{24,16},{28,12},{1,9},{5... | collective-permute-start | bytes 393224 | tf_op jit(solution)/shard_map/ppermute | solution.py:356
  30.0 8.4 %collective-permute-start.13 = (bf16[64,2048]{1,0:T(8,128)(2,1)S(1)}, bf16[64,2048]{1,0:T(8,128)(2,1)S(1)}, u32[]{:S(2)}, u32[]{:S(2)}) collective-permute-start(bf16[64,2048]{1,0:T(8,128)(2,1)S(1)} %join.7.refs_0_), channel_id=1, source_target_pairs={{0,16},{4,12},{8,24},{12,4},{16,0},{20,28},{24,8},{28,20},{1,17},{... | collective-permute-start | bytes 786440 | tf_op jit(solution)/shard_map/ppermute | solution.py:356
  36.2 2.2 %collective-permute-start.11 = (bf16[64,2048]{1,0:T(8,128)(2,1)S(1)}, bf16[64,2048]{1,0:T(8,128)(2,1)S(1)}, u32[]{:S(2)}, u32[]{:S(2)}) collective-permute-start(bf16[64,2048]{1,0:T(8,128)(2,1)S(1)} %join.8.refs_0_), channel_id=1, source_target_pairs={{0,4},{4,0},{8,12},{12,8},{16,20},{20,16},{24,28},{28,24},{1,5},{5... | collective-permute-start | bytes 786440 | tf_op jit(solution)/shard_map/ppermute | solution.py:361
  36.3 5.0 %collective-permute-start.9 = (bf16[32,2048]{1,0:T(8,128)(2,1)S(1)}, bf16[32,2048]{1,0:T(8,128)(2,1)S(1)}, u32[]{:S(2)}, u32[]{:S(2)}) collective-permute-start(bf16[32,2048]{1,0:T(8,128)(2,1)S(1)} %collective-permute-done.7.refs_0_), channel_id=1, source_target_pairs={{0,16},{4,12},{8,24},{12,4},{16,0},{20,28},{24,8},{28,20},{1,17},{... | collective-permute-start | bytes 393224 | tf_op jit(solution)/shard_map/ppermute | solution.py:356
  37.9 5.0 %collective-permute-start.10 = (bf16[32,2048]{1,0:T(8,128)(2,1)S(1)}, bf16[32,2048]{1,0:T(8,128)(2,1)S(1)}, u32[]{:S(2)}, u32[]{:S(2)}) collective-permute-start(bf16[32,2048]{1,0:T(8,128)(2,1)S(1)} %collective-permute-done.8.refs_1_), channel_id=1, source_target_pairs={{0,16},{4,12},{8,24},{12,4},{16,0},{20,28},{24,8},{28,20},{1,17},{... | collective-permute-start | bytes 393224 | tf_op jit(solution)/shard_map/ppermute | solution.py:356
  38.4 4.6 %collective-permute-start.14 = (bf16[64,2048]{1,0:T(8,128)(2,1)S(1)}, bf16[64,2048]{1,0:T(8,128)(2,1)S(1)}, u32[]{:S(2)}, u32[]{:S(2)}) collective-permute-start(bf16[64,2048]{1,0:T(8,128)(2,1)S(1)} %collective-permute-done.13.refs_0_), channel_id=1, source_target_pairs={{0,4},{4,0},{8,12},{12,8},{16,20},{20,16},{24,28},{28,24},{1,5},{5... | collective-permute-start | bytes 786440 | tf_op jit(solution)/shard_map/ppermute | solution.py:361
  42.9 1.6 %collective-permute-start.12 = (bf16[64,2048]{1,0:T(8,128)(2,1)S(1)}, bf16[64,2048]{1,0:T(8,128)(2,1)S(1)}, u32[]{:S(2)}, u32[]{:S(2)}) collective-permute-start(bf16[64,2048]{1,0:T(8,128)(2,1)S(1)} %join.9.refs_0_), channel_id=1, source_target_pairs={{0,4},{4,0},{8,12},{12,8},{16,20},{20,16},{24,28},{28,24},{1,5},{5... | collective-permute-start | bytes 786440 | tf_op jit(solution)/shard_map/ppermute | solution.py:361
  45.6 1.6 %collective-permute-start.19 = (bf16[64,2048]{1,0:T(8,128)(2,1)S(1)}, bf16[64,2048]{1,0:T(8,128)(2,1)S(1)}, u32[]{:S(2)}, u32[]{:S(2)}) collective-permute-start(bf16[64,2048]{1,0:T(8,128)(2,1)S(1)} %get-tuple-element.86), channel_id=1, source_target_pairs={{0,4},{4,0},{8,12},{12,8},{16,20},{20,16},{24,28},{28,24},{1,5},{5... | collective-permute-start | bytes 786440 | tf_op jit(solution)/shard_map/ppermute | solution.py:361
  45.8 2.9 %collective-permute-start.16 = (bf16[64,2048]{1,0:T(8,128)(2,1)S(1)}, bf16[64,2048]{1,0:T(8,128)(2,1)S(1)}, u32[]{:S(2)}, u32[]{:S(2)}) collective-permute-start(bf16[64,2048]{1,0:T(8,128)(2,1)S(1)} %get-tuple-element.79), channel_id=1, source_target_pairs={{0,4},{4,0},{8,12},{12,8},{16,20},{20,16},{24,28},{28,24},{1,5},{5... | collective-permute-start | bytes 786440 | tf_op jit(solution)/shard_map/ppermute | solution.py:361
  46.2 2.6 %collective-permute-start.18 = (bf16[64,2048]{1,0:T(8,128)(2,1)S(1)}, bf16[64,2048]{1,0:T(8,128)(2,1)S(1)}, u32[]{:S(2)}, u32[]{:S(2)}) collective-permute-start(bf16[64,2048]{1,0:T(8,128)(2,1)S(1)} %get-tuple-element.83), channel_id=1, source_target_pairs={{0,4},{4,0},{8,12},{12,8},{16,20},{20,16},{24,28},{28,24},{1,5},{5... | collective-permute-start | bytes 786440 | tf_op jit(solution)/shard_map/ppermute | solution.py:361
  46.3 2.6 %collective-permute-start.15 = (bf16[64,2048]{1,0:T(8,128)(2,1)S(1)}, bf16[64,2048]{1,0:T(8,128)(2,1)S(1)}, u32[]{:S(2)}, u32[]{:S(2)}) collective-permute-start(bf16[64,2048]{1,0:T(8,128)(2,1)S(1)} %get-tuple-element.77), channel_id=1, source_target_pairs={{0,4},{4,0},{8,12},{12,8},{16,20},{20,16},{24,28},{28,24},{1,5},{5... | collective-permute-start | bytes 786440 | tf_op jit(solution)/shard_map/ppermute | solution.py:361
  47.2 6.4 %collective-permute-start.20 = (bf16[64,2048]{1,0:T(8,128)(2,1)S(1)}, bf16[64,2048]{1,0:T(8,128)(2,1)S(1)}, u32[]{:S(2)}, u32[]{:S(2)}) collective-permute-start(bf16[64,2048]{1,0:T(8,128)(2,1)S(1)} %add.9), channel_id=1, source_target_pairs={{0,16},{4,12},{8,24},{12,4},{16,0},{20,28},{24,8},{28,20},{1,17},{... | collective-permute-start | bytes 786440 | tf_op jit(solution)/shard_map/ppermute | solution.py:356
  48.9 8.3 %collective-permute-start.17 = (bf16[64,2048]{1,0:T(8,128)(2,1)S(1)}, bf16[64,2048]{1,0:T(8,128)(2,1)S(1)}, u32[]{:S(2)}, u32[]{:S(2)}) collective-permute-start(bf16[64,2048]{1,0:T(8,128)(2,1)S(1)} %add.6), channel_id=1, source_target_pairs={{0,16},{4,12},{8,24},{12,4},{16,0},{20,28},{24,8},{28,20},{1,17},{... | collective-permute-start | bytes 786440 | tf_op jit(solution)/shard_map/ppermute | solution.py:356
  53.7 6.4 %collective-permute-start.21 = (bf16[64,2048]{1,0:T(8,128)(2,1)S(1)}, bf16[64,2048]{1,0:T(8,128)(2,1)S(1)}, u32[]{:S(2)}, u32[]{:S(2)}) collective-permute-start(bf16[64,2048]{1,0:T(8,128)(2,1)S(1)} %add.10), channel_id=1, source_target_pairs={{0,8},{4,20},{8,0},{12,28},{16,24},{20,4},{24,16},{28,12},{1,9},{5... | collective-permute-start | bytes 786440 | tf_op jit(solution)/shard_map/ppermute | solution.py:356
  60.3 6.6 %collective-permute-start.22 = (bf16[16,2048]{1,0:T(8,128)(2,1)S(1)}, bf16[16,2048]{1,0:T(8,128)(2,1)S(1)}, u32[]{:S(2)}, u32[]{:S(2)}) collective-permute-start(bf16[16,2048]{1,0:T(8,128)(2,1)S(1)} %get-tuple-element.88), channel_id=1, source_target_pairs={{0,1},{1,2},{2,3},{3,0},{4,5},{5,6},{6,7},{7,4},{8,9},{9,10},{10,1... | collective-permute-start | bytes 196616 | tf_op jit(solution)/shard_map/ppermute | solution.py:353
  61.6 7.2 %collective-permute-start.23 = (bf16[16,2048]{1,0:T(8,128)(2,1)S(1)}, bf16[16,2048]{1,0:T(8,128)(2,1)S(1)}, u32[]{:S(2)}, u32[]{:S(2)}) collective-permute-start(bf16[16,2048]{1,0:T(8,128)(2,1)S(1)} %get-tuple-element.89), channel_id=1, source_target_pairs={{0,2},{1,3},{2,0},{3,1},{4,6},{5,7},{6,4},{7,5},{8,10},{9,11},{10,... | collective-permute-start | bytes 196616 | tf_op jit(solution)/shard_map/ppermute | solution.py:353
  63.8 5.0 %collective-permute-start.24 = (bf16[16,2048]{1,0:T(8,128)(2,1)S(1)}, bf16[16,2048]{1,0:T(8,128)(2,1)S(1)}, u32[]{:S(2)}, u32[]{:S(2)}) collective-permute-start(bf16[16,2048]{1,0:T(8,128)(2,1)S(1)} %get-tuple-element.90), channel_id=1, source_target_pairs={{0,3},{1,0},{2,1},{3,2},{4,7},{5,4},{6,5},{7,6},{8,11},{9,8},{10,9... | collective-permute-start | bytes 196616 | tf_op jit(solution)/shard_map/ppermute | solution.py:353

commit v5 on v4

--- a/solution.py
+++ b/solution.py
@@ -10,6 +10,7 @@
 HK = 128
 HV = 128
 EPS = 1e-06
+AHEAD = 3
 
 
 def attend_kernel(place, spot, *refs, blocks):
@@ -44,9 +45,18 @@
     large = pltpu.make_async_copy(weight_hbm, weight, weight_sems.at[0])
     for copy in small[:2]:
         copy.start()
-    for r in range(requests // 2):
-        pltpu.make_async_copy(states_hbm.at[r], state.at[r], state_sems.at[r]).start()
+    parts = [
+        pltpu.make_async_copy(
+            states_hbm.at[:, pl.ds(g * repeat, repeat)],
+            state.at[:, pl.ds(g * repeat, repeat)],
+            state_sems.at[g],
+        )
+        for g in range(pairs)
+    ]
+    parts[0].start()
     for copy in small[2:]:
+        copy.start()
+    for copy in parts[1:AHEAD]:
         copy.start()
     for copy in small[:2]:
         copy.wait()
@@ -65,37 +75,28 @@
                 rows[g, pl.ds(vectors + i, requests, stride=2 * vectors), :] = value - high
             unit_q[g, t], unit_k[g, t] = q, k
 
-    def read_states(r, carry):
-        pltpu.make_async_copy(states_hbm.at[r], state.at[r], state_sems.at[r]).wait()
-
-        @pl.when(r < requests // 2)
-        def _():
-            after = r + requests // 2
-            pltpu.make_async_copy(
-                states_hbm.at[after], state.at[after], state_sems.at[after]
-            ).start()
-
+    def read_states(g, r, carry):
         both = pl.ds(pl.multiple_of(r * 2 * vectors, 2 * vectors), 2 * vectors)
         at = pl.ds(pl.multiple_of(r * vectors, vectors), vectors)
-        for g in range(pairs):
-            left = rows[g, both, :].astype(jnp.bfloat16)
-            right = [state[r, g * repeat + i].astype(jnp.bfloat16) for i in range(repeat)]
-            read = jnp.dot(left, jnp.concatenate(right, axis=1), preferred_element_type=jnp.float32)
-            read = read[:vectors] + read[vectors:]
-            for i in range(repeat):
-                reads[g * repeat + i, at, :] = read[:, i * HV : (i + 1) * HV]
+        left = rows[g, both, :].astype(jnp.bfloat16)
+        right = [state[r, g * repeat + i].astype(jnp.bfloat16) for i in range(repeat)]
+        read = jnp.dot(left, jnp.concatenate(right, axis=1), preferred_element_type=jnp.float32)
+        read = read[:vectors] + read[vectors:]
+        for i in range(repeat):
+            reads[g * repeat + i, at, :] = read[:, i * HV : (i + 1) * HV]
         return carry
-
-    early = requests * 3 // 4
-    lax.fori_loop(0, early, read_states, 0)
-    large.start()
-    lax.fori_loop(early, requests, read_states, 0)
 
     for copy in small[2:]:
         copy.wait()
     betas = jax.nn.sigmoid(beta_ref[...].reshape(steps * heads, requests).T)
     decays = decay_ref[...].reshape(steps * heads, requests).T
     for g in range(pairs):
+        parts[g].wait()
+        if g + AHEAD < pairs:
+            parts[g + AHEAD].start()
+        if g == max(pairs - AHEAD, 0):
+            large.start()
+        lax.fori_loop(0, requests, functools.partial(read_states, g), 0, unroll=True)
         kk, qk = {}, {}
         for t in range(steps):
             for s in range(t + 1):
@@ -173,7 +174,7 @@
             pltpu.VMEM((heads, requests * 2 * steps, HV), jnp.float32),
             pltpu.VMEM((steps * requests, heads * HV), jnp.bfloat16),
             pltpu.SemaphoreType.DMA((len(small),)),
-            pltpu.SemaphoreType.DMA((requests,)),
+            pltpu.SemaphoreType.DMA((pairs,)),
             pltpu.SemaphoreType.DMA((1,)),
         ],
         compiler_params=pltpu.CompilerParams(vmem_limit_bytes=32 << 20),
@@ -434,7 +435,10 @@
         for m in range(1, top):
             parts[m + top] = [across(x, j) for x in parts[m]]
             if m not in served:
-                serve(m, other(sets[m]))
+                peers = other(sets[m])
+                if top in sets:
+                    peers, sets[top] = lax.optimization_barrier((peers, sets[top]))
+                serve(m, peers)
                 parts[m + top], served[m] = lax.optimization_barrier((parts[m + top], served[m]))
         for m in range(1, 2 * top):
             if m not in sets:

time: 69.6 us -> 67.2 us (0.966)
  Pallas kernels: 16.7 us -> 14.8 us
    pallas_call x1, Pallas kernels: 8.03 us -> 6.14 us  [attend(): pl.pallas_call(functools.partial(attend_kernel, blocks=blocks), out_shape...]
where the time goes in v5:
time: 67.2 us; the launch traced here: 67.1 us
  waiting for transfers between devices  26.9 us (40%)
  starting transfers between devices  25.2 us (38%)
  Pallas kernels  14.8 us (22%)
    ppermute x8, waiting for transfers between devices, across(): lax.ppermute(x, 'dev', [(i, i ^ 2 << (j + i % 2) % bits) for i in range(w...  16 us
    ppermute x9, starting transfers between devices, along(): return lax.ppermute(x, 'head', [(i, (i + k) % ring) for i in range(ring)])  14.7 us
    ppermute x9, waiting for transfers between devices, along(): return lax.ppermute(x, 'head', [(i, (i + k) % ring) for i in range(ring)])  10 us
    ppermute x8, starting transfers between devices, across(): lax.ppermute(x, 'dev', [(i, i ^ 2 << (j + i % 2) % bits) for i in range(w...  9.06 us
    pallas_call x1, Pallas kernels, attend(): pl.pallas_call(functools.partial(attend_kernel, blocks=blocks), out_shape...  6.14 us
    pallas_call x17, Pallas kernels, local(): pl.pallas_call(kernel, out_shape=out_shape, in_specs=[pl.BlockSpec(memory...  5.79 us
    pallas_call x1, Pallas kernels, load(): pl.pallas_call(load_kernel, out_shape=[jax.ShapeDtypeStruct(mat.shape[1:]...  2.88 us
    ppermute x8, starting transfers between devices, other(): return lax.ppermute(x, 'dev', [(i, i ^ 1) for i in range(width)])  1.37 us
  transfers between devices with their start and end apart: 25, of which 15 were waited for; matrix products, arithmetic and copies ran while one was open for 0% of the time, Pallas kernels for 10%

profile of v5, /device:TPU:0, one launch (start us, length us, event | category | flops | bytes accessed | tf_op | source)
XLA Modules:
  0.0 67.1 jit_solution(15973532152983067605)
XLA Ops:
  0.0 6.1 %attend.1 = (f32[16,2048]{1,0:T(8,128)S(1)}, bf16[16,2048]{1,0:T(8,128)(2,1)S(1)}, bf16[16,2048]{1,0:T(8,128)(2,1)S(1)}, bf16[16,2048]{1,0:T(8,128)(2,1)S(1)}) custom-call(s32[1]{0:T(128)} %bitcast.place, s32[1]{0:T(128)} %bitcast.1.spot, bf16[4,16,512]{2,1,0:T(8,128)(2,1)} %refs_0_.2, bf16[4,16,512]{2,1,0:T(8,128)(2,1)} %refs_1_.2, ...), custom_call_target="tpu_custom_call" | custom-call | tf_op jit(solution)/shard_map/attend/pallas_call | solution.py:163
  6.1 3.1 %collective-permute-start = (bf16[16,2048]{1,0:T(8,128)(2,1)S(1)}, bf16[16,2048]{1,0:T(8,128)(2,1)S(1)}, u32[]{:S(2)}, u32[]{:S(2)}) collective-permute-start(bf16[16,2048]{1,0:T(8,128)(2,1)S(1)} %get-tuple-element.51), channel_id=1, source_target_pairs={{0,1},{1,2},{2,3},{3,0},{4,5},{5,6},{6,7},{7,4},{8,9},{9,10},{10,1... | collective-permute-start | bytes 196616 | tf_op jit(solution)/shard_map/ppermute | solution.py:354
  9.2 2.6 %collective-permute-start.1 = (bf16[16,2048]{1,0:T(8,128)(2,1)S(1)}, bf16[16,2048]{1,0:T(8,128)(2,1)S(1)}, u32[]{:S(2)}, u32[]{:S(2)}) collective-permute-start(bf16[16,2048]{1,0:T(8,128)(2,1)S(1)} %get-tuple-element.52), channel_id=1, source_target_pairs={{0,2},{1,3},{2,0},{3,1},{4,6},{5,7},{6,4},{7,5},{8,10},{9,11},{10,... | collective-permute-start | bytes 196616 | tf_op jit(solution)/shard_map/ppermute | solution.py:354
  11.8 1.4 %collective-permute-start.2 = (bf16[16,2048]{1,0:T(8,128)(2,1)S(1)}, bf16[16,2048]{1,0:T(8,128)(2,1)S(1)}, u32[]{:S(2)}, u32[]{:S(2)}) collective-permute-start(bf16[16,2048]{1,0:T(8,128)(2,1)S(1)} %get-tuple-element.53), channel_id=1, source_target_pairs={{0,3},{1,0},{2,1},{3,2},{4,7},{5,4},{6,5},{7,6},{8,11},{9,8},{10,9... | collective-permute-start | bytes 196616 | tf_op jit(solution)/shard_map/ppermute | solution.py:354
  13.2 2.9 %load.1 = (bf16[2048,512]{1,0:T(8,128)(2,1)S(1)}, bf16[2048,512]{1,0:T(8,128)(2,1)S(1)}, bf16[512,2048]{1,0:T(8,128)(2,1)S(1)}) custom-call(bf16[1,2048,512]{2,1,0:T(8,128)(2,1)} %refs_0_.3, bf16[1,2048,512]{2,1,0:T(8,128)(2,1)} %refs_1_.3, bf16[1,512,2048]{2,1,0:T(8,128)(2,1)} %refs_2_.3), custom_call_target="tpu_custom_call" | custom-call | tf_op jit(solution)/shard_map/load/pallas_call | solution.py:226
  16.1 0.2 collective-permute-done.1.rest_1_
  16.3 0.3 collective-permute-done.2.rest_2_
  16.6 0.2 norm.1
  16.8 3.0 %collective-permute-start.3 = (bf16[16,2048]{1,0:T(8,128)(2,1)S(1)}, bf16[16,2048]{1,0:T(8,128)(2,1)S(1)}, u32[]{:S(2)}, u32[]{:S(2)}) collective-permute-start(bf16[16,2048]{1,0:T(8,128)(2,1)S(1)} %get-tuple-element.61.refs_0_), channel_id=1, source_target_pairs={{0,3},{1,0},{2,1},{3,2},{4,7},{5,4},{6,5},{7,6},{8,11},{9,8},{10,9... | collective-permute-start | bytes 196616 | tf_op jit(solution)/shard_map/ppermute | solution.py:354
  19.8 0.6 collective-permute-start.5
  20.4 1.3 %collective-permute-done.3.refs_1_ = bf16[16,2048]{1,0:T(8,128)(2,1)S(1)} collective-permute-done((bf16[16,2048]{1,0:T(8,128)(2,1)S(1)}, bf16[16,2048]{1,0:T(8,128)(2,1)S(1)}, u32[]{:S(2)}, u32[]{:S(2)}) %collective-permute-start.3) | collective-permute-done | bytes 65568 | tf_op jit(solution)/shard_map/ppermute | solution.py:354
  21.7 4.5 %collective-permute-done.4.refs_0_ = bf16[16,2048]{1,0:T(8,128)(2,1)S(1)} collective-permute-done((bf16[16,2048]{1,0:T(8,128)(2,1)S(1)}, bf16[16,2048]{1,0:T(8,128)(2,1)S(1)}, u32[]{:S(2)}, u32[]{:S(2)}) %collective-permute-start.4) | collective-permute-done | bytes 65568 | tf_op jit(solution)/shard_map/ppermute | solution.py:354
  26.2 0.1 collective-permute-start.6
  26.3 1.3 %collective-permute-start.7 = (bf16[32,2048]{1,0:T(8,128)(2,1)S(1)}, bf16[32,2048]{1,0:T(8,128)(2,1)S(1)}, u32[]{:S(2)}, u32[]{:S(2)}) collective-permute-start(bf16[32,2048]{1,0:T(8,128)(2,1)S(1)} %join.5.refs_0_), channel_id=1, source_target_pairs={{0,8},{4,20},{8,0},{12,28},{16,24},{20,4},{24,16},{28,12},{1,9},{5... | collective-permute-start | bytes 393224 | tf_op jit(solution)/shard_map/ppermute | solution.py:357
  27.6 0.8 %collective-permute-start.8 = (bf16[32,2048]{1,0:T(8,128)(2,1)S(1)}, bf16[32,2048]{1,0:T(8,128)(2,1)S(1)}, u32[]{:S(2)}, u32[]{:S(2)}) collective-permute-start(bf16[32,2048]{1,0:T(8,128)(2,1)S(1)} %join.6.refs_1_), channel_id=1, source_target_pairs={{0,8},{4,20},{8,0},{12,28},{16,24},{20,4},{24,16},{28,12},{1,9},{5... | collective-permute-start | bytes 393224 | tf_op jit(solution)/shard_map/ppermute | solution.py:357
  28.4 1.3 %collective-permute-start.12 = (bf16[64,2048]{1,0:T(8,128)(2,1)S(1)}, bf16[64,2048]{1,0:T(8,128)(2,1)S(1)}, u32[]{:S(2)}, u32[]{:S(2)}) collective-permute-start(bf16[64,2048]{1,0:T(8,128)(2,1)S(1)} %join.7.refs_0_), channel_id=1, source_target_pairs={{0,16},{4,12},{8,24},{12,4},{16,0},{20,28},{24,8},{28,20},{1,17},{... | collective-permute-start | bytes 786440 | tf_op jit(solution)/shard_map/ppermute | solution.py:357
  29.7 1.1 %experts.4 = (f32[64,2048]{1,0:T(8,128)S(1)}, bf16[64,2048]{1,0:T(8,128)(2,1)S(1)}) custom-call(s32[1]{0:T(128)} %bitcast.place, s32[1]{0:T(128)} %bitcast.1.spot, s32[10,4,128]{2,1,0:T(4,128)S(1)} %bitcast.8, f32[10,4,128]{2,1,0:T(4,128)S(1)} %bitcast.12, bf16[2048,512]{1,0:T(8,128)(2,1)S(1)} %get-tuple-element.62.gate, ...), custom_call_target="tpu_custom_call" | custom-call | tf_op jit(solution)/shard_map/experts/pallas_call | solution.py:188
  30.8 1.0 %collective-permute-done.7.refs_0_ = bf16[32,2048]{1,0:T(8,128)(2,1)S(1)} collective-permute-done((bf16[32,2048]{1,0:T(8,128)(2,1)S(1)}, bf16[32,2048]{1,0:T(8,128)(2,1)S(1)}, u32[]{:S(2)}, u32[]{:S(2)}) %collective-permute-start.7) | collective-permute-done | bytes 131104 | tf_op jit(solution)/shard_map/ppermute | solution.py:357
  31.8 2.8 %collective-permute-done.8.refs_1_ = bf16[32,2048]{1,0:T(8,128)(2,1)S(1)} collective-permute-done((bf16[32,2048]{1,0:T(8,128)(2,1)S(1)}, bf16[32,2048]{1,0:T(8,128)(2,1)S(1)}, u32[]{:S(2)}, u32[]{:S(2)}) %collective-permute-start.8) | collective-permute-done | bytes 131104 | tf_op jit(solution)/shard_map/ppermute | solution.py:357
  34.7 0.1 collective-permute-start.11
  34.7 1.3 %collective-permute-start.9 = (bf16[32,2048]{1,0:T(8,128)(2,1)S(1)}, bf16[32,2048]{1,0:T(8,128)(2,1)S(1)}, u32[]{:S(2)}, u32[]{:S(2)}) collective-permute-start(bf16[32,2048]{1,0:T(8,128)(2,1)S(1)} %collective-permute-done.7.refs_0_), channel_id=1, source_target_pairs={{0,16},{4,12},{8,24},{12,4},{16,0},{20,28},{24,8},{28,20},{1,17},{... | collective-permute-start | bytes 393224 | tf_op jit(solution)/shard_map/ppermute | solution.py:357
  36.1 0.8 %collective-permute-start.10 = (bf16[32,2048]{1,0:T(8,128)(2,1)S(1)}, bf16[32,2048]{1,0:T(8,128)(2,1)S(1)}, u32[]{:S(2)}, u32[]{:S(2)}) collective-permute-start(bf16[32,2048]{1,0:T(8,128)(2,1)S(1)} %collective-permute-done.8.refs_1_), channel_id=1, source_target_pairs={{0,16},{4,12},{8,24},{12,4},{16,0},{20,28},{24,8},{28,20},{1,17},{... | collective-permute-start | bytes 393224 | tf_op jit(solution)/shard_map/ppermute | solution.py:357
  36.8 1.1 %experts.5 = (f32[64,2048]{1,0:T(8,128)S(1)}, bf16[64,2048]{1,0:T(8,128)(2,1)S(1)}) custom-call(s32[1]{0:T(128)} %bitcast.place, s32[1]{0:T(128)} %bitcast.1.spot, s32[10,4,128]{2,1,0:T(4,128)S(1)} %bitcast.9, f32[10,4,128]{2,1,0:T(4,128)S(1)} %bitcast.13, bf16[2048,512]{1,0:T(8,128)(2,1)S(1)} %get-tuple-element.62.gate, ...), custom_call_target="tpu_custom_call" | custom-call | tf_op jit(solution)/shard_map/experts/pallas_call | solution.py:188
  38.0 0.1 collective-permute-start.14
  38.1 1.7 %collective-permute-done.9.refs_0_ = bf16[32,2048]{1,0:T(8,128)(2,1)S(1)} collective-permute-done((bf16[32,2048]{1,0:T(8,128)(2,1)S(1)}, bf16[32,2048]{1,0:T(8,128)(2,1)S(1)}, u32[]{:S(2)}, u32[]{:S(2)}) %collective-permute-start.9) | collective-permute-done | bytes 131104 | tf_op jit(solution)/shard_map/ppermute | solution.py:357
  39.8 1.4 %collective-permute-done.10.refs_1_ = bf16[32,2048]{1,0:T(8,128)(2,1)S(1)} collective-permute-done((bf16[32,2048]{1,0:T(8,128)(2,1)S(1)}, bf16[32,2048]{1,0:T(8,128)(2,1)S(1)}, u32[]{:S(2)}, u32[]{:S(2)}) %collective-permute-start.10) | collective-permute-done | bytes 131104 | tf_op jit(solution)/shard_map/ppermute | solution.py:357
  41.2 0.1 collective-permute-start.13
  41.3 1.1 %experts.6 = (f32[64,2048]{1,0:T(8,128)S(1)}, bf16[64,2048]{1,0:T(8,128)(2,1)S(1)}) custom-call(s32[1]{0:T(128)} %bitcast.place, s32[1]{0:T(128)} %bitcast.1.spot, s32[10,4,128]{2,1,0:T(4,128)S(1)} %bitcast.10, f32[10,4,128]{2,1,0:T(4,128)S(1)} %bitcast.14, bf16[2048,512]{1,0:T(8,128)(2,1)S(1)} %get-tuple-element.62.gate, ...), custom_call_target="tpu_custom_call" | custom-call | tf_op jit(solution)/shard_map/experts/pallas_call | solution.py:188
  42.4 0.4 collective-permute-done.13.refs_1_
  42.8 1.1 %experts.7 = (f32[64,2048]{1,0:T(8,128)S(1)}, bf16[64,2048]{1,0:T(8,128)(2,1)S(1)}) custom-call(s32[1]{0:T(128)} %bitcast.place, s32[1]{0:T(128)} %bitcast.1.spot, s32[10,4,128]{2,1,0:T(4,128)S(1)} %bitcast.11, f32[10,4,128]{2,1,0:T(4,128)S(1)} %bitcast.15, bf16[2048,512]{1,0:T(8,128)(2,1)S(1)} %get-tuple-element.62.gate, ...), custom_call_target="tpu_custom_call" | custom-call | tf_op jit(solution)/shard_map/experts/pallas_call | solution.py:188
  43.9 0.2 collective-permute-start.19
  44.1 0.4 collective-permute-start.16
  44.5 0.1 collective-permute-start.15
  44.6 0.4 collective-permute-start.18
  45.0 0.5 collective-permute-done.19.refs_1_
  45.6 1.3 %collective-permute-start.20 = (bf16[64,2048]{1,0:T(8,128)(2,1)S(1)}, bf16[64,2048]{1,0:T(8,128)(2,1)S(1)}, u32[]{:S(2)}, u32[]{:S(2)}) collective-permute-start(bf16[64,2048]{1,0:T(8,128)(2,1)S(1)} %add.9), channel_id=1, source_target_pairs={{0,16},{4,12},{8,24},{12,4},{16,0},{20,28},{24,8},{28,20},{1,17},{... | collective-permute-start | bytes 786440 | tf_op jit(solution)/shard_map/ppermute | solution.py:357
  46.9 0.1 add.7.refs_0_
  47.1 0.8 %collective-permute-start.17 = (bf16[64,2048]{1,0:T(8,128)(2,1)S(1)}, bf16[64,2048]{1,0:T(8,128)(2,1)S(1)}, u32[]{:S(2)}, u32[]{:S(2)}) collective-permute-start(bf16[64,2048]{1,0:T(8,128)(2,1)S(1)} %add.6), channel_id=1, source_target_pairs={{0,16},{4,12},{8,24},{12,4},{16,0},{20,28},{24,8},{28,20},{1,17},{... | collective-permute-start | bytes 786440 | tf_op jit(solution)/shard_map/ppermute | solution.py:357
  48.0 4.1 %collective-permute-done.20.refs_1_ = bf16[64,2048]{1,0:T(8,128)(2,1)S(1)} collective-permute-done((bf16[64,2048]{1,0:T(8,128)(2,1)S(1)}, bf16[64,2048]{1,0:T(8,128)(2,1)S(1)}, u32[]{:S(2)}, u32[]{:S(2)}) %collective-permute-start.20) | collective-permute-done | bytes 262176 | tf_op jit(solution)/shard_map/ppermute | solution.py:357
  52.1 1.4 %collective-permute-start.21 = (bf16[64,2048]{1,0:T(8,128)(2,1)S(1)}, bf16[64,2048]{1,0:T(8,128)(2,1)S(1)}, u32[]{:S(2)}, u32[]{:S(2)}) collective-permute-start(bf16[64,2048]{1,0:T(8,128)(2,1)S(1)} %add.10), channel_id=1, source_target_pairs={{0,8},{4,20},{8,0},{12,28},{16,24},{20,4},{24,16},{28,12},{1,9},{5... | collective-permute-start | bytes 786440 | tf_op jit(solution)/shard_map/ppermute | solution.py:357
  53.5 2.1 %collective-permute-done.17.refs_1_ = bf16[64,2048]{1,0:T(8,128)(2,1)S(1)} collective-permute-done((bf16[64,2048]{1,0:T(8,128)(2,1)S(1)}, bf16[64,2048]{1,0:T(8,128)(2,1)S(1)}, u32[]{:S(2)}, u32[]{:S(2)}) %collective-permute-start.17) | collective-permute-done | bytes 262176 | tf_op jit(solution)/shard_map/ppermute | solution.py:357
  55.6 2.9 %collective-permute-done.21.refs_2_ = bf16[64,2048]{1,0:T(8,128)(2,1)S(1)} collective-permute-done((bf16[64,2048]{1,0:T(8,128)(2,1)S(1)}, bf16[64,2048]{1,0:T(8,128)(2,1)S(1)}, u32[]{:S(2)}, u32[]{:S(2)}) %collective-permute-start.21) | collective-permute-done | bytes 262176 | tf_op jit(solution)/shard_map/ppermute | solution.py:357
  58.5 0.1 add.11
  58.7 1.8 %collective-permute-start.23 = (bf16[16,2048]{1,0:T(8,128)(2,1)S(1)}, bf16[16,2048]{1,0:T(8,128)(2,1)S(1)}, u32[]{:S(2)}, u32[]{:S(2)}) collective-permute-start(bf16[16,2048]{1,0:T(8,128)(2,1)S(1)} %get-tuple-element.93), channel_id=1, source_target_pairs={{0,2},{1,3},{2,0},{3,1},{4,6},{5,7},{6,4},{7,5},{8,10},{9,11},{10,... | collective-permute-start | bytes 196616 | tf_op jit(solution)/shard_map/ppermute | solution.py:354
  60.4 2.2 %collective-permute-start.24 = (bf16[16,2048]{1,0:T(8,128)(2,1)S(1)}, bf16[16,2048]{1,0:T(8,128)(2,1)S(1)}, u32[]{:S(2)}, u32[]{:S(2)}) collective-permute-start(bf16[16,2048]{1,0:T(8,128)(2,1)S(1)} %get-tuple-element.94), channel_id=1, source_target_pairs={{0,3},{1,0},{2,1},{3,2},{4,7},{5,4},{6,5},{7,6},{8,11},{9,8},{10,9... | collective-permute-start | bytes 196616 | tf_op jit(solution)/shard_map/ppermute | solution.py:354
  62.6 2.6 %collective-permute-done.22.rest_0_ = bf16[16,2048]{1,0:T(8,128)(2,1)S(1)} collective-permute-done((bf16[16,2048]{1,0:T(8,128)(2,1)S(1)}, bf16[16,2048]{1,0:T(8,128)(2,1)S(1)}, u32[]{:S(2)}, u32[]{:S(2)}) %collective-permute-start.22) | collective-permute-done | bytes 65568 | tf_op jit(solution)/shard_map/ppermute | solution.py:354
  65.1 1.3 %collective-permute-done.23.rest_1_ = bf16[16,2048]{1,0:T(8,128)(2,1)S(1)} collective-permute-done((bf16[16,2048]{1,0:T(8,128)(2,1)S(1)}, bf16[16,2048]{1,0:T(8,128)(2,1)S(1)}, u32[]{:S(2)}, u32[]{:S(2)}) %collective-permute-start.23) | collective-permute-done | bytes 65568 | tf_op jit(solution)/shard_map/ppermute | solution.py:354
  66.4 0.7 %finish.1 = bf16[4,4,2048]{2,1,0:T(4,128)(2,1)} custom-call(f32[16,2048]{1,0:T(8,128)S(1)} %get-tuple-element.60.stream_ref, f32[16,2048]{1,0:T(8,128)S(1)} %get-tuple-element.91.own_ref, bf16[16,2048]{1,0:T(8,128)(2,1)S(1)} %collective-permute-done.22.rest_0_, bf16[16,2048]{1,0:T(8,128)(2,1)S(1)} %collective-permute-done.23.rest_1_, ...), custom_call_target="tpu_custom_call" | custom-call | tf_op jit(solution)/shard_map/finish/pallas_call | solution.py:188
  (29 shorter events, 0.4 us)
Async XLA Ops:
  6.1 10.0 %collective-permute-start = (bf16[16,2048]{1,0:T(8,128)(2,1)S(1)}, bf16[16,2048]{1,0:T(8,128)(2,1)S(1)}, u32[]{:S(2)}, u32[]{:S(2)}) collective-permute-start(bf16[16,2048]{1,0:T(8,128)(2,1)S(1)} %get-tuple-element.51), channel_id=1, source_target_pairs={{0,1},{1,2},{2,3},{3,0},{4,5},{5,6},{6,7},{7,4},{8,9},{9,10},{10,1... | collective-permute-start | bytes 196616 | tf_op jit(solution)/shard_map/ppermute | solution.py:354
  9.2 7.1 %collective-permute-start.1 = (bf16[16,2048]{1,0:T(8,128)(2,1)S(1)}, bf16[16,2048]{1,0:T(8,128)(2,1)S(1)}, u32[]{:S(2)}, u32[]{:S(2)}) collective-permute-start(bf16[16,2048]{1,0:T(8,128)(2,1)S(1)} %get-tuple-element.52), channel_id=1, source_target_pairs={{0,2},{1,3},{2,0},{3,1},{4,6},{5,7},{6,4},{7,5},{8,10},{9,11},{10,... | collective-permute-start | bytes 196616 | tf_op jit(solution)/shard_map/ppermute | solution.py:354
  11.8 4.8 %copy-start.2 = (bf16[4,4,2048]{2,1,0:T(4,128)(2,1)S(1)}, bf16[4,4,2048]{2,1,0:T(4,128)(2,1)}, u32[]{:S(2)}) copy-start(bf16[4,4,2048]{2,1,0:T(4,128)(2,1)} %residual_ref.1) | copy-start | bytes 196612
  11.8 4.8 %copy-start.3 = (f32[2048]{0:T(1024)S(1)}, f32[2048]{0:T(1024)}, u32[]{:S(2)}) copy-start(f32[2048]{0:T(1024)} %param.26) | copy-start | bytes 24580
  11.8 17.9 %copy-start = (s32[4,128,10]{1,0,2:T(4,128)S(1)}, s32[4,128,10]{1,0,2:T(4,128)}, u32[]{:S(2)}) copy-start(s32[4,128,10]{1,0,2:T(4,128)} %param.27) | copy-start | bytes 61444
  11.8 17.9 %copy-start.1 = (f32[4,128,10]{1,0,2:T(4,128)S(1)}, f32[4,128,10]{1,0,2:T(4,128)}, u32[]{:S(2)}) copy-start(f32[4,128,10]{1,0,2:T(4,128)} %param.28) | copy-start | bytes 61444
  11.8 4.8 %collective-permute-start.2 = (bf16[16,2048]{1,0:T(8,128)(2,1)S(1)}, bf16[16,2048]{1,0:T(8,128)(2,1)S(1)}, u32[]{:S(2)}, u32[]{:S(2)}) collective-permute-start(bf16[16,2048]{1,0:T(8,128)(2,1)S(1)} %get-tuple-element.53), channel_id=1, source_target_pairs={{0,3},{1,0},{2,1},{3,2},{4,7},{5,4},{6,5},{7,6},{8,11},{9,8},{10,9... | collective-permute-start | bytes 196616 | tf_op jit(solution)/shard_map/ppermute | solution.py:354
  16.8 4.9 %collective-permute-start.3 = (bf16[16,2048]{1,0:T(8,128)(2,1)S(1)}, bf16[16,2048]{1,0:T(8,128)(2,1)S(1)}, u32[]{:S(2)}, u32[]{:S(2)}) collective-permute-start(bf16[16,2048]{1,0:T(8,128)(2,1)S(1)} %get-tuple-element.61.refs_0_), channel_id=1, source_target_pairs={{0,3},{1,0},{2,1},{3,2},{4,7},{5,4},{6,5},{7,6},{8,11},{9,8},{10,9... | collective-permute-start | bytes 196616 | tf_op jit(solution)/shard_map/ppermute | solution.py:354
  19.8 6.4 %collective-permute-start.4 = (bf16[16,2048]{1,0:T(8,128)(2,1)S(1)}, bf16[16,2048]{1,0:T(8,128)(2,1)S(1)}, u32[]{:S(2)}, u32[]{:S(2)}) collective-permute-start(bf16[16,2048]{1,0:T(8,128)(2,1)S(1)} %get-tuple-element.61.refs_0_), channel_id=1, source_target_pairs={{0,2},{1,3},{2,0},{3,1},{4,6},{5,7},{6,4},{7,5},{8,10},{9,11},{10,... | collective-permute-start | bytes 196616 | tf_op jit(solution)/shard_map/ppermute | solution.py:354
  19.8 6.4 %collective-permute-start.5 = (bf16[16,2048]{1,0:T(8,128)(2,1)S(1)}, bf16[16,2048]{1,0:T(8,128)(2,1)S(1)}, u32[]{:S(2)}, u32[]{:S(2)}) collective-permute-start(bf16[16,2048]{1,0:T(8,128)(2,1)S(1)} %get-tuple-element.61.refs_0_), channel_id=1, source_target_pairs={{0,1},{1,2},{2,3},{3,0},{4,5},{5,6},{6,7},{7,4},{8,9},{9,10},{10,1... | collective-permute-start | bytes 196616 | tf_op jit(solution)/shard_map/ppermute | solution.py:354
  26.2 3.5 %collective-permute-start.6 = (bf16[64,2048]{1,0:T(8,128)(2,1)S(1)}, bf16[64,2048]{1,0:T(8,128)(2,1)S(1)}, u32[]{:S(2)}, u32[]{:S(2)}) collective-permute-start(bf16[64,2048]{1,0:T(8,128)(2,1)S(1)} %join.7.refs_0_), channel_id=1, source_target_pairs={{0,4},{4,0},{8,12},{12,8},{16,20},{20,16},{24,28},{28,24},{1,5},{5... | collective-permute-start | bytes 786440 | tf_op jit(solution)/shard_map/ppermute | solution.py:362
  26.3 5.5 %collective-permute-start.7 = (bf16[32,2048]{1,0:T(8,128)(2,1)S(1)}, bf16[32,2048]{1,0:T(8,128)(2,1)S(1)}, u32[]{:S(2)}, u32[]{:S(2)}) collective-permute-start(bf16[32,2048]{1,0:T(8,128)(2,1)S(1)} %join.5.refs_0_), channel_id=1, source_target_pairs={{0,8},{4,20},{8,0},{12,28},{16,24},{20,4},{24,16},{28,12},{1,9},{5... | collective-permute-start | bytes 393224 | tf_op jit(solution)/shard_map/ppermute | solution.py:357
  27.6 7.0 %collective-permute-start.8 = (bf16[32,2048]{1,0:T(8,128)(2,1)S(1)}, bf16[32,2048]{1,0:T(8,128)(2,1)S(1)}, u32[]{:S(2)}, u32[]{:S(2)}) collective-permute-start(bf16[32,2048]{1,0:T(8,128)(2,1)S(1)} %join.6.refs_1_), channel_id=1, source_target_pairs={{0,8},{4,20},{8,0},{12,28},{16,24},{20,4},{24,16},{28,12},{1,9},{5... | collective-permute-start | bytes 393224 | tf_op jit(solution)/shard_map/ppermute | solution.py:357
  28.4 8.4 %collective-permute-start.12 = (bf16[64,2048]{1,0:T(8,128)(2,1)S(1)}, bf16[64,2048]{1,0:T(8,128)(2,1)S(1)}, u32[]{:S(2)}, u32[]{:S(2)}) collective-permute-start(bf16[64,2048]{1,0:T(8,128)(2,1)S(1)} %join.7.refs_0_), channel_id=1, source_target_pairs={{0,16},{4,12},{8,24},{12,4},{16,0},{20,28},{24,8},{28,20},{1,17},{... | collective-permute-start | bytes 786440 | tf_op jit(solution)/shard_map/ppermute | solution.py:357
  34.7 2.2 %collective-permute-start.11 = (bf16[64,2048]{1,0:T(8,128)(2,1)S(1)}, bf16[64,2048]{1,0:T(8,128)(2,1)S(1)}, u32[]{:S(2)}, u32[]{:S(2)}) collective-permute-start(bf16[64,2048]{1,0:T(8,128)(2,1)S(1)} %join.8.refs_0_), channel_id=1, source_target_pairs={{0,4},{4,0},{8,12},{12,8},{16,20},{20,16},{24,28},{28,24},{1,5},{5... | collective-permute-start | bytes 786440 | tf_op jit(solution)/shard_map/ppermute | solution.py:362
  34.7 5.0 %collective-permute-start.9 = (bf16[32,2048]{1,0:T(8,128)(2,1)S(1)}, bf16[32,2048]{1,0:T(8,128)(2,1)S(1)}, u32[]{:S(2)}, u32[]{:S(2)}) collective-permute-start(bf16[32,2048]{1,0:T(8,128)(2,1)S(1)} %collective-permute-done.7.refs_0_), channel_id=1, source_target_pairs={{0,16},{4,12},{8,24},{12,4},{16,0},{20,28},{24,8},{28,20},{1,17},{... | collective-permute-start | bytes 393224 | tf_op jit(solution)/shard_map/ppermute | solution.py:357
  36.1 5.1 %collective-permute-start.10 = (bf16[32,2048]{1,0:T(8,128)(2,1)S(1)}, bf16[32,2048]{1,0:T(8,128)(2,1)S(1)}, u32[]{:S(2)}, u32[]{:S(2)}) collective-permute-start(bf16[32,2048]{1,0:T(8,128)(2,1)S(1)} %collective-permute-done.8.refs_1_), channel_id=1, source_target_pairs={{0,16},{4,12},{8,24},{12,4},{16,0},{20,28},{24,8},{28,20},{1,17},{... | collective-permute-start | bytes 393224 | tf_op jit(solution)/shard_map/ppermute | solution.py:357
  38.0 3.3 %collective-permute-start.14 = (bf16[64,2048]{1,0:T(8,128)(2,1)S(1)}, bf16[64,2048]{1,0:T(8,128)(2,1)S(1)}, u32[]{:S(2)}, u32[]{:S(2)}) collective-permute-start(bf16[64,2048]{1,0:T(8,128)(2,1)S(1)} %collective-permute-done.12.refs_0_), channel_id=1, source_target_pairs={{0,4},{4,0},{8,12},{12,8},{16,20},{20,16},{24,28},{28,24},{1,5},{5... | collective-permute-start | bytes 786440 | tf_op jit(solution)/shard_map/ppermute | solution.py:362
  41.2 1.6 %collective-permute-start.13 = (bf16[64,2048]{1,0:T(8,128)(2,1)S(1)}, bf16[64,2048]{1,0:T(8,128)(2,1)S(1)}, u32[]{:S(2)}, u32[]{:S(2)}) collective-permute-start(bf16[64,2048]{1,0:T(8,128)(2,1)S(1)} %join.9.refs_0_), channel_id=1, source_target_pairs={{0,4},{4,0},{8,12},{12,8},{16,20},{20,16},{24,28},{28,24},{1,5},{5... | collective-permute-start | bytes 786440 | tf_op jit(solution)/shard_map/ppermute | solution.py:362
  43.9 1.6 %collective-permute-start.19 = (bf16[64,2048]{1,0:T(8,128)(2,1)S(1)}, bf16[64,2048]{1,0:T(8,128)(2,1)S(1)}, u32[]{:S(2)}, u32[]{:S(2)}) collective-permute-start(bf16[64,2048]{1,0:T(8,128)(2,1)S(1)} %get-tuple-element.90), channel_id=1, source_target_pairs={{0,4},{4,0},{8,12},{12,8},{16,20},{20,16},{24,28},{28,24},{1,5},{5... | collective-permute-start | bytes 786440 | tf_op jit(solution)/shard_map/ppermute | solution.py:362
  44.1 2.8 %collective-permute-start.16 = (bf16[64,2048]{1,0:T(8,128)(2,1)S(1)}, bf16[64,2048]{1,0:T(8,128)(2,1)S(1)}, u32[]{:S(2)}, u32[]{:S(2)}) collective-permute-start(bf16[64,2048]{1,0:T(8,128)(2,1)S(1)} %get-tuple-element.83), channel_id=1, source_target_pairs={{0,4},{4,0},{8,12},{12,8},{16,20},{20,16},{24,28},{28,24},{1,5},{5... | collective-permute-start | bytes 786440 | tf_op jit(solution)/shard_map/ppermute | solution.py:362
  44.5 2.5 %collective-permute-start.15 = (bf16[64,2048]{1,0:T(8,128)(2,1)S(1)}, bf16[64,2048]{1,0:T(8,128)(2,1)S(1)}, u32[]{:S(2)}, u32[]{:S(2)}) collective-permute-start(bf16[64,2048]{1,0:T(8,128)(2,1)S(1)} %get-tuple-element.81), channel_id=1, source_target_pairs={{0,4},{4,0},{8,12},{12,8},{16,20},{20,16},{24,28},{28,24},{1,5},{5... | collective-permute-start | bytes 786440 | tf_op jit(solution)/shard_map/ppermute | solution.py:362
  44.6 3.2 %collective-permute-start.18 = (bf16[64,2048]{1,0:T(8,128)(2,1)S(1)}, bf16[64,2048]{1,0:T(8,128)(2,1)S(1)}, u32[]{:S(2)}, u32[]{:S(2)}) collective-permute-start(bf16[64,2048]{1,0:T(8,128)(2,1)S(1)} %get-tuple-element.87), channel_id=1, source_target_pairs={{0,4},{4,0},{8,12},{12,8},{16,20},{20,16},{24,28},{28,24},{1,5},{5... | collective-permute-start | bytes 786440 | tf_op jit(solution)/shard_map/ppermute | solution.py:362
  45.6 6.4 %collective-permute-start.20 = (bf16[64,2048]{1,0:T(8,128)(2,1)S(1)}, bf16[64,2048]{1,0:T(8,128)(2,1)S(1)}, u32[]{:S(2)}, u32[]{:S(2)}) collective-permute-start(bf16[64,2048]{1,0:T(8,128)(2,1)S(1)} %add.9), channel_id=1, source_target_pairs={{0,16},{4,12},{8,24},{12,4},{16,0},{20,28},{24,8},{28,20},{1,17},{... | collective-permute-start | bytes 786440 | tf_op jit(solution)/shard_map/ppermute | solution.py:357
  47.1 8.5 %collective-permute-start.17 = (bf16[64,2048]{1,0:T(8,128)(2,1)S(1)}, bf16[64,2048]{1,0:T(8,128)(2,1)S(1)}, u32[]{:S(2)}, u32[]{:S(2)}) collective-permute-start(bf16[64,2048]{1,0:T(8,128)(2,1)S(1)} %add.6), channel_id=1, source_target_pairs={{0,16},{4,12},{8,24},{12,4},{16,0},{20,28},{24,8},{28,20},{1,17},{... | collective-permute-start | bytes 786440 | tf_op jit(solution)/shard_map/ppermute | solution.py:357
  52.1 6.4 %collective-permute-start.21 = (bf16[64,2048]{1,0:T(8,128)(2,1)S(1)}, bf16[64,2048]{1,0:T(8,128)(2,1)S(1)}, u32[]{:S(2)}, u32[]{:S(2)}) collective-permute-start(bf16[64,2048]{1,0:T(8,128)(2,1)S(1)} %add.10), channel_id=1, source_target_pairs={{0,8},{4,20},{8,0},{12,28},{16,24},{20,4},{24,16},{28,12},{1,9},{5... | collective-permute-start | bytes 786440 | tf_op jit(solution)/shard_map/ppermute | solution.py:357
  58.6 6.5 %collective-permute-start.22 = (bf16[16,2048]{1,0:T(8,128)(2,1)S(1)}, bf16[16,2048]{1,0:T(8,128)(2,1)S(1)}, u32[]{:S(2)}, u32[]{:S(2)}) collective-permute-start(bf16[16,2048]{1,0:T(8,128)(2,1)S(1)} %get-tuple-element.92), channel_id=1, source_target_pairs={{0,1},{1,2},{2,3},{3,0},{4,5},{5,6},{6,7},{7,4},{8,9},{9,10},{10,1... | collective-permute-start | bytes 196616 | tf_op jit(solution)/shard_map/ppermute | solution.py:354
  58.7 7.8 %collective-permute-start.23 = (bf16[16,2048]{1,0:T(8,128)(2,1)S(1)}, bf16[16,2048]{1,0:T(8,128)(2,1)S(1)}, u32[]{:S(2)}, u32[]{:S(2)}) collective-permute-start(bf16[16,2048]{1,0:T(8,128)(2,1)S(1)} %get-tuple-element.93), channel_id=1, source_target_pairs={{0,2},{1,3},{2,0},{3,1},{4,6},{5,7},{6,4},{7,5},{8,10},{9,11},{10,... | collective-permute-start | bytes 196616 | tf_op jit(solution)/shard_map/ppermute | solution.py:354
  60.4 6.0 %collective-permute-start.24 = (bf16[16,2048]{1,0:T(8,128)(2,1)S(1)}, bf16[16,2048]{1,0:T(8,128)(2,1)S(1)}, u32[]{:S(2)}, u32[]{:S(2)}) collective-permute-start(bf16[16,2048]{1,0:T(8,128)(2,1)S(1)} %get-tuple-element.94), channel_id=1, source_target_pairs={{0,3},{1,0},{2,1},{3,2},{4,7},{5,4},{6,5},{7,6},{8,11},{9,8},{10,9... | collective-permute-start | bytes 196616 | tf_op jit(solution)/shard_map/ppermute | solution.py:354

commit v6 on v5

--- a/solution.py
+++ b/solution.py
@@ -448,25 +448,27 @@
         if m > 1 and m - 1 in served:
             peers, served[m - 1] = lax.optimization_barrier((peers, served[m - 1]))
         serve(m, peers)
+    cut = 2
     for m in range(last + 1):
         leaves = m >> (bits - 1)
-        totals[m] = add(
-            (served[m][0], other(served[m][1])), (held, jnp.bfloat16 if leaves else jnp.float32)
-        )[0]
+        kind = jnp.bfloat16 if leaves else jnp.float32
+        pieces = cut if m % 2 else 1
+        totals[m] = add((served[m][0], other(served[m][1])), *[(held // pieces, kind)] * pieces)
     came = {}
     for j in reversed(range(bits)):
         top = 1 << j
         for m in reversed(range(1, top)):
-            leaves = m >> (j - 1)
-            totals[m] = add(
-                (totals[m], across(totals[m + top], j)),
-                (held, jnp.bfloat16 if leaves else jnp.float32),
-            )[0]
+            kind = jnp.bfloat16 if m >> (j - 1) else jnp.float32
+            totals[m] = [
+                add((x, across(y, j)), (x.shape[0], kind))[0]
+                for x, y in zip(totals[m], totals[m + top])
+            ]
         if top > 1:
             totals[top], totals[0] = lax.optimization_barrier((totals[top], totals[0]))
-        came[j] = across(totals[top], j)
+        sent = [across(x, j) for x in totals[top]]
+        came[j] = join(*sent) if len(sent) > 1 else sent[0]
     total, *blocks = add(
-        (totals[0], *[came[j] for j in reversed(range(bits))]),
+        (totals[0][0], *[came[j] for j in reversed(range(bits))]),
         (size, jnp.float32),
         *[(size, jnp.bfloat16)] * (ring - 1),
     )

time: 67.2 us -> 66.8 us (level)
  waiting for transfers between devices: 26.9 us -> 23.7 us
  starting transfers between devices: 25.2 us -> 27.9 us
    ppermute x8 -> x10, waiting for transfers between devices: 16 us -> 12.1 us  [across(): lax.ppermute(x, 'dev', [(i, i ^ 2 << (j + i % 2) % bits) for i in range(w...]
    ppermute x8 -> x10, starting transfers between devices: 9.06 us -> 11.7 us  [across(): lax.ppermute(x, 'dev', [(i, i ^ 2 << (j + i % 2) % bits) for i in range(w...]
    ppermute x9, waiting for transfers between devices: 10 us -> 10.8 us  [along(): return lax.ppermute(x, 'head', [(i, (i + k) % ring) for i in range(ring)])]
    pallas_call x17 -> x19, Pallas kernels: 5.79 us -> 5.83 us  [local(): pl.pallas_call(kernel, out_shape=out_shape, in_specs=[pl.BlockSpec(memory...]
  transfers between devices with their start and end apart: 25 -> 27, of which waited for: 15 -> 14; matrix products, arithmetic and copies ran while one was open for 0% -> 0% of each run, Pallas kernels for 10% -> 12%
where the time goes in v6:
time: 66.8 us; the launch traced here: 66.7 us
  starting transfers between devices  27.9 us (42%)
  waiting for transfers between devices  23.7 us (35%)
  Pallas kernels  14.9 us (22%)
    ppermute x9, starting transfers between devices, along(): return lax.ppermute(x, 'head', [(i, (i + k) % ring) for i in range(ring)])  14.8 us
    ppermute x10, waiting for transfers between devices, across(): lax.ppermute(x, 'dev', [(i, i ^ 2 << (j + i % 2) % bits) for i in range(w...  12.1 us
    ppermute x10, starting transfers between devices, across(): lax.ppermute(x, 'dev', [(i, i ^ 2 << (j + i % 2) % bits) for i in range(w...  11.7 us
    ppermute x9, waiting for transfers between devices, along(): return lax.ppermute(x, 'head', [(i, (i + k) % ring) for i in range(ring)])  10.8 us
    pallas_call x1, Pallas kernels, attend(): pl.pallas_call(functools.partial(attend_kernel, blocks=blocks), out_shape...  6.14 us
    pallas_call x19, Pallas kernels, local(): pl.pallas_call(kernel, out_shape=out_shape, in_specs=[pl.BlockSpec(memory...  5.83 us
    pallas_call x1, Pallas kernels, load(): pl.pallas_call(load_kernel, out_shape=[jax.ShapeDtypeStruct(mat.shape[1:]...  2.88 us
    ppermute x8, starting transfers between devices, other(): return lax.ppermute(x, 'dev', [(i, i ^ 1) for i in range(width)])  1.44 us
  transfers between devices with their start and end apart: 27, of which 14 were waited for; matrix products, arithmetic and copies ran while one was open for 0% of the time, Pallas kernels for 12%

profile of v6, /device:TPU:0, one launch (start us, length us, event | category | flops | bytes accessed | tf_op | source)
XLA Modules:
  0.0 66.7 jit_solution(7717814654174049245)
XLA Ops:
  0.0 6.1 %attend.1 = (f32[16,2048]{1,0:T(8,128)S(1)}, bf16[16,2048]{1,0:T(8,128)(2,1)S(1)}, bf16[16,2048]{1,0:T(8,128)(2,1)S(1)}, bf16[16,2048]{1,0:T(8,128)(2,1)S(1)}) custom-call(s32[1]{0:T(128)} %bitcast.place, s32[1]{0:T(128)} %bitcast.1.spot, bf16[4,16,512]{2,1,0:T(8,128)(2,1)} %refs_0_.2, bf16[4,16,512]{2,1,0:T(8,128)(2,1)} %refs_1_.2, ...), custom_call_target="tpu_custom_call" | custom-call | tf_op jit(solution)/shard_map/attend/pallas_call | solution.py:163
  6.1 3.1 %collective-permute-start = (bf16[16,2048]{1,0:T(8,128)(2,1)S(1)}, bf16[16,2048]{1,0:T(8,128)(2,1)S(1)}, u32[]{:S(2)}, u32[]{:S(2)}) collective-permute-start(bf16[16,2048]{1,0:T(8,128)(2,1)S(1)} %get-tuple-element.55), channel_id=1, source_target_pairs={{0,1},{1,2},{2,3},{3,0},{4,5},{5,6},{6,7},{7,4},{8,9},{9,10},{10,1... | collective-permute-start | bytes 196616 | tf_op jit(solution)/shard_map/ppermute | solution.py:354
  9.2 2.6 %collective-permute-start.1 = (bf16[16,2048]{1,0:T(8,128)(2,1)S(1)}, bf16[16,2048]{1,0:T(8,128)(2,1)S(1)}, u32[]{:S(2)}, u32[]{:S(2)}) collective-permute-start(bf16[16,2048]{1,0:T(8,128)(2,1)S(1)} %get-tuple-element.56), channel_id=1, source_target_pairs={{0,2},{1,3},{2,0},{3,1},{4,6},{5,7},{6,4},{7,5},{8,10},{9,11},{10,... | collective-permute-start | bytes 196616 | tf_op jit(solution)/shard_map/ppermute | solution.py:354
  11.8 1.4 %collective-permute-start.2 = (bf16[16,2048]{1,0:T(8,128)(2,1)S(1)}, bf16[16,2048]{1,0:T(8,128)(2,1)S(1)}, u32[]{:S(2)}, u32[]{:S(2)}) collective-permute-start(bf16[16,2048]{1,0:T(8,128)(2,1)S(1)} %get-tuple-element.57), channel_id=1, source_target_pairs={{0,3},{1,0},{2,1},{3,2},{4,7},{5,4},{6,5},{7,6},{8,11},{9,8},{10,9... | collective-permute-start | bytes 196616 | tf_op jit(solution)/shard_map/ppermute | solution.py:354
  13.2 2.9 %load.1 = (bf16[2048,512]{1,0:T(8,128)(2,1)S(1)}, bf16[2048,512]{1,0:T(8,128)(2,1)S(1)}, bf16[512,2048]{1,0:T(8,128)(2,1)S(1)}) custom-call(bf16[1,2048,512]{2,1,0:T(8,128)(2,1)} %refs_0_.3, bf16[1,2048,512]{2,1,0:T(8,128)(2,1)} %refs_1_.3, bf16[1,512,2048]{2,1,0:T(8,128)(2,1)} %refs_2_.3), custom_call_target="tpu_custom_call" | custom-call | tf_op jit(solution)/shard_map/load/pallas_call | solution.py:226
  16.1 0.2 collective-permute-done.1.rest_1_
  16.3 0.3 collective-permute-done.2.rest_2_
  16.6 0.2 norm.1
  16.8 3.0 %collective-permute-start.3 = (bf16[16,2048]{1,0:T(8,128)(2,1)S(1)}, bf16[16,2048]{1,0:T(8,128)(2,1)S(1)}, u32[]{:S(2)}, u32[]{:S(2)}) collective-permute-start(bf16[16,2048]{1,0:T(8,128)(2,1)S(1)} %get-tuple-element.65.refs_0_), channel_id=1, source_target_pairs={{0,3},{1,0},{2,1},{3,2},{4,7},{5,4},{6,5},{7,6},{8,11},{9,8},{10,9... | collective-permute-start | bytes 196616 | tf_op jit(solution)/shard_map/ppermute | solution.py:354
  19.8 0.6 collective-permute-start.5
  20.4 1.3 %collective-permute-done.3.refs_1_ = bf16[16,2048]{1,0:T(8,128)(2,1)S(1)} collective-permute-done((bf16[16,2048]{1,0:T(8,128)(2,1)S(1)}, bf16[16,2048]{1,0:T(8,128)(2,1)S(1)}, u32[]{:S(2)}, u32[]{:S(2)}) %collective-permute-start.3) | collective-permute-done | bytes 65568 | tf_op jit(solution)/shard_map/ppermute | solution.py:354
  21.7 4.5 %collective-permute-done.4.refs_0_ = bf16[16,2048]{1,0:T(8,128)(2,1)S(1)} collective-permute-done((bf16[16,2048]{1,0:T(8,128)(2,1)S(1)}, bf16[16,2048]{1,0:T(8,128)(2,1)S(1)}, u32[]{:S(2)}, u32[]{:S(2)}) %collective-permute-start.4) | collective-permute-done | bytes 65568 | tf_op jit(solution)/shard_map/ppermute | solution.py:354
  26.2 0.1 collective-permute-start.6
  26.3 1.3 %collective-permute-start.7 = (bf16[32,2048]{1,0:T(8,128)(2,1)S(1)}, bf16[32,2048]{1,0:T(8,128)(2,1)S(1)}, u32[]{:S(2)}, u32[]{:S(2)}) collective-permute-start(bf16[32,2048]{1,0:T(8,128)(2,1)S(1)} %join.6.refs_0_), channel_id=1, source_target_pairs={{0,8},{4,20},{8,0},{12,28},{16,24},{20,4},{24,16},{28,12},{1,9},{5... | collective-permute-start | bytes 393224 | tf_op jit(solution)/shard_map/ppermute | solution.py:357
  27.6 0.8 %collective-permute-start.8 = (bf16[32,2048]{1,0:T(8,128)(2,1)S(1)}, bf16[32,2048]{1,0:T(8,128)(2,1)S(1)}, u32[]{:S(2)}, u32[]{:S(2)}) collective-permute-start(bf16[32,2048]{1,0:T(8,128)(2,1)S(1)} %join.7.refs_1_), channel_id=1, source_target_pairs={{0,8},{4,20},{8,0},{12,28},{16,24},{20,4},{24,16},{28,12},{1,9},{5... | collective-permute-start | bytes 393224 | tf_op jit(solution)/shard_map/ppermute | solution.py:357
  28.4 1.3 %collective-permute-start.12 = (bf16[64,2048]{1,0:T(8,128)(2,1)S(1)}, bf16[64,2048]{1,0:T(8,128)(2,1)S(1)}, u32[]{:S(2)}, u32[]{:S(2)}) collective-permute-start(bf16[64,2048]{1,0:T(8,128)(2,1)S(1)} %join.8.refs_0_), channel_id=1, source_target_pairs={{0,16},{4,12},{8,24},{12,4},{16,0},{20,28},{24,8},{28,20},{1,17},{... | collective-permute-start | bytes 786440 | tf_op jit(solution)/shard_map/ppermute | solution.py:357
  29.7 1.1 %experts.4 = (f32[64,2048]{1,0:T(8,128)S(1)}, bf16[64,2048]{1,0:T(8,128)(2,1)S(1)}) custom-call(s32[1]{0:T(128)} %bitcast.place, s32[1]{0:T(128)} %bitcast.1.spot, s32[10,4,128]{2,1,0:T(4,128)S(1)} %bitcast.8, f32[10,4,128]{2,1,0:T(4,128)S(1)} %bitcast.12, bf16[2048,512]{1,0:T(8,128)(2,1)S(1)} %get-tuple-element.66.gate, ...), custom_call_target="tpu_custom_call" | custom-call | tf_op jit(solution)/shard_map/experts/pallas_call | solution.py:188
  30.8 1.0 %collective-permute-done.7.refs_0_ = bf16[32,2048]{1,0:T(8,128)(2,1)S(1)} collective-permute-done((bf16[32,2048]{1,0:T(8,128)(2,1)S(1)}, bf16[32,2048]{1,0:T(8,128)(2,1)S(1)}, u32[]{:S(2)}, u32[]{:S(2)}) %collective-permute-start.7) | collective-permute-done | bytes 131104 | tf_op jit(solution)/shard_map/ppermute | solution.py:357
  31.8 2.8 %collective-permute-done.8.refs_1_ = bf16[32,2048]{1,0:T(8,128)(2,1)S(1)} collective-permute-done((bf16[32,2048]{1,0:T(8,128)(2,1)S(1)}, bf16[32,2048]{1,0:T(8,128)(2,1)S(1)}, u32[]{:S(2)}, u32[]{:S(2)}) %collective-permute-start.8) | collective-permute-done | bytes 131104 | tf_op jit(solution)/shard_map/ppermute | solution.py:357
  34.7 0.1 collective-permute-start.11
  34.7 1.3 %collective-permute-start.9 = (bf16[32,2048]{1,0:T(8,128)(2,1)S(1)}, bf16[32,2048]{1,0:T(8,128)(2,1)S(1)}, u32[]{:S(2)}, u32[]{:S(2)}) collective-permute-start(bf16[32,2048]{1,0:T(8,128)(2,1)S(1)} %collective-permute-done.7.refs_0_), channel_id=1, source_target_pairs={{0,16},{4,12},{8,24},{12,4},{16,0},{20,28},{24,8},{28,20},{1,17},{... | collective-permute-start | bytes 393224 | tf_op jit(solution)/shard_map/ppermute | solution.py:357
  36.1 0.8 %collective-permute-start.10 = (bf16[32,2048]{1,0:T(8,128)(2,1)S(1)}, bf16[32,2048]{1,0:T(8,128)(2,1)S(1)}, u32[]{:S(2)}, u32[]{:S(2)}) collective-permute-start(bf16[32,2048]{1,0:T(8,128)(2,1)S(1)} %collective-permute-done.8.refs_1_), channel_id=1, source_target_pairs={{0,16},{4,12},{8,24},{12,4},{16,0},{20,28},{24,8},{28,20},{1,17},{... | collective-permute-start | bytes 393224 | tf_op jit(solution)/shard_map/ppermute | solution.py:357
  36.8 1.1 %experts.5 = (f32[64,2048]{1,0:T(8,128)S(1)}, bf16[64,2048]{1,0:T(8,128)(2,1)S(1)}) custom-call(s32[1]{0:T(128)} %bitcast.place, s32[1]{0:T(128)} %bitcast.1.spot, s32[10,4,128]{2,1,0:T(4,128)S(1)} %bitcast.9, f32[10,4,128]{2,1,0:T(4,128)S(1)} %bitcast.13, bf16[2048,512]{1,0:T(8,128)(2,1)S(1)} %get-tuple-element.66.gate, ...), custom_call_target="tpu_custom_call" | custom-call | tf_op jit(solution)/shard_map/experts/pallas_call | solution.py:188
  38.0 0.1 collective-permute-start.14
  38.1 1.7 %collective-permute-done.9.refs_0_ = bf16[32,2048]{1,0:T(8,128)(2,1)S(1)} collective-permute-done((bf16[32,2048]{1,0:T(8,128)(2,1)S(1)}, bf16[32,2048]{1,0:T(8,128)(2,1)S(1)}, u32[]{:S(2)}, u32[]{:S(2)}) %collective-permute-start.9) | collective-permute-done | bytes 131104 | tf_op jit(solution)/shard_map/ppermute | solution.py:357
  39.8 1.4 %collective-permute-done.10.refs_1_ = bf16[32,2048]{1,0:T(8,128)(2,1)S(1)} collective-permute-done((bf16[32,2048]{1,0:T(8,128)(2,1)S(1)}, bf16[32,2048]{1,0:T(8,128)(2,1)S(1)}, u32[]{:S(2)}, u32[]{:S(2)}) %collective-permute-start.10) | collective-permute-done | bytes 131104 | tf_op jit(solution)/shard_map/ppermute | solution.py:357
  41.2 0.1 collective-permute-start.13
  41.3 0.5 collective-permute-start.16
  41.8 1.1 %experts.6 = (f32[64,2048]{1,0:T(8,128)S(1)}, bf16[64,2048]{1,0:T(8,128)(2,1)S(1)}) custom-call(s32[1]{0:T(128)} %bitcast.place, s32[1]{0:T(128)} %bitcast.1.spot, s32[10,4,128]{2,1,0:T(4,128)S(1)} %bitcast.10, f32[10,4,128]{2,1,0:T(4,128)S(1)} %bitcast.14, bf16[2048,512]{1,0:T(8,128)(2,1)S(1)} %get-tuple-element.66.gate, ...), custom_call_target="tpu_custom_call" | custom-call | tf_op jit(solution)/shard_map/experts/pallas_call | solution.py:188
  42.9 1.1 %experts.7 = (f32[64,2048]{1,0:T(8,128)S(1)}, bf16[64,2048]{1,0:T(8,128)(2,1)S(1)}) custom-call(s32[1]{0:T(128)} %bitcast.place, s32[1]{0:T(128)} %bitcast.1.spot, s32[10,4,128]{2,1,0:T(4,128)S(1)} %bitcast.11, f32[10,4,128]{2,1,0:T(4,128)S(1)} %bitcast.15, bf16[2048,512]{1,0:T(8,128)(2,1)S(1)} %get-tuple-element.66.gate, ...), custom_call_target="tpu_custom_call" | custom-call | tf_op jit(solution)/shard_map/experts/pallas_call | solution.py:188
  44.1 0.1 collective-permute-start.19
  44.2 0.4 collective-permute-start.15
  44.6 0.1 collective-permute-start.18
  44.8 0.9 %collective-permute-done.19.refs_1_ = bf16[64,2048]{1,0:T(8,128)(2,1)S(1)} collective-permute-done((bf16[64,2048]{1,0:T(8,128)(2,1)S(1)}, bf16[64,2048]{1,0:T(8,128)(2,1)S(1)}, u32[]{:S(2)}, u32[]{:S(2)}) %collective-permute-start.19) | collective-permute-done | bytes 262176 | tf_op jit(solution)/shard_map/ppermute | solution.py:362
  45.7 1.3 %collective-permute-start.20 = (bf16[32,2048]{1,0:T(8,128)(2,1)S(1)}, bf16[32,2048]{1,0:T(8,128)(2,1)S(1)}, u32[]{:S(2)}, u32[]{:S(2)}) collective-permute-start(bf16[32,2048]{1,0:T(8,128)(2,1)S(1)} %get-tuple-element.96), channel_id=1, source_target_pairs={{0,16},{4,12},{8,24},{12,4},{16,0},{20,28},{24,8},{28,20},{1,17},{... | collective-permute-start | bytes 393224 | tf_op jit(solution)/shard_map/ppermute | solution.py:357
  47.0 0.8 %collective-permute-start.22 = (bf16[32,2048]{1,0:T(8,128)(2,1)S(1)}, bf16[32,2048]{1,0:T(8,128)(2,1)S(1)}, u32[]{:S(2)}, u32[]{:S(2)}) collective-permute-start(bf16[32,2048]{1,0:T(8,128)(2,1)S(1)} %get-tuple-element.98), channel_id=1, source_target_pairs={{0,16},{4,12},{8,24},{12,4},{16,0},{20,28},{24,8},{28,20},{1,17},{... | collective-permute-start | bytes 393224 | tf_op jit(solution)/shard_map/ppermute | solution.py:357
  47.9 1.3 %collective-permute-start.17 = (bf16[64,2048]{1,0:T(8,128)(2,1)S(1)}, bf16[64,2048]{1,0:T(8,128)(2,1)S(1)}, u32[]{:S(2)}, u32[]{:S(2)}) collective-permute-start(bf16[64,2048]{1,0:T(8,128)(2,1)S(1)} %add.7), channel_id=1, source_target_pairs={{0,16},{4,12},{8,24},{12,4},{16,0},{20,28},{24,8},{28,20},{1,17},{... | collective-permute-start | bytes 786440 | tf_op jit(solution)/shard_map/ppermute | solution.py:357
  49.3 1.5 %collective-permute-done.20.refs_1_ = bf16[32,2048]{1,0:T(8,128)(2,1)S(1)} collective-permute-done((bf16[32,2048]{1,0:T(8,128)(2,1)S(1)}, bf16[32,2048]{1,0:T(8,128)(2,1)S(1)}, u32[]{:S(2)}, u32[]{:S(2)}) %collective-permute-start.20) | collective-permute-done | bytes 131104 | tf_op jit(solution)/shard_map/ppermute | solution.py:357
  50.8 1.4 %collective-permute-start.21 = (bf16[32,2048]{1,0:T(8,128)(2,1)S(1)}, bf16[32,2048]{1,0:T(8,128)(2,1)S(1)}, u32[]{:S(2)}, u32[]{:S(2)}) collective-permute-start(bf16[32,2048]{1,0:T(8,128)(2,1)S(1)} %add.11), channel_id=1, source_target_pairs={{0,8},{4,20},{8,0},{12,28},{16,24},{20,4},{24,16},{28,12},{1,9},{5... | collective-permute-start | bytes 393224 | tf_op jit(solution)/shard_map/ppermute | solution.py:357
  52.3 1.4 %collective-permute-start.23 = (bf16[32,2048]{1,0:T(8,128)(2,1)S(1)}, bf16[32,2048]{1,0:T(8,128)(2,1)S(1)}, u32[]{:S(2)}, u32[]{:S(2)}) collective-permute-start(bf16[32,2048]{1,0:T(8,128)(2,1)S(1)} %add.12), channel_id=1, source_target_pairs={{0,8},{4,20},{8,0},{12,28},{16,24},{20,4},{24,16},{28,12},{1,9},{5... | collective-permute-start | bytes 393224 | tf_op jit(solution)/shard_map/ppermute | solution.py:357
  53.6 2.2 %collective-permute-done.21.refs_0_ = bf16[32,2048]{1,0:T(8,128)(2,1)S(1)} collective-permute-done((bf16[32,2048]{1,0:T(8,128)(2,1)S(1)}, bf16[32,2048]{1,0:T(8,128)(2,1)S(1)}, u32[]{:S(2)}, u32[]{:S(2)}) %collective-permute-start.21) | collective-permute-done | bytes 131104 | tf_op jit(solution)/shard_map/ppermute | solution.py:357
  55.8 1.5 %collective-permute-done.23.refs_1_ = bf16[32,2048]{1,0:T(8,128)(2,1)S(1)} collective-permute-done((bf16[32,2048]{1,0:T(8,128)(2,1)S(1)}, bf16[32,2048]{1,0:T(8,128)(2,1)S(1)}, u32[]{:S(2)}, u32[]{:S(2)}) %collective-permute-start.23) | collective-permute-done | bytes 131104 | tf_op jit(solution)/shard_map/ppermute | solution.py:357
  57.3 0.1 add.13
  57.5 1.7 %collective-permute-start.25 = (bf16[16,2048]{1,0:T(8,128)(2,1)S(1)}, bf16[16,2048]{1,0:T(8,128)(2,1)S(1)}, u32[]{:S(2)}, u32[]{:S(2)}) collective-permute-start(bf16[16,2048]{1,0:T(8,128)(2,1)S(1)} %get-tuple-element.101), channel_id=1, source_target_pairs={{0,2},{1,3},{2,0},{3,1},{4,6},{5,7},{6,4},{7,5},{8,10},{9,11},{10,... | collective-permute-start | bytes 196616 | tf_op jit(solution)/shard_map/ppermute | solution.py:354
  59.2 2.2 %collective-permute-start.26 = (bf16[16,2048]{1,0:T(8,128)(2,1)S(1)}, bf16[16,2048]{1,0:T(8,128)(2,1)S(1)}, u32[]{:S(2)}, u32[]{:S(2)}) collective-permute-start(bf16[16,2048]{1,0:T(8,128)(2,1)S(1)} %get-tuple-element.102), channel_id=1, source_target_pairs={{0,3},{1,0},{2,1},{3,2},{4,7},{5,4},{6,5},{7,6},{8,11},{9,8},{10,9... | collective-permute-start | bytes 196616 | tf_op jit(solution)/shard_map/ppermute | solution.py:354
  61.4 2.8 %collective-permute-done.24.rest_0_ = bf16[16,2048]{1,0:T(8,128)(2,1)S(1)} collective-permute-done((bf16[16,2048]{1,0:T(8,128)(2,1)S(1)}, bf16[16,2048]{1,0:T(8,128)(2,1)S(1)}, u32[]{:S(2)}, u32[]{:S(2)}) %collective-permute-start.24) | collective-permute-done | bytes 65568 | tf_op jit(solution)/shard_map/ppermute | solution.py:354
  64.3 1.7 %collective-permute-done.25.rest_1_ = bf16[16,2048]{1,0:T(8,128)(2,1)S(1)} collective-permute-done((bf16[16,2048]{1,0:T(8,128)(2,1)S(1)}, bf16[16,2048]{1,0:T(8,128)(2,1)S(1)}, u32[]{:S(2)}, u32[]{:S(2)}) %collective-permute-start.25) | collective-permute-done | bytes 65568 | tf_op jit(solution)/shard_map/ppermute | solution.py:354
  66.0 0.7 %finish.1 = bf16[4,4,2048]{2,1,0:T(4,128)(2,1)} custom-call(f32[16,2048]{1,0:T(8,128)S(1)} %get-tuple-element.64.stream_ref, f32[16,2048]{1,0:T(8,128)S(1)} %get-tuple-element.99.own_ref, bf16[16,2048]{1,0:T(8,128)(2,1)S(1)} %collective-permute-done.24.rest_0_, bf16[16,2048]{1,0:T(8,128)(2,1)S(1)} %collective-permute-done.25.rest_1_, ...), custom_call_target="tpu_custom_call" | custom-call | tf_op jit(solution)/shard_map/finish/pallas_call | solution.py:188
  (35 shorter events, 0.5 us)
Async XLA Ops:
  6.1 10.0 %collective-permute-start = (bf16[16,2048]{1,0:T(8,128)(2,1)S(1)}, bf16[16,2048]{1,0:T(8,128)(2,1)S(1)}, u32[]{:S(2)}, u32[]{:S(2)}) collective-permute-start(bf16[16,2048]{1,0:T(8,128)(2,1)S(1)} %get-tuple-element.55), channel_id=1, source_target_pairs={{0,1},{1,2},{2,3},{3,0},{4,5},{5,6},{6,7},{7,4},{8,9},{9,10},{10,1... | collective-permute-start | bytes 196616 | tf_op jit(solution)/shard_map/ppermute | solution.py:354
  9.2 7.1 %collective-permute-start.1 = (bf16[16,2048]{1,0:T(8,128)(2,1)S(1)}, bf16[16,2048]{1,0:T(8,128)(2,1)S(1)}, u32[]{:S(2)}, u32[]{:S(2)}) collective-permute-start(bf16[16,2048]{1,0:T(8,128)(2,1)S(1)} %get-tuple-element.56), channel_id=1, source_target_pairs={{0,2},{1,3},{2,0},{3,1},{4,6},{5,7},{6,4},{7,5},{8,10},{9,11},{10,... | collective-permute-start | bytes 196616 | tf_op jit(solution)/shard_map/ppermute | solution.py:354
  11.8 4.8 %copy-start.2 = (bf16[4,4,2048]{2,1,0:T(4,128)(2,1)S(1)}, bf16[4,4,2048]{2,1,0:T(4,128)(2,1)}, u32[]{:S(2)}) copy-start(bf16[4,4,2048]{2,1,0:T(4,128)(2,1)} %residual_ref.1) | copy-start | bytes 196612
  11.8 4.8 %copy-start.3 = (f32[2048]{0:T(1024)S(1)}, f32[2048]{0:T(1024)}, u32[]{:S(2)}) copy-start(f32[2048]{0:T(1024)} %param.26) | copy-start | bytes 24580
  11.8 17.9 %copy-start = (s32[4,128,10]{1,0,2:T(4,128)S(1)}, s32[4,128,10]{1,0,2:T(4,128)}, u32[]{:S(2)}) copy-start(s32[4,128,10]{1,0,2:T(4,128)} %param.27) | copy-start | bytes 61444
  11.8 17.9 %copy-start.1 = (f32[4,128,10]{1,0,2:T(4,128)S(1)}, f32[4,128,10]{1,0,2:T(4,128)}, u32[]{:S(2)}) copy-start(f32[4,128,10]{1,0,2:T(4,128)} %param.28) | copy-start | bytes 61444
  11.8 4.8 %collective-permute-start.2 = (bf16[16,2048]{1,0:T(8,128)(2,1)S(1)}, bf16[16,2048]{1,0:T(8,128)(2,1)S(1)}, u32[]{:S(2)}, u32[]{:S(2)}) collective-permute-start(bf16[16,2048]{1,0:T(8,128)(2,1)S(1)} %get-tuple-element.57), channel_id=1, source_target_pairs={{0,3},{1,0},{2,1},{3,2},{4,7},{5,4},{6,5},{7,6},{8,11},{9,8},{10,9... | collective-permute-start | bytes 196616 | tf_op jit(solution)/shard_map/ppermute | solution.py:354
  16.8 4.9 %collective-permute-start.3 = (bf16[16,2048]{1,0:T(8,128)(2,1)S(1)}, bf16[16,2048]{1,0:T(8,128)(2,1)S(1)}, u32[]{:S(2)}, u32[]{:S(2)}) collective-permute-start(bf16[16,2048]{1,0:T(8,128)(2,1)S(1)} %get-tuple-element.65.refs_0_), channel_id=1, source_target_pairs={{0,3},{1,0},{2,1},{3,2},{4,7},{5,4},{6,5},{7,6},{8,11},{9,8},{10,9... | collective-permute-start | bytes 196616 | tf_op jit(solution)/shard_map/ppermute | solution.py:354
  19.8 6.4 %collective-permute-start.4 = (bf16[16,2048]{1,0:T(8,128)(2,1)S(1)}, bf16[16,2048]{1,0:T(8,128)(2,1)S(1)}, u32[]{:S(2)}, u32[]{:S(2)}) collective-permute-start(bf16[16,2048]{1,0:T(8,128)(2,1)S(1)} %get-tuple-element.65.refs_0_), channel_id=1, source_target_pairs={{0,2},{1,3},{2,0},{3,1},{4,6},{5,7},{6,4},{7,5},{8,10},{9,11},{10,... | collective-permute-start | bytes 196616 | tf_op jit(solution)/shard_map/ppermute | solution.py:354
  19.8 6.4 %collective-permute-start.5 = (bf16[16,2048]{1,0:T(8,128)(2,1)S(1)}, bf16[16,2048]{1,0:T(8,128)(2,1)S(1)}, u32[]{:S(2)}, u32[]{:S(2)}) collective-permute-start(bf16[16,2048]{1,0:T(8,128)(2,1)S(1)} %get-tuple-element.65.refs_0_), channel_id=1, source_target_pairs={{0,1},{1,2},{2,3},{3,0},{4,5},{5,6},{6,7},{7,4},{8,9},{9,10},{10,1... | collective-permute-start | bytes 196616 | tf_op jit(solution)/shard_map/ppermute | solution.py:354
  26.2 3.5 %collective-permute-start.6 = (bf16[64,2048]{1,0:T(8,128)(2,1)S(1)}, bf16[64,2048]{1,0:T(8,128)(2,1)S(1)}, u32[]{:S(2)}, u32[]{:S(2)}) collective-permute-start(bf16[64,2048]{1,0:T(8,128)(2,1)S(1)} %join.8.refs_0_), channel_id=1, source_target_pairs={{0,4},{4,0},{8,12},{12,8},{16,20},{20,16},{24,28},{28,24},{1,5},{5... | collective-permute-start | bytes 786440 | tf_op jit(solution)/shard_map/ppermute | solution.py:362
  26.3 5.5 %collective-permute-start.7 = (bf16[32,2048]{1,0:T(8,128)(2,1)S(1)}, bf16[32,2048]{1,0:T(8,128)(2,1)S(1)}, u32[]{:S(2)}, u32[]{:S(2)}) collective-permute-start(bf16[32,2048]{1,0:T(8,128)(2,1)S(1)} %join.6.refs_0_), channel_id=1, source_target_pairs={{0,8},{4,20},{8,0},{12,28},{16,24},{20,4},{24,16},{28,12},{1,9},{5... | collective-permute-start | bytes 393224 | tf_op jit(solution)/shard_map/ppermute | solution.py:357
  27.6 7.0 %collective-permute-start.8 = (bf16[32,2048]{1,0:T(8,128)(2,1)S(1)}, bf16[32,2048]{1,0:T(8,128)(2,1)S(1)}, u32[]{:S(2)}, u32[]{:S(2)}) collective-permute-start(bf16[32,2048]{1,0:T(8,128)(2,1)S(1)} %join.7.refs_1_), channel_id=1, source_target_pairs={{0,8},{4,20},{8,0},{12,28},{16,24},{20,4},{24,16},{28,12},{1,9},{5... | collective-permute-start | bytes 393224 | tf_op jit(solution)/shard_map/ppermute | solution.py:357
  28.4 8.4 %collective-permute-start.12 = (bf16[64,2048]{1,0:T(8,128)(2,1)S(1)}, bf16[64,2048]{1,0:T(8,128)(2,1)S(1)}, u32[]{:S(2)}, u32[]{:S(2)}) collective-permute-start(bf16[64,2048]{1,0:T(8,128)(2,1)S(1)} %join.8.refs_0_), channel_id=1, source_target_pairs={{0,16},{4,12},{8,24},{12,4},{16,0},{20,28},{24,8},{28,20},{1,17},{... | collective-permute-start | bytes 786440 | tf_op jit(solution)/shard_map/ppermute | solution.py:357
  34.7 2.2 %collective-permute-start.11 = (bf16[64,2048]{1,0:T(8,128)(2,1)S(1)}, bf16[64,2048]{1,0:T(8,128)(2,1)S(1)}, u32[]{:S(2)}, u32[]{:S(2)}) collective-permute-start(bf16[64,2048]{1,0:T(8,128)(2,1)S(1)} %join.9.refs_0_), channel_id=1, source_target_pairs={{0,4},{4,0},{8,12},{12,8},{16,20},{20,16},{24,28},{28,24},{1,5},{5... | collective-permute-start | bytes 786440 | tf_op jit(solution)/shard_map/ppermute | solution.py:362
  34.7 5.0 %collective-permute-start.9 = (bf16[32,2048]{1,0:T(8,128)(2,1)S(1)}, bf16[32,2048]{1,0:T(8,128)(2,1)S(1)}, u32[]{:S(2)}, u32[]{:S(2)}) collective-permute-start(bf16[32,2048]{1,0:T(8,128)(2,1)S(1)} %collective-permute-done.7.refs_0_), channel_id=1, source_target_pairs={{0,16},{4,12},{8,24},{12,4},{16,0},{20,28},{24,8},{28,20},{1,17},{... | collective-permute-start | bytes 393224 | tf_op jit(solution)/shard_map/ppermute | solution.py:357
  36.1 5.1 %collective-permute-start.10 = (bf16[32,2048]{1,0:T(8,128)(2,1)S(1)}, bf16[32,2048]{1,0:T(8,128)(2,1)S(1)}, u32[]{:S(2)}, u32[]{:S(2)}) collective-permute-start(bf16[32,2048]{1,0:T(8,128)(2,1)S(1)} %collective-permute-done.8.refs_1_), channel_id=1, source_target_pairs={{0,16},{4,12},{8,24},{12,4},{16,0},{20,28},{24,8},{28,20},{1,17},{... | collective-permute-start | bytes 393224 | tf_op jit(solution)/shard_map/ppermute | solution.py:357
  38.0 3.8 %collective-permute-start.14 = (bf16[64,2048]{1,0:T(8,128)(2,1)S(1)}, bf16[64,2048]{1,0:T(8,128)(2,1)S(1)}, u32[]{:S(2)}, u32[]{:S(2)}) collective-permute-start(bf16[64,2048]{1,0:T(8,128)(2,1)S(1)} %collective-permute-done.12.refs_0_), channel_id=1, source_target_pairs={{0,4},{4,0},{8,12},{12,8},{16,20},{20,16},{24,28},{28,24},{1,5},{5... | collective-permute-start | bytes 786440 | tf_op jit(solution)/shard_map/ppermute | solution.py:362
  41.2 1.7 %collective-permute-start.13 = (bf16[64,2048]{1,0:T(8,128)(2,1)S(1)}, bf16[64,2048]{1,0:T(8,128)(2,1)S(1)}, u32[]{:S(2)}, u32[]{:S(2)}) collective-permute-start(bf16[64,2048]{1,0:T(8,128)(2,1)S(1)} %join.10.refs_0_), channel_id=1, source_target_pairs={{0,4},{4,0},{8,12},{12,8},{16,20},{20,16},{24,28},{28,24},{1,5},{5... | collective-permute-start | bytes 786440 | tf_op jit(solution)/shard_map/ppermute | solution.py:362
  41.3 3.4 %collective-permute-start.16 = (bf16[64,2048]{1,0:T(8,128)(2,1)S(1)}, bf16[64,2048]{1,0:T(8,128)(2,1)S(1)}, u32[]{:S(2)}, u32[]{:S(2)}) collective-permute-start(bf16[64,2048]{1,0:T(8,128)(2,1)S(1)} %get-tuple-element.87), channel_id=1, source_target_pairs={{0,4},{4,0},{8,12},{12,8},{16,20},{20,16},{24,28},{28,24},{1,5},{5... | collective-permute-start | bytes 786440 | tf_op jit(solution)/shard_map/ppermute | solution.py:362
  44.1 1.6 %collective-permute-start.19 = (bf16[64,2048]{1,0:T(8,128)(2,1)S(1)}, bf16[64,2048]{1,0:T(8,128)(2,1)S(1)}, u32[]{:S(2)}, u32[]{:S(2)}) collective-permute-start(bf16[64,2048]{1,0:T(8,128)(2,1)S(1)} %get-tuple-element.95), channel_id=1, source_target_pairs={{0,4},{4,0},{8,12},{12,8},{16,20},{20,16},{24,28},{28,24},{1,5},{5... | collective-permute-start | bytes 786440 | tf_op jit(solution)/shard_map/ppermute | solution.py:362
  44.2 3.6 %collective-permute-start.15 = (bf16[64,2048]{1,0:T(8,128)(2,1)S(1)}, bf16[64,2048]{1,0:T(8,128)(2,1)S(1)}, u32[]{:S(2)}, u32[]{:S(2)}) collective-permute-start(bf16[64,2048]{1,0:T(8,128)(2,1)S(1)} %get-tuple-element.85), channel_id=1, source_target_pairs={{0,4},{4,0},{8,12},{12,8},{16,20},{20,16},{24,28},{28,24},{1,5},{5... | collective-permute-start | bytes 786440 | tf_op jit(solution)/shard_map/ppermute | solution.py:362
  44.6 4.6 %collective-permute-start.18 = (bf16[64,2048]{1,0:T(8,128)(2,1)S(1)}, bf16[64,2048]{1,0:T(8,128)(2,1)S(1)}, u32[]{:S(2)}, u32[]{:S(2)}) collective-permute-start(bf16[64,2048]{1,0:T(8,128)(2,1)S(1)} %get-tuple-element.91), channel_id=1, source_target_pairs={{0,4},{4,0},{8,12},{12,8},{16,20},{20,16},{24,28},{28,24},{1,5},{5... | collective-permute-start | bytes 786440 | tf_op jit(solution)/shard_map/ppermute | solution.py:362
  45.7 5.0 %collective-permute-start.20 = (bf16[32,2048]{1,0:T(8,128)(2,1)S(1)}, bf16[32,2048]{1,0:T(8,128)(2,1)S(1)}, u32[]{:S(2)}, u32[]{:S(2)}) collective-permute-start(bf16[32,2048]{1,0:T(8,128)(2,1)S(1)} %get-tuple-element.96), channel_id=1, source_target_pairs={{0,16},{4,12},{8,24},{12,4},{16,0},{20,28},{24,8},{28,20},{1,17},{... | collective-permute-start | bytes 393224 | tf_op jit(solution)/shard_map/ppermute | solution.py:357
  47.0 5.2 %collective-permute-start.22 = (bf16[32,2048]{1,0:T(8,128)(2,1)S(1)}, bf16[32,2048]{1,0:T(8,128)(2,1)S(1)}, u32[]{:S(2)}, u32[]{:S(2)}) collective-permute-start(bf16[32,2048]{1,0:T(8,128)(2,1)S(1)} %get-tuple-element.98), channel_id=1, source_target_pairs={{0,16},{4,12},{8,24},{12,4},{16,0},{20,28},{24,8},{28,20},{1,17},{... | collective-permute-start | bytes 393224 | tf_op jit(solution)/shard_map/ppermute | solution.py:357
  47.9 9.4 %collective-permute-start.17 = (bf16[64,2048]{1,0:T(8,128)(2,1)S(1)}, bf16[64,2048]{1,0:T(8,128)(2,1)S(1)}, u32[]{:S(2)}, u32[]{:S(2)}) collective-permute-start(bf16[64,2048]{1,0:T(8,128)(2,1)S(1)} %add.7), channel_id=1, source_target_pairs={{0,16},{4,12},{8,24},{12,4},{16,0},{20,28},{24,8},{28,20},{1,17},{... | collective-permute-start | bytes 786440 | tf_op jit(solution)/shard_map/ppermute | solution.py:357
  50.8 5.0 %collective-permute-start.21 = (bf16[32,2048]{1,0:T(8,128)(2,1)S(1)}, bf16[32,2048]{1,0:T(8,128)(2,1)S(1)}, u32[]{:S(2)}, u32[]{:S(2)}) collective-permute-start(bf16[32,2048]{1,0:T(8,128)(2,1)S(1)} %add.11), channel_id=1, source_target_pairs={{0,8},{4,20},{8,0},{12,28},{16,24},{20,4},{24,16},{28,12},{1,9},{5... | collective-permute-start | bytes 393224 | tf_op jit(solution)/shard_map/ppermute | solution.py:357
  52.3 5.0 %collective-permute-start.23 = (bf16[32,2048]{1,0:T(8,128)(2,1)S(1)}, bf16[32,2048]{1,0:T(8,128)(2,1)S(1)}, u32[]{:S(2)}, u32[]{:S(2)}) collective-permute-start(bf16[32,2048]{1,0:T(8,128)(2,1)S(1)} %add.12), channel_id=1, source_target_pairs={{0,8},{4,20},{8,0},{12,28},{16,24},{20,4},{24,16},{28,12},{1,9},{5... | collective-permute-start | bytes 393224 | tf_op jit(solution)/shard_map/ppermute | solution.py:357
  57.4 6.9 %collective-permute-start.24 = (bf16[16,2048]{1,0:T(8,128)(2,1)S(1)}, bf16[16,2048]{1,0:T(8,128)(2,1)S(1)}, u32[]{:S(2)}, u32[]{:S(2)}) collective-permute-start(bf16[16,2048]{1,0:T(8,128)(2,1)S(1)} %get-tuple-element.100), channel_id=1, source_target_pairs={{0,1},{1,2},{2,3},{3,0},{4,5},{5,6},{6,7},{7,4},{8,9},{9,10},{10,1... | collective-permute-start | bytes 196616 | tf_op jit(solution)/shard_map/ppermute | solution.py:354
  57.5 8.5 %collective-permute-start.25 = (bf16[16,2048]{1,0:T(8,128)(2,1)S(1)}, bf16[16,2048]{1,0:T(8,128)(2,1)S(1)}, u32[]{:S(2)}, u32[]{:S(2)}) collective-permute-start(bf16[16,2048]{1,0:T(8,128)(2,1)S(1)} %get-tuple-element.101), channel_id=1, source_target_pairs={{0,2},{1,3},{2,0},{3,1},{4,6},{5,7},{6,4},{7,5},{8,10},{9,11},{10,... | collective-permute-start | bytes 196616 | tf_op jit(solution)/shard_map/ppermute | solution.py:354
  59.2 6.8 %collective-permute-start.26 = (bf16[16,2048]{1,0:T(8,128)(2,1)S(1)}, bf16[16,2048]{1,0:T(8,128)(2,1)S(1)}, u32[]{:S(2)}, u32[]{:S(2)}) collective-permute-start(bf16[16,2048]{1,0:T(8,128)(2,1)S(1)} %get-tuple-element.102), channel_id=1, source_target_pairs={{0,3},{1,0},{2,1},{3,2},{4,7},{5,4},{6,5},{7,6},{8,11},{9,8},{10,9... | collective-permute-start | bytes 196616 | tf_op jit(solution)/shard_map/ppermute | solution.py:354
